TPU v7x, 256 devices: a whole 4x4x8 slice. The times are simulated.
256 devices in a mesh: rx: 8 (over x, core), ry: 32 (over y, z).
Axes of the slice: x: 4, y: 4, z: 8, core: 2. Of those that a mesh axis runs over, the one named last changes fastest.
Arguments:
- rhs: float32 [2, 11, 64, 16384], P(None, None, 'rx', 'ry'), may hold values from -6 to 6
- viscosity: float32 [10, 2, 64, 16384], P(None, None, 'rx', 'ry'), may hold values from 0.2 to 4
- cell_mask: int32 [64, 16384], P('rx', 'ry'), may hold values 0 or 1
- friction: float32 [64, 16384], P('rx', 'ry'), may hold values from 0.1 to 10
- stiffness: float32 [2, 12, 12], replicated, may hold values from -1.75 to 1.75
Outputs:
- update: float32 [2, 11, 64, 16384], P(None, None, 'rx', 'ry')
- last_basis: float32 [2, 11, 64, 16384], P(None, None, 'rx', 'ry')
All inputs are finite; a program needn't handle non-finite values. No bound on the sum of `cell_mask` on one device may be relied on, other than what follows from the above.
Results may differ from a plain program's by a relative error of at most 0.00012.
Values sent between devices are 32-bit elements; how exact they have to be, the bound alone decides.
No kernel may reach another device: no remote copies, remote signals or barrier semaphores. Data moves between devices by JAX's collectives and lax.ppermute only.
A program may use at most 64 MiB of HBM per device.

v0:
```python
import jax
import jax.numpy as jnp
from jax import lax
from jax.sharding import PartitionSpec as P

ITERS = 3


OFFSETS = ((0, 0), (1, 0), (0, 1), (1, 1))
TRIANGLES = ((0, 1, 2), (1, 3, 2))


def passed_along(shard, axis, by):
    devices = lax.axis_size(axis)
    pairs = [(i, i + by) for i in range(devices) if 0 <= i + by < devices]
    return lax.ppermute(shard, axis, pairs)


def element_apply(nodes, coef, stiff):
    rows = coef.shape[2]
    cols = coef.shape[3]
    layers = coef.shape[0]
    corners = [nodes[:, :, oi : oi + rows, oj : oj + cols] for oi, oj in OFFSETS]
    result = jnp.zeros_like(nodes)
    for tri in range(2):
        trio = TRIANGLES[tri]
        stacked = jnp.stack([corners[k] for k in trio], axis=0)
        levels = jnp.stack([stacked[:, :, :-1], stacked[:, :, 1:]], axis=0)
        local = jnp.transpose(levels, (2, 0, 1, 3, 4, 5)).reshape(12, layers, rows, cols)
        mixed = jnp.einsum("pq,qlrc->plrc", stiff[tri], local, precision=lax.Precision.HIGHEST)
        mixed = (mixed * coef[:, tri][None]).reshape(2, 2, 3, layers, rows, cols)
        for slot in range(3):
            node_part = jnp.pad(mixed[:, 0, slot], ((0, 0), (0, 1), (0, 0), (0, 0)))
            node_part = node_part + jnp.pad(mixed[:, 1, slot], ((0, 0), (1, 0), (0, 0), (0, 0)))
            shift_i, shift_j = OFFSETS[trio[slot]]
            result = result + jnp.pad(
                node_part, ((0, 0), (0, 0), (shift_i, 1 - shift_i), (shift_j, 1 - shift_j))
            )
    return result


def basal(field, friction):
    bottom = (friction[None] * field[:, 0])[:, None]
    return jnp.concatenate([bottom, jnp.zeros_like(field[:, 1:])], axis=1)


def least_squares(hess, norm0):
    count = len(hess[0])
    table = [list(line) for line in hess]
    target = [norm0] + [norm0 * 0.0 for step in range(count)]
    rotations = []
    for col in range(count):
        for row in range(col):
            cosine, sine = rotations[row]
            upper, lower = (table[row][col], table[row + 1][col])
            table[row][col] = cosine * upper + sine * lower
            table[row + 1][col] = cosine * lower - sine * upper
        first, second = (table[col][col], table[col + 1][col])
        radius = jnp.sqrt(first * first + second * second)
        cosine, sine = (first / radius, second / radius)
        rotations.append((cosine, sine))
        table[col][col] = radius
        upper, lower = (target[col], target[col + 1])
        target[col] = cosine * upper + sine * lower
        target[col + 1] = cosine * lower - sine * upper
    solved = [None] * count
    for col in range(count - 1, -1, -1):
        total = target[col]
        for later in range(col + 1, count):
            total = total - table[col][later] * solved[later]
        solved[col] = total / table[col][col]
    return solved


def body(rhs, viscosity, cell_mask, friction, stiffness):
    coef = viscosity * cell_mask.astype(jnp.float32)[None, None]
    rows = rhs.shape[2]
    cols = rhs.shape[3]
    norm0 = jnp.sqrt(lax.psum(jnp.sum(rhs * rhs), ("rx", "ry")))
    basis = [rhs / norm0]
    hess = [[norm0 * 0.0 for col in range(ITERS)] for row in range(ITERS + 1)]
    for col in range(ITERS):
        field = basis[col]
        below = passed_along(field[:, :, :1, :], "rx", -1)
        extended = jnp.concatenate([field, below], axis=2)
        beside = passed_along(extended[:, :, :, :1], "ry", -1)
        extended = jnp.concatenate([extended, beside], axis=3)
        partial_value = element_apply(extended, coef, stiffness)
        came_rows = passed_along(partial_value[:, :, rows:, :], "rx", 1)
        inner = partial_value[:, :, :rows, :]
        inner = jnp.concatenate([inner[:, :, :1, :] + came_rows, inner[:, :, 1:, :]], axis=2)
        came_cols = passed_along(inner[:, :, :, cols:], "ry", 1)
        inner = inner[:, :, :, :cols]
        assembled = jnp.concatenate([inner[:, :, :, :1] + came_cols, inner[:, :, :, 1:]], axis=3)
        work = assembled + field + basal(field, friction)
        for row in range(col + 1):
            single = lax.psum(jnp.sum(work * basis[row]), ("rx", "ry"))
            work = work - single * basis[row]
            hess[row][col] = single
        length = jnp.sqrt(lax.psum(jnp.sum(work * work), ("rx", "ry")))
        hess[col + 1][col] = length
        basis.append(work / length)
    solved = least_squares(hess, norm0)
    update = solved[0] * basis[0]
    for col in range(1, ITERS):
        update = update + solved[col] * basis[col]
    return (update, basis[ITERS])


def solution(mesh):
    in_specs = (
        P(None, None, "rx", "ry"),
        P(None, None, "rx", "ry"),
        P("rx", "ry"),
        P("rx", "ry"),
        P(),
    )
    out_specs = (P(None, None, "rx", "ry"), P(None, None, "rx", "ry"))
    return jax.shard_map(body, mesh=mesh, in_specs=in_specs, out_specs=out_specs, check_vma=False)
```

profile of v0, /device:TPU:1, one launch (start us, length us, event | category | flops | bytes accessed | tf_op | source)
XLA Modules:
  0.0 887.2 jit_solution(422260823760097853)
XLA Ops:
  2.4 81.4 %psum.70 = f32[]{:T(128)} all-reduce(f32[]{:T(128)} %multiply_reduce_fusion.9), channel_id=1, replica_groups=mesh['rx'=8,'ry'=32] {'rx','ry'}, use_global_device_ids=true, to_apply=%region_1.0 | all-reduce | flops 1 | bytes 8 | tf_op jit(solution)/shard_map/psum | solution.py:79
  92.2 6.0 collective-permute-done.1
  99.6 4.4 multiply_bitcast_fusion.4
  105.8 4.4 multiply_bitcast_fusion.5
  112.3 3.0 collective-permute-start.2
  122.1 77.1 %psum.71 = f32[]{:T(128)} all-reduce(f32[]{:T(128)} %multiply_reduce_fusion.8), channel_id=1, replica_groups=mesh['rx'=8,'ry'=32] {'rx','ry'}, use_global_device_ids=true, to_apply=%region_3.4 | all-reduce | flops 1 | bytes 8 | tf_op jit(solution)/shard_map/psum | solution.py:97
  200.7 73.2 %psum.72 = f32[]{:T(128)} all-reduce(f32[]{:T(128)} %get-tuple-element.8), channel_id=1, replica_groups=mesh['rx'=8,'ry'=32] {'rx','ry'}, use_global_device_ids=true, to_apply=%region_5.6 | all-reduce | flops 1 | bytes 8 | tf_op jit(solution)/shard_map/psum | solution.py:100
  281.4 5.7 collective-permute-done.5
  288.5 4.4 multiply_bitcast_fusion.2
  294.9 4.4 multiply_bitcast_fusion.3
  301.6 3.9 collective-permute-start.6
  307.0 3.3 collective-permute-start.7
  313.2 76.8 %psum.73 = f32[]{:T(128)} all-reduce(f32[]{:T(128)} %multiply_reduce_fusion.6), channel_id=1, replica_groups=mesh['rx'=8,'ry'=32] {'rx','ry'}, use_global_device_ids=true, to_apply=%region_7.8 | all-reduce | flops 1 | bytes 8 | tf_op jit(solution)/shard_map/psum | solution.py:97
  391.4 72.4 %psum.74 = f32[]{:T(128)} all-reduce(f32[]{:T(128)} %multiply_reduce_fusion.5), channel_id=1, replica_groups=mesh['rx'=8,'ry'=32] {'rx','ry'}, use_global_device_ids=true, to_apply=%region_9.10 | all-reduce | flops 1 | bytes 8 | tf_op jit(solution)/shard_map/psum | solution.py:97
  466.0 73.7 %psum.75 = f32[]{:T(128)} all-reduce(f32[]{:T(128)} %get-tuple-element.6), channel_id=1, replica_groups=mesh['rx'=8,'ry'=32] {'rx','ry'}, use_global_device_ids=true, to_apply=%region_11.12 | all-reduce | flops 1 | bytes 8 | tf_op jit(solution)/shard_map/psum | solution.py:100
  548.4 4.4 collective-permute-done.9
  554.3 4.4 multiply_bitcast_fusion
  560.7 4.4 multiply_bitcast_fusion.1
  567.1 3.9 collective-permute-start.10
  572.6 3.4 collective-permute-start.11
  578.3 77.4 %psum.76 = f32[]{:T(128)} all-reduce(f32[]{:T(128)} %get-tuple-element.4), channel_id=1, replica_groups=mesh['rx'=8,'ry'=32] {'rx','ry'}, use_global_device_ids=true, to_apply=%region_13.14 | all-reduce | flops 1 | bytes 8 | tf_op jit(solution)/shard_map/psum | solution.py:97
  657.0 72.6 %psum.77 = f32[]{:T(128)} all-reduce(f32[]{:T(128)} %multiply_reduce_fusion.2), channel_id=1, replica_groups=mesh['rx'=8,'ry'=32] {'rx','ry'}, use_global_device_ids=true, to_apply=%region_15.16 | all-reduce | flops 1 | bytes 8 | tf_op jit(solution)/shard_map/psum | solution.py:97
  732.3 73.5 %psum.78 = f32[]{:T(128)} all-reduce(f32[]{:T(128)} %get-tuple-element.2), channel_id=1, replica_groups=mesh['rx'=8,'ry'=32] {'rx','ry'}, use_global_device_ids=true, to_apply=%region_17.18 | all-reduce | flops 1 | bytes 8 | tf_op jit(solution)/shard_map/psum | solution.py:97
  808.6 73.8 %psum.79 = f32[]{:T(128)} all-reduce(f32[]{:T(128)} %multiply_reduce_fusion), channel_id=1, replica_groups=mesh['rx'=8,'ry'=32] {'rx','ry'}, use_global_device_ids=true, to_apply=%region_19.20 | all-reduce | flops 1 | bytes 8 | tf_op jit(solution)/shard_map/psum | solution.py:100
  (119 shorter events, 62.2 us)
Async XLA Ops:
  0.6 89.5 %copy-start.1 = (f32[10,2,8,512]{3,2,1,0:T(8,128)S(1)}, f32[10,2,8,512]{3,2,1,0:T(8,128)}, u32[]{:S(2)}) copy-start(f32[10,2,8,512]{3,2,1,0:T(8,128)} %param.6) | copy-start | bytes 983044
  0.6 91.5 %copy-start.3 = (f32[2,12,12]{2,0,1:T(2,128)S(1)}, f32[2,12,12]{2,0,1:T(2,128)}, u32[]{:S(2)}) copy-start(f32[2,12,12]{2,0,1:T(2,128)} %param.9) | copy-start | bytes 3460
  85.5 5.4 collective-permute-start
  90.9 7.3 collective-permute-start.1
  112.3 4.2 collective-permute-start.2
  115.8 3.7 copy-start.2
  115.8 5.6 copy-start
  116.9 4.4 collective-permute-start.3
  274.7 5.4 collective-permute-start.4
  280.0 7.0 collective-permute-start.5
  301.6 5.1 collective-permute-start.6
  307.0 5.3 collective-permute-start.7
  540.4 5.4 collective-permute-start.8
  545.8 7.0 collective-permute-start.9
  567.1 5.1 collective-permute-start.10
  572.6 4.9 collective-permute-start.11
where the time goes:
time: 899 us; the launch traced here: 887 us
  blocking collectives  752 us (84%)
  starting transfers between devices  31.9 us (4%)
  other arithmetic  26.8 us (3%)
  waiting for transfers between devices  26.6 us (3%)
  matrix products  26.2 us (3%)
  between operations  13.2 us (1%)
  local copies, waits for them, and re-layouts  10.5 us (1%)
    psum x6, blocking collectives, body(): single = lax.psum(jnp.sum(work * basis[row]), ('rx', 'ry'))  450 us
    psum x3, blocking collectives, body(): length = jnp.sqrt(lax.psum(jnp.sum(work * work), ('rx', 'ry')))  221 us
    psum x1, blocking collectives, body(): norm0 = jnp.sqrt(lax.psum(jnp.sum(rhs * rhs), ('rx', 'ry')))  81.4 us
    ppermute x12, starting transfers between devices, passed_along(): return lax.ppermute(shard, axis, pairs)  31.9 us
    ppermute x12, waiting for transfers between devices, passed_along(): return lax.ppermute(shard, axis, pairs)  26.6 us
    dot_general x6, matrix products, element_apply(): jnp.einsum('pq,qlrc->plrc', stiff[tri], local, precision=lax.Precision.HI...  26.2 us
  transfers between devices with their start and end apart: 12, of which 11 were waited for; matrix products, arithmetic and copies ran while one was open for 0% of the time, Pallas kernels for 0%

commit v1 on v0

v1 whole, which is shorter than its diff:
```python
import functools

import jax
import jax.numpy as jnp
from jax import lax
from jax.experimental import pallas as pl
from jax.experimental.pallas import tpu as pltpu
from jax.sharding import PartitionSpec as P


DEPTH = 3
NROW = 8 + 2 * DEPTH
LANES = 640
HALF = 80
BLOCK = 2 * HALF
GROUPS = 144
VMEM_LIMIT = 56 * 1024 * 1024


def shift_of(stiff):
    rows = lax.broadcasted_iota(jnp.int32, (12, 12), 0)
    cols = lax.broadcasted_iota(jnp.int32, (12, 12), 1)
    trace = jnp.sum(jnp.where(rows == cols, stiff[0] + stiff[1], 0.0))
    return 1.0 + trace * (1.2 * 10.0 / 22.0)


def own_row(out, rhs, visc, mask, fric, row):
    ice = mask[row : row + 1, :].astype(jnp.float32)
    out[0:22, 0:512] = rhs[:, row, :]
    out[22:23, 0:512] = jnp.ones_like(ice)
    out[23:24, 0:512] = fric[row : row + 1, :]
    out[24:34, 0:512] = visc[:, 0, row, :] * ice
    out[34:44, 0:512] = visc[:, 1, row, :] * ice
    out[44:48, 0:512] = jnp.zeros((4, 512), jnp.float32)


def rows_kernel(rhs, visc, mask, fric, up, down):
    for j in range(DEPTH):
        own_row(up.at[j], rhs, visc, mask, fric, 8 - DEPTH + j)
        own_row(down.at[j], rhs, visc, mask, fric, j)


def cols_kernel(rhs, visc, mask, fric, low, high, right, left, work):
    lane = lax.broadcasted_iota(jnp.int32, (48, 128), 1)
    to_right = jnp.zeros((48, 128), jnp.float32)
    to_left = jnp.zeros((48, 128), jnp.float32)
    for i in range(NROW):
        if i < DEPTH:
            row = low.at[i]
        elif i >= 8 + DEPTH:
            row = high.at[i - 8 - DEPTH]
        else:
            own_row(work, rhs, visc, mask, fric, i - DEPTH)
            row = work
        here = (lane >= 8 * i) & (lane < 8 * i + DEPTH)
        first = row[:, 0:128]
        last = row[:, 384:512]
        to_right = jnp.where(here, pltpu.roll(last, (8 * i + DEPTH) % 128, 1), to_right)
        to_left = jnp.where(here, pltpu.roll(first, 8 * i, 1) if i else first, to_left)
    right[...] = to_right
    left[...] = to_left


def weights_kernel(stiff, weights):
    row = lax.broadcasted_iota(jnp.int32, (GROUPS, 12), 0)
    col = lax.broadcasted_iota(jnp.int32, (GROUPS, 12), 1)

    def of_row(r):
        group, plane = (r // 24, r % 24)
        slot, lev = (group // 2, group % 2)
        comp, level = (plane // 11, plane % 11)
        layer = level - lev
        good = (plane < 22) & (layer >= 0) & (layer < 10)
        return comp * 6 + lev * 3 + slot, layer, good

    pick = jnp.where(of_row(row)[0] == col, 1.0, 0.0)
    r = lax.broadcasted_iota(jnp.int32, (GROUPS, 3 * HALF), 0)
    k = lax.broadcasted_iota(jnp.int32, (GROUPS, 3 * HALF), 1)
    _, layer, good = of_row(r)
    part = (k % HALF) // 24
    plane = (k % HALF) % 24
    lev_in = plane % 11 - layer
    good = good & (part < 3) & (plane < 22)
    q = lax.broadcasted_iota(jnp.int32, (12, 3 * HALF), 0)
    kq = lax.broadcasted_iota(jnp.int32, (12, 3 * HALF), 1)
    comp_in = ((kq % HALF) % 24) // 11
    block = kq // HALF
    for tri in range(2):
        first, second, third = ((0, 2, 1), (2, 0, 1))[tri]
        place = jnp.where(block == 0, first, jnp.where(block == 1, second, third))
        rows = jnp.dot(
            pick, stiff[tri], precision=lax.Precision.HIGHEST, preferred_element_type=jnp.float32
        )
        total = jnp.zeros((GROUPS, 3 * HALF), jnp.float32)
        for lev in range(2):
            sel = jnp.where(comp_in * 6 + lev * 3 + place == q, 1.0, 0.0)
            spread = jnp.dot(
                rows, sel, precision=lax.Precision.HIGHEST, preferred_element_type=jnp.float32
            )
            total = jnp.where(good & (lev_in == lev), spread, total)
        high = total.astype(jnp.bfloat16).astype(jnp.float32)
        weights[tri] = jnp.where(part == 2, total - high, high).astype(jnp.bfloat16)


def split_rows(x):
    high = x.astype(jnp.bfloat16).astype(jnp.float32)
    pad = jnp.zeros((HALF - 72, x.shape[1]), jnp.float32)
    return jnp.concatenate([high, x - high, high, pad], axis=0).astype(jnp.bfloat16)


def put_operand(operand, i, x):
    start = pl.multiple_of(i * BLOCK, BLOCK)
    operand[pl.ds(start, HALF), :] = split_rows(x)
    operand[pl.ds(start + HALF, HALF), :] = split_rows(pltpu.roll(x, LANES - 1, 1))


def main_kernel(
    rhs, visc, mask, fric, low, high, from_left, from_right, stiff, weights,
    powers, gram,
    full, scale, diag, field, operand, carry,
):
    lane = lax.broadcasted_iota(jnp.int32, (48, 128), 1)
    theta = shift_of(stiff)
    plane = lax.broadcasted_iota(jnp.int32, (24, LANES), 0)
    bottom = (plane == 0) | (plane == 11)
    for i in range(NROW):
        row = full.at[i]
        if i < DEPTH:
            row[:, 0:512] = low[i]
        elif i >= 8 + DEPTH:
            row[:, 0:512] = high[i - 8 - DEPTH]
        else:
            own_row(row, rhs, visc, mask, fric, i - DEPTH)
        on_right = from_right[...]
        on_right = pltpu.roll(on_right, 128 - 8 * i, 1) if i else on_right
        on_left = pltpu.roll(from_left[...], (128 - DEPTH - 8 * i) % 128, 1)
        row[:, 512:640] = jnp.where(
            lane < DEPTH, on_right, jnp.where(lane >= 128 - DEPTH, on_left, 0.0)
        )
        real = row[22:23, :]
        x = jnp.where(plane < 22, row[0:24, :], 0.0)
        field[0, i] = x
        put_operand(operand.at[0], i, x)
        diag[i] = real * (1.0 - theta) + jnp.where(bottom, row[23:24, :], 0.0)
        if i < NROW - 1:
            for tri in range(2):
                coef = row[24 + 10 * tri : 34 + 10 * tri, :]
                for lev in range(2):
                    base = 48 * tri + 24 * lev
                    out = scale.at[i]
                    out[base : base + 24, :] = jnp.zeros((24, LANES), jnp.float32)
                    out[base + lev : base + lev + 10, :] = coef
                    out[base + 11 + lev : base + 21 + lev, :] = coef

    for step in range(1, DEPTH + 1):
        source = operand.at[(step - 1) % 2]
        target = operand.at[step % 2]
        carry[...] = jnp.zeros_like(carry)

        def cell_row(i, _, step=step, source=source, target=target):
            start = pl.multiple_of(i * BLOCK, BLOCK)
            mixed = [
                jnp.dot(
                    weights[tri],
                    source[pl.ds(start + HALF * tri, 3 * HALF), :],
                    preferred_element_type=jnp.float32,
                )
                for tri in range(2)
            ]
            grown = []
            for tri in range(2):
                upper = scale[i, 48 * tri : 48 * tri + 24, :]
                lower = scale[i, 48 * tri + 24 : 48 * tri + 48, :]
                for slot in range(3):
                    at = 48 * slot
                    grown.append(
                        upper * mixed[tri][at : at + 24] + lower * mixed[tri][at + 24 : at + 48]
                    )
            near = grown[0] + carry[0]
            far = grown[2] + grown[5] + carry[1]
            carry[0] = grown[1] + grown[3]
            carry[1] = grown[4]
            total = near + pltpu.roll(far, 1, 1)
            x = full[i, 22:23, :] * total + diag[i] * field[step - 1, i]
            field[step, i] = x
            if step < DEPTH:
                put_operand(target, i, x)
            return 0

        lax.fori_loop(step - 1, NROW - step, cell_row, 0)

    pairs = [(a, b) for a in range(4) for b in range(a, 4)]

    def add_row(r, sums):
        vectors = [field[a, r + DEPTH, :, 0:512] for a in range(4)]
        result = []
        for total, (a, b) in zip(sums, pairs):
            product = vectors[a] * vectors[b]
            for s in range(3):
                for l in range(4):
                    total = total + product[8 * s : 8 * s + 8, 128 * l : 128 * l + 128]
            result.append(total)
        for a in range(1, 4):
            powers[a - 1, r] = vectors[a]
        return tuple(result)

    sums = lax.fori_loop(
        0, 8, add_row, tuple(jnp.zeros((8, 128), jnp.float32) for _ in pairs)
    )
    place = lax.broadcasted_iota(jnp.int32, (8, 128), 1)
    line = jnp.zeros((8, 128), jnp.float32)
    for n, total in enumerate(sums):
        line = jnp.where(place == n, jnp.sum(total), line)
    devices = gram.shape[0]
    gram[...] = jnp.broadcast_to(line[0:1], (devices, 128))


def combine_kernel(rhs, powers, grams, stiff, update, last):
    theta = shift_of(stiff)
    entry = jnp.sum(grams[...], axis=0, keepdims=True)
    place = lax.broadcasted_iota(jnp.int32, (1, 128), 1)
    pairs = [(a, b) for a in range(4) for b in range(a, 4)]
    g = {}
    for n, pair in enumerate(pairs):
        g[pair] = jnp.sum(jnp.where(place == n, entry, 0.0), axis=1, keepdims=True)
    upper = [[None] * 4 for _ in range(4)]
    for a in range(4):
        for b in range(a, 4):
            value = g[a, b]
            for c in range(a):
                value = value - upper[c][a] * upper[c][b]
            if a == b:
                upper[a][a] = jnp.sqrt(value)
            else:
                upper[a][b] = value / upper[a][a]
    zero = jnp.zeros((1, 1), jnp.float32)
    table = [
        [
            (upper[a][b + 1] if a <= b + 1 else zero) + (theta * upper[a][b] if a <= b else zero)
            for b in range(3)
        ]
        for a in range(4)
    ]
    target = [upper[0][0], zero, zero, zero]
    for col in range(3):
        first, second = (table[col][col], table[col + 1][col])
        radius = jnp.sqrt(first * first + second * second)
        cosine, sine = (first / radius, second / radius)
        for c in range(col, 3):
            one, two = (table[col][c], table[col + 1][c])
            table[col][c] = cosine * one + sine * two
            table[col + 1][c] = cosine * two - sine * one
        one, two = (target[col], target[col + 1])
        target[col] = cosine * one + sine * two
        target[col + 1] = cosine * two - sine * one
    z = [None] * 3
    for col in (2, 1, 0):
        value = target[col]
        for c in range(col + 1, 3):
            value = value - table[col][c] * z[c]
        z[col] = value / table[col][col]
    w = [None] * 4
    w[3] = 1.0 / upper[3][3]
    for a in (2, 1, 0):
        value = zero
        for c in range(a + 1, 4):
            value = value - upper[a][c] * w[c]
        w[a] = value / upper[a][a]
    for r in range(8):
        one = rhs[:, r, :]
        rest = [powers[a, r, 0:22, :] for a in range(3)]
        update[:, r, :] = z[0] * one + z[1] * rest[0] + z[2] * rest[1]
        last[:, r, :] = w[0] * one + w[1] * rest[0] + w[2] * rest[1] + w[3] * rest[2]


def call(kernel, outs, scratch=(), flops=0, bytes_accessed=0):
    single = not isinstance(outs, (list, tuple))
    return pl.pallas_call(
        kernel,
        out_shape=outs if single else tuple(outs),
        scratch_shapes=list(scratch),
        compiler_params=pltpu.CompilerParams(vmem_limit_bytes=VMEM_LIMIT),
        cost_estimate=pl.CostEstimate(
            flops=flops, bytes_accessed=bytes_accessed, transcendentals=0
        ),
    )


def f32(*shape):
    return jax.ShapeDtypeStruct(shape, jnp.float32)


def passed_along(shard, axis, by):
    devices = lax.axis_size(axis)
    pairs = [(i, i + by) for i in range(devices) if 0 <= i + by < devices]
    return lax.ppermute(shard, axis, pairs)


def body(rhs, viscosity, cell_mask, friction, stiffness):
    devices = lax.axis_size("rx") * lax.axis_size("ry")
    field = rhs.reshape(22, 8, 512)
    local = (field, viscosity, cell_mask, friction)
    weights = call(
        weights_kernel, jax.ShapeDtypeStruct((2, GROUPS, 3 * HALF), jnp.bfloat16), flops=10**7, bytes_accessed=10**5
    )(stiffness)
    up, down = call(rows_kernel, (f32(DEPTH, 48, 512),) * 2, bytes_accessed=10**6)(*local)
    low = passed_along(up, "rx", 1)
    high = passed_along(down, "rx", -1)
    right, left = call(
        cols_kernel, (f32(48, 128),) * 2, [pltpu.VMEM((48, 512), jnp.float32)], bytes_accessed=10**6
    )(*local, low, high)
    from_left = passed_along(right, "ry", 1)
    from_right = passed_along(left, "ry", -1)
    powers, gram = call(
        main_kernel,
        (f32(3, 8, 24, 512), f32(devices, 128)),
        [
            pltpu.VMEM((NROW, 48, LANES), jnp.float32),
            pltpu.VMEM((NROW - 1, 96, LANES), jnp.float32),
            pltpu.VMEM((NROW, 24, LANES), jnp.float32),
            pltpu.VMEM((4, NROW, 24, LANES), jnp.float32),
            pltpu.VMEM((2, NROW * BLOCK, LANES), jnp.bfloat16),
            pltpu.VMEM((2, 24, LANES), jnp.float32),
        ],
        flops=3 * 10**9,
        bytes_accessed=3 * 10**6,
    )(*local, low, high, from_left, from_right, stiffness, weights)
    grams = lax.all_to_all(gram.reshape(devices, 1, 128), ("rx", "ry"), 0, 0)
    update, last = call(combine_kernel, (f32(22, 8, 512),) * 2, bytes_accessed=3 * 10**6)(
        field, powers, grams.reshape(devices, 128), stiffness
    )
    return update.reshape(2, 11, 8, 512), last.reshape(2, 11, 8, 512)


def solution(mesh):
    in_specs = (
        P(None, None, "rx", "ry"),
        P(None, None, "rx", "ry"),
        P("rx", "ry"),
        P("rx", "ry"),
        P(),
    )
    out_specs = (P(None, None, "rx", "ry"), P(None, None, "rx", "ry"))
    return jax.shard_map(body, mesh=mesh, in_specs=in_specs, out_specs=out_specs, check_vma=False)
```

time: 899 us -> 78.6 us (0.09); the launches traced: 887 us -> 78.2 us
  blocking collectives: 752 us -> 29.2 us
  Pallas kernels: 0 us -> 28.2 us
  other arithmetic: 26.8 us -> 0 us
  matrix products: 26.2 us -> 0 us
  starting transfers between devices: 31.9 us -> 11.3 us
  waiting for transfers between devices: 26.6 us -> 6.75 us
  between operations: 13.2 us -> 0.69 us
    psum x10 -> x0, blocking collectives: 752 us -> none  [the longest x6 450 us: body(): single = lax.psum(jnp.sum(work * basis[row]), ('rx', 'ry'))]
    all_to_all x0 -> x1, blocking collectives: none -> 29.2 us  [body(): grams = lax.all_to_all(gram.reshape(devices, 1, 128), ('rx', 'ry'), 0, 0)]
    pallas_call x0 -> x5, Pallas kernels: none -> 28.2 us  [the longest x1 18.4 us: body(): call(main_kernel, (f32(3, 8, 24, 512), f32(devices, 128)), [pltpu.VMEM((N...]
    dot_general x6 -> x0, matrix products: 26.2 us -> none  [element_apply(): jnp.einsum('pq,qlrc->plrc', stiff[tri], local, precision=lax.Precision.HI...]
    ppermute x12 -> x4, starting transfers between devices: 31.9 us -> 11.3 us  [passed_along(): return lax.ppermute(shard, axis, pairs)]
    ppermute x12 -> x4, waiting for transfers between devices: 26.6 us -> 6.75 us  [passed_along(): return lax.ppermute(shard, axis, pairs)]
    reduce_sum x10 -> x0, other arithmetic: 13.7 us -> none  [the longest x6 7.04 us: body(): single = lax.psum(jnp.sum(work * basis[row]), ('rx', 'ry'))]
  transfers between devices with their start and end apart: 12 -> 4, of which waited for: 11 -> 3; matrix products, arithmetic and copies ran while one was open for 0% -> 1% of each run, Pallas kernels for 0% -> 3%
where the time goes in v1:
time: 78.6 us; the launch traced here: 78.2 us
  blocking collectives  29.2 us (37%)
  Pallas kernels  28.2 us (36%)
  starting transfers between devices  11.3 us (14%)
  waiting for transfers between devices  6.75 us (9%)
  local copies, waits for them, and re-layouts  2.09 us (3%)
    all_to_all x1, blocking collectives, body(): grams = lax.all_to_all(gram.reshape(devices, 1, 128), ('rx', 'ry'), 0, 0)  29.2 us
    pallas_call x1, Pallas kernels, body(): call(main_kernel, (f32(3, 8, 24, 512), f32(devices, 128)), [pltpu.VMEM((N...  18.4 us
    ppermute x4, starting transfers between devices, passed_along(): return lax.ppermute(shard, axis, pairs)  11.3 us
    ppermute x4, waiting for transfers between devices, passed_along(): return lax.ppermute(shard, axis, pairs)  6.75 us
    pallas_call x1, Pallas kernels, body(): call(combine_kernel, (f32(22, 8, 512),) * 2, bytes_accessed=3 * 10 ** 6)  2.92 us
    pallas_call x1, Pallas kernels, body(): call(weights_kernel, jax.ShapeDtypeStruct((2, GROUPS, 3 * HALF), jnp.bflo...  2.6 us
    pallas_call x1, Pallas kernels, body(): call(cols_kernel, (f32(48, 128),) * 2, [pltpu.VMEM((48, 512), jnp.float32...  2.25 us
    unnamed x11, local copies, waits for them, and re-layouts  2.09 us
  transfers between devices with their start and end apart: 4, of which 3 were waited for; matrix products, arithmetic and copies ran while one was open for 1% of the time, Pallas kernels for 3%

profile of v1, /device:TPU:1, one launch (start us, length us, event | category | flops | bytes accessed | tf_op | source)
XLA Modules:
  0.0 78.2 jit_solution(6447206732431420642)
XLA Ops:
  0.6 0.0 copy-start.2
  0.6 2.0 %shard_map.68 = (f32[3,48,512]{2,1,0:T(8,128)}, f32[3,48,512]{2,1,0:T(8,128)}) custom-call(f32[22,8,512]{2,1,0:T(8,128)} %bitcast.7, f32[10,2,8,512]{3,2,1,0:T(8,128)} %visc.5, s32[8,512]{1,0:T(8,128)} %mask.5, f32[8,512]{1,0:T(8,128)} %fric.5), custom_call_target="tpu_custom_call" | custom-call | bytes 1000000 | tf_op jit(solution)/shard_map/pallas_call | solution.py:306
  2.7 4.5 %collective-permute-start = (f32[3,48,512]{2,1,0:T(8,128)}, f32[3,48,512]{2,1,0:T(8,128)S(1)}, u32[]{:S(2)}, u32[]{:S(2)}) collective-permute-start(f32[3,48,512]{2,1,0:T(8,128)} %get-tuple-element.10), channel_id=1, source_target_pairs={{0,32},{32,64},{64,96},{96,128},{128,160},{160,192},{192,224},{1,3... | collective-permute-start | bytes 884744 | tf_op jit(solution)/shard_map/ppermute | solution.py:296
  7.2 1.9 %collective-permute-start.1 = (f32[3,48,512]{2,1,0:T(8,128)}, f32[3,48,512]{2,1,0:T(8,128)S(1)}, u32[]{:S(2)}, u32[]{:S(2)}) collective-permute-start(f32[3,48,512]{2,1,0:T(8,128)} %get-tuple-element.11), channel_id=1, source_target_pairs={{32,0},{64,32},{96,64},{128,96},{160,128},{192,160},{224,192},{33,... | collective-permute-start | bytes 884744 | tf_op jit(solution)/shard_map/ppermute | solution.py:296
  9.1 2.0 %collective-permute-done.low = f32[3,48,512]{2,1,0:T(8,128)S(1)} collective-permute-done((f32[3,48,512]{2,1,0:T(8,128)}, f32[3,48,512]{2,1,0:T(8,128)S(1)}, u32[]{:S(2)}, u32[]{:S(2)}) %collective-permute-start) | collective-permute-done | bytes 294944 | tf_op jit(solution)/shard_map/ppermute | solution.py:296
  11.1 0.0 copy-start
  11.1 4.3 %collective-permute-done.1.high = f32[3,48,512]{2,1,0:T(8,128)S(1)} collective-permute-done((f32[3,48,512]{2,1,0:T(8,128)}, f32[3,48,512]{2,1,0:T(8,128)S(1)}, u32[]{:S(2)}, u32[]{:S(2)}) %collective-permute-start.1) | collective-permute-done | bytes 294944 | tf_op jit(solution)/shard_map/ppermute | solution.py:296
  15.4 0.0 copy-done
  15.4 0.0 copy-start.1
  15.4 0.7 copy-done.1
  16.1 2.2 %shard_map.69 = (f32[48,128]{1,0:T(8,128)}, f32[48,128]{1,0:T(8,128)}) custom-call(f32[22,8,512]{2,1,0:T(8,128)} %bitcast.8, f32[10,2,8,512]{3,2,1,0:T(8,128)} %visc.5, s32[8,512]{1,0:T(8,128)} %mask.5, f32[8,512]{1,0:T(8,128)} %fric.5, f32[3,48,512]{2,1,0:T(8,128)} %copy-done, f32[3,48,512]{2,1,0:T(8,128)} %copy-done.1), custom_call_target="tpu_custom_call" | custom-call | bytes 1000000 | tf_op jit(solution)/shard_map/pallas_call | solution.py:309
  18.4 3.5 %collective-permute-start.2 = (f32[48,128]{1,0:T(8,128)}, f32[48,128]{1,0:T(8,128)S(1)}, u32[]{:S(2)}, u32[]{:S(2)}) collective-permute-start(f32[48,128]{1,0:T(8,128)} %get-tuple-element.12), channel_id=1, source_target_pairs={{0,1},{1,2},{2,3},{3,4},{4,5},{5,6},{6,7},{7,8},{8,9},{9,10},{10,1... | collective-permute-start | bytes 73736 | tf_op jit(solution)/shard_map/ppermute | solution.py:296
  21.9 1.3 %collective-permute-start.3 = (f32[48,128]{1,0:T(8,128)}, f32[48,128]{1,0:T(8,128)S(1)}, u32[]{:S(2)}, u32[]{:S(2)}) collective-permute-start(f32[48,128]{1,0:T(8,128)} %get-tuple-element.13), channel_id=1, source_target_pairs={{1,0},{2,1},{3,2},{4,3},{5,4},{6,5},{7,6},{8,7},{9,8},{10,9},{11,1... | collective-permute-start | bytes 73736 | tf_op jit(solution)/shard_map/ppermute | solution.py:296
  23.2 0.0 copy-done.2
  23.2 0.6 copy.11.stiff
  23.8 2.6 %shard_map.70.weights = bf16[2,144,240]{2,1,0:T(8,128)(2,1)} custom-call(f32[2,12,12]{2,1,0:T(8,128)} %copy.11.stiff), custom_call_target="tpu_custom_call" | custom-call | flops 10000000 | bytes 100000 | tf_op jit(solution)/shard_map/pallas_call | solution.py:303
  26.4 0.0 collective-permute-done.2.from_left
  26.4 0.0 copy-start.3
  26.4 0.5 collective-permute-done.3.from_right
  26.9 0.2 copy-done.3
  27.1 0.6 copy-done.4
  27.7 18.4 %shard_map.71 = (f32[3,8,24,512]{3,2,1,0:T(8,128)}, f32[256,128]{1,0:T(8,128)}) custom-call(f32[22,8,512]{2,1,0:T(8,128)} %bitcast.9, f32[10,2,8,512]{3,2,1,0:T(8,128)} %visc.5, s32[8,512]{1,0:T(8,128)} %mask.5, f32[8,512]{1,0:T(8,128)} %fric.5, f32[3,48,512]{2,1,0:T(8,128)} %copy-done, f32[3,48,512]{2,1,0:T(8,128)} %copy-done.1, f32[48,128]{1,0:T(8,128)} %copy-done.3, ...), custom_call_target="tpu_custom_call" | custom-call | flops 3000000000 | bytes 3000000 | tf_op jit(solution)/shard_map/pallas_call | solution.py:314
  46.1 29.2 %all_to_all.5 = f32[256,1,128]{2,1,0:T(1,128)} all-to-all(f32[256,1,128]{2,1,0:T(1,128)} %bitcast.12), channel_id=1, replica_groups=mesh['rx'=8,'ry'=32] {'rx','ry'}, dimensions={0} | all-to-all | bytes 262144 | tf_op jit(solution)/shard_map/all_to_all | solution.py:328
  75.3 2.9 %shard_map.72 = (f32[22,8,512]{2,1,0:T(8,128)}, f32[22,8,512]{2,1,0:T(8,128)}) custom-call(f32[22,8,512]{2,1,0:T(8,128)} %bitcast.10, f32[3,8,24,512]{3,2,1,0:T(8,128)} %get-tuple-element.14.powers, f32[256,128]{1,0:T(8,128)} %bitcast.11, f32[2,12,12]{2,1,0:T(8,128)} %copy.11.stiff), custom_call_target="tpu_custom_call" | custom-call | bytes 3000000 | tf_op jit(solution)/shard_map/pallas_call | solution.py:329
  (1 shorter events, 0.0 us)
Async XLA Ops:
  0.6 22.6 %copy-start.2 = (f32[2,12,12]{2,0,1:T(2,128)S(1)}, f32[2,12,12]{2,0,1:T(2,128)}, u32[]{:S(2)}) copy-start(f32[2,12,12]{2,0,1:T(2,128)} %param.9) | copy-start | bytes 3460
  2.7 8.5 %collective-permute-start = (f32[3,48,512]{2,1,0:T(8,128)}, f32[3,48,512]{2,1,0:T(8,128)S(1)}, u32[]{:S(2)}, u32[]{:S(2)}) collective-permute-start(f32[3,48,512]{2,1,0:T(8,128)} %get-tuple-element.10), channel_id=1, source_target_pairs={{0,32},{32,64},{64,96},{96,128},{128,160},{160,192},{192,224},{1,3... | collective-permute-start | bytes 884744 | tf_op jit(solution)/shard_map/ppermute | solution.py:296
  7.2 8.3 %collective-permute-start.1 = (f32[3,48,512]{2,1,0:T(8,128)}, f32[3,48,512]{2,1,0:T(8,128)S(1)}, u32[]{:S(2)}, u32[]{:S(2)}) collective-permute-start(f32[3,48,512]{2,1,0:T(8,128)} %get-tuple-element.11), channel_id=1, source_target_pairs={{32,0},{64,32},{96,64},{128,96},{160,128},{192,160},{224,192},{33,... | collective-permute-start | bytes 884744 | tf_op jit(solution)/shard_map/ppermute | solution.py:296
  11.1 4.3 %copy-start = (f32[3,48,512]{2,1,0:T(8,128)}, f32[3,48,512]{2,1,0:T(8,128)S(1)}, u32[]{:S(2)}) copy-start(f32[3,48,512]{2,1,0:T(8,128)S(1)} %collective-permute-done.low) | copy-start | bytes 884740
  15.4 0.7 copy-start.1
  18.4 8.1 %collective-permute-start.2 = (f32[48,128]{1,0:T(8,128)}, f32[48,128]{1,0:T(8,128)S(1)}, u32[]{:S(2)}, u32[]{:S(2)}) collective-permute-start(f32[48,128]{1,0:T(8,128)} %get-tuple-element.12), channel_id=1, source_target_pairs={{0,1},{1,2},{2,3},{3,4},{4,5},{5,6},{6,7},{7,8},{8,9},{9,10},{10,1... | collective-permute-start | bytes 73736 | tf_op jit(solution)/shard_map/ppermute | solution.py:296
  21.9 5.0 %collective-permute-start.3 = (f32[48,128]{1,0:T(8,128)}, f32[48,128]{1,0:T(8,128)S(1)}, u32[]{:S(2)}, u32[]{:S(2)}) collective-permute-start(f32[48,128]{1,0:T(8,128)} %get-tuple-element.13), channel_id=1, source_target_pairs={{1,0},{2,1},{3,2},{4,3},{5,4},{6,5},{7,6},{8,7},{9,8},{10,9},{11,1... | collective-permute-start | bytes 73736 | tf_op jit(solution)/shard_map/ppermute | solution.py:296
  26.4 0.6 copy-start.3
  27.1 0.6 copy-start.4

commit v2 on v1

--- a/solution.py
+++ b/solution.py
@@ -1,5 +1,3 @@
-import functools
-
 import jax
 import jax.numpy as jnp
 from jax import lax
@@ -14,7 +12,6 @@
 HALF = 80
 BLOCK = 2 * HALF
 GROUPS = 144
-VMEM_LIMIT = 56 * 1024 * 1024
 
 
 def shift_of(stiff):
@@ -34,31 +31,49 @@
     out[44:48, 0:512] = jnp.zeros((4, 512), jnp.float32)
 
 
-def rows_kernel(rhs, visc, mask, fric, up, down):
+def odd_along(axis):
+    return lax.rem(lax.axis_index(axis), 2) == 1
+
+
+def rows_kernel(rhs, visc, mask, fric, first, second, work):
+    odd = odd_along("rx")
     for j in range(DEPTH):
-        own_row(up.at[j], rhs, visc, mask, fric, 8 - DEPTH + j)
-        own_row(down.at[j], rhs, visc, mask, fric, j)
-
-
-def cols_kernel(rhs, visc, mask, fric, low, high, right, left, work):
+        own_row(work.at[0], rhs, visc, mask, fric, 8 - DEPTH + j)
+        own_row(work.at[1], rhs, visc, mask, fric, j)
+        up, down = (work[0], work[1])
+        first[j] = jnp.where(odd, down, up)
+        second[j] = jnp.where(odd, up, down)
+
+
+def pack_row(row, i, lane, packs):
+    here = (lane >= 8 * i) & (lane < 8 * i + DEPTH)
+    start, end = (row[:, 0:128], row[:, 384:512])
+    to_right = jnp.where(here, pltpu.roll(end, (8 * i + DEPTH) % 128, 1), packs[0])
+    to_left = jnp.where(here, pltpu.roll(start, 8 * i, 1) if i else start, packs[1])
+    return to_right, to_left
+
+
+def own_kernel(rhs, visc, mask, fric, stiff, own, packs, weights):
+    weights_kernel(stiff, weights)
     lane = lax.broadcasted_iota(jnp.int32, (48, 128), 1)
-    to_right = jnp.zeros((48, 128), jnp.float32)
-    to_left = jnp.zeros((48, 128), jnp.float32)
-    for i in range(NROW):
-        if i < DEPTH:
-            row = low.at[i]
-        elif i >= 8 + DEPTH:
-            row = high.at[i - 8 - DEPTH]
-        else:
-            own_row(work, rhs, visc, mask, fric, i - DEPTH)
-            row = work
-        here = (lane >= 8 * i) & (lane < 8 * i + DEPTH)
-        first = row[:, 0:128]
-        last = row[:, 384:512]
-        to_right = jnp.where(here, pltpu.roll(last, (8 * i + DEPTH) % 128, 1), to_right)
-        to_left = jnp.where(here, pltpu.roll(first, 8 * i, 1) if i else first, to_left)
-    right[...] = to_right
-    left[...] = to_left
+    both = (jnp.zeros((48, 128), jnp.float32),) * 2
+    for r in range(8):
+        own_row(own.at[r], rhs, visc, mask, fric, r)
+        both = pack_row(own.at[r], r + DEPTH, lane, both)
+    packs[0], packs[1] = both
+
+
+def cols_kernel(packs, first_rows, second_rows, first, second):
+    odd_row = odd_along("rx")
+    odd = odd_along("ry")
+    lane = lax.broadcasted_iota(jnp.int32, (48, 128), 1)
+    both = (packs[0], packs[1])
+    for j in range(DEPTH):
+        one, two = (first_rows[j], second_rows[j])
+        both = pack_row(jnp.where(odd_row, one, two), j, lane, both)
+        both = pack_row(jnp.where(odd_row, two, one), j + 8 + DEPTH, lane, both)
+    first[...] = jnp.where(odd, both[1], both[0])
+    second[...] = jnp.where(odd, both[0], both[1])
 
 
 def weights_kernel(stiff, weights):
@@ -115,25 +130,29 @@
 
 
 def main_kernel(
-    rhs, visc, mask, fric, low, high, from_left, from_right, stiff, weights,
+    own, first_rows, second_rows, first_cols, second_cols, stiff, weights,
     powers, gram,
     full, scale, diag, field, operand, carry,
 ):
     lane = lax.broadcasted_iota(jnp.int32, (48, 128), 1)
+    odd_row = odd_along("rx")
+    odd_col = odd_along("ry")
+    from_left = jnp.where(odd_col, first_cols[...], second_cols[...])
+    from_right = jnp.where(odd_col, second_cols[...], first_cols[...])
     theta = shift_of(stiff)
     plane = lax.broadcasted_iota(jnp.int32, (24, LANES), 0)
     bottom = (plane == 0) | (plane == 11)
     for i in range(NROW):
         row = full.at[i]
         if i < DEPTH:
-            row[:, 0:512] = low[i]
+            row[:, 0:512] = jnp.where(odd_row, first_rows[i], second_rows[i])
         elif i >= 8 + DEPTH:
-            row[:, 0:512] = high[i - 8 - DEPTH]
+            j = i - 8 - DEPTH
+            row[:, 0:512] = jnp.where(odd_row, second_rows[j], first_rows[j])
         else:
-            own_row(row, rhs, visc, mask, fric, i - DEPTH)
-        on_right = from_right[...]
-        on_right = pltpu.roll(on_right, 128 - 8 * i, 1) if i else on_right
-        on_left = pltpu.roll(from_left[...], (128 - DEPTH - 8 * i) % 128, 1)
+            row[:, 0:512] = own[i - DEPTH]
+        on_right = pltpu.roll(from_right, 128 - 8 * i, 1) if i else from_right
+        on_left = pltpu.roll(from_left, (128 - DEPTH - 8 * i) % 128, 1)
         row[:, 512:640] = jnp.where(
             lane < DEPTH, on_right, jnp.where(lane >= 128 - DEPTH, on_left, 0.0)
         )
@@ -187,7 +206,7 @@
                 put_operand(target, i, x)
             return 0
 
-        lax.fori_loop(step - 1, NROW - step, cell_row, 0)
+        lax.fori_loop(step - 1, NROW - step, cell_row, 0, unroll=True)
 
     pairs = [(a, b) for a in range(4) for b in range(a, 4)]
 
@@ -215,7 +234,7 @@
     gram[...] = jnp.broadcast_to(line[0:1], (devices, 128))
 
 
-def combine_kernel(rhs, powers, grams, stiff, update, last):
+def combine_kernel(own, powers, grams, stiff, update, last):
     theta = shift_of(stiff)
     entry = jnp.sum(grams[...], axis=0, keepdims=True)
     place = lax.broadcasted_iota(jnp.int32, (1, 128), 1)
@@ -267,19 +286,19 @@
             value = value - upper[a][c] * w[c]
         w[a] = value / upper[a][a]
     for r in range(8):
-        one = rhs[:, r, :]
+        one = own[r, 0:22, :]
         rest = [powers[a, r, 0:22, :] for a in range(3)]
         update[:, r, :] = z[0] * one + z[1] * rest[0] + z[2] * rest[1]
         last[:, r, :] = w[0] * one + w[1] * rest[0] + w[2] * rest[1] + w[3] * rest[2]
 
 
-def call(kernel, outs, scratch=(), flops=0, bytes_accessed=0):
+def call(kernel, outs, scratch=(), flops=0, bytes_accessed=0, limit=8):
     single = not isinstance(outs, (list, tuple))
     return pl.pallas_call(
         kernel,
         out_shape=outs if single else tuple(outs),
         scratch_shapes=list(scratch),
-        compiler_params=pltpu.CompilerParams(vmem_limit_bytes=VMEM_LIMIT),
+        compiler_params=pltpu.CompilerParams(vmem_limit_bytes=limit * 1024 * 1024),
         cost_estimate=pl.CostEstimate(
             flops=flops, bytes_accessed=bytes_accessed, transcendentals=0
         ),
@@ -290,27 +309,30 @@
     return jax.ShapeDtypeStruct(shape, jnp.float32)
 
 
-def passed_along(shard, axis, by):
-    devices = lax.axis_size(axis)
-    pairs = [(i, i + by) for i in range(devices) if 0 <= i + by < devices]
+def swapped(shard, axis, start):
+    pairs = []
+    for i in range(start, lax.axis_size(axis) - 1, 2):
+        pairs += [(i, i + 1), (i + 1, i)]
     return lax.ppermute(shard, axis, pairs)
 
 
 def body(rhs, viscosity, cell_mask, friction, stiffness):
     devices = lax.axis_size("rx") * lax.axis_size("ry")
-    field = rhs.reshape(22, 8, 512)
-    local = (field, viscosity, cell_mask, friction)
-    weights = call(
-        weights_kernel, jax.ShapeDtypeStruct((2, GROUPS, 3 * HALF), jnp.bfloat16), flops=10**7, bytes_accessed=10**5
-    )(stiffness)
-    up, down = call(rows_kernel, (f32(DEPTH, 48, 512),) * 2, bytes_accessed=10**6)(*local)
-    low = passed_along(up, "rx", 1)
-    high = passed_along(down, "rx", -1)
-    right, left = call(
-        cols_kernel, (f32(48, 128),) * 2, [pltpu.VMEM((48, 512), jnp.float32)], bytes_accessed=10**6
-    )(*local, low, high)
-    from_left = passed_along(right, "ry", 1)
-    from_right = passed_along(left, "ry", -1)
+    local = (rhs.reshape(22, 8, 512), viscosity, cell_mask, friction)
+    first, second = call(
+        rows_kernel, (f32(DEPTH, 48, 512),) * 2, [pltpu.VMEM((2, 48, 512), jnp.float32)], bytes_accessed=10**6
+    )(*local)
+    first_rows = swapped(first, "rx", 0)
+    second_rows = swapped(second, "rx", 1)
+    own, packs, weights = call(
+        own_kernel,
+        (f32(8, 48, 512), f32(2, 48, 128), jax.ShapeDtypeStruct((2, GROUPS, 3 * HALF), jnp.bfloat16)),
+        flops=10**7,
+        bytes_accessed=10**6,
+    )(*local, stiffness)
+    first, second = call(cols_kernel, (f32(48, 128),) * 2, bytes_accessed=10**6)(packs, first_rows, second_rows)
+    first_cols = swapped(first, "ry", 0)
+    second_cols = swapped(second, "ry", 1)
     powers, gram = call(
         main_kernel,
         (f32(3, 8, 24, 512), f32(devices, 128)),
@@ -324,10 +346,11 @@
         ],
         flops=3 * 10**9,
         bytes_accessed=3 * 10**6,
-    )(*local, low, high, from_left, from_right, stiffness, weights)
+        limit=28,
+    )(own, first_rows, second_rows, first_cols, second_cols, stiffness, weights)
     grams = lax.all_to_all(gram.reshape(devices, 1, 128), ("rx", "ry"), 0, 0)
     update, last = call(combine_kernel, (f32(22, 8, 512),) * 2, bytes_accessed=3 * 10**6)(
-        field, powers, grams.reshape(devices, 128), stiffness
+        own, powers, grams.reshape(devices, 128), stiffness
     )
     return update.reshape(2, 11, 8, 512), last.reshape(2, 11, 8, 512)
 

time: 78.6 us -> 57.2 us (0.73)
  Pallas kernels: 28.2 us -> 9.17 us
  local copies, waits for them, and re-layouts: 2.09 us -> 7.49 us
  starting transfers between devices: 11.3 us -> 6.35 us
  waiting for transfers between devices: 6.75 us -> 2.29 us
  blocking collectives: 29.2 us -> 30.6 us
    pallas_call x1, Pallas kernels: 18.4 us -> 6.08 us  [body(): call(main_kernel, (f32(3, 8, 24, 512), f32(devices, 128)), [pltpu.VMEM((N...]
    unnamed x11 -> x17, local copies, waits for them, and re-layouts: 2.09 us -> 7.49 us
    pallas_call x3, Pallas kernels: 6.88 us -> 1.68 us  [the longest x1 1.35 us: body(): call(own_kernel, (f32(8, 48, 512), f32(2, 48, 128), jax.ShapeDtypeStruct(...]
    ppermute x4, starting transfers between devices: 11.3 us -> 6.35 us  [swapped(): return lax.ppermute(shard, axis, pairs)]
    ppermute x4, waiting for transfers between devices: 6.75 us -> 2.29 us  [swapped(): return lax.ppermute(shard, axis, pairs)]
    pallas_call x1, Pallas kernels: 2.92 us -> 1.41 us  [body(): call(combine_kernel, (f32(22, 8, 512),) * 2, bytes_accessed=3 * 10 ** 6)]
    all_to_all x1, blocking collectives: 29.2 us -> 30.6 us  [body(): grams = lax.all_to_all(gram.reshape(devices, 1, 128), ('rx', 'ry'), 0, 0)]
  transfers between devices with their start and end apart: 4 -> 4, of which waited for: 3 -> 2; matrix products, arithmetic and copies ran while one was open for 1% -> 1% of each run, Pallas kernels for 3% -> 2%
where the time goes in v2:
time: 57.2 us; the launch traced here: 56.6 us
  blocking collectives  30.6 us (53%)
  Pallas kernels  9.17 us (16%)
  local copies, waits for them, and re-layouts  7.49 us (13%)
  starting transfers between devices  6.35 us (11%)
  waiting for transfers between devices  2.29 us (4%)
  between operations  0.7 us (1%)
    all_to_all x1, blocking collectives, body(): grams = lax.all_to_all(gram.reshape(devices, 1, 128), ('rx', 'ry'), 0, 0)  30.6 us
    unnamed x17, local copies, waits for them, and re-layouts  7.49 us
    ppermute x4, starting transfers between devices, swapped(): return lax.ppermute(shard, axis, pairs)  6.35 us
    pallas_call x1, Pallas kernels, body(): call(main_kernel, (f32(3, 8, 24, 512), f32(devices, 128)), [pltpu.VMEM((N...  6.08 us
    ppermute x4, waiting for transfers between devices, swapped(): return lax.ppermute(shard, axis, pairs)  2.29 us
    pallas_call x1, Pallas kernels, body(): call(combine_kernel, (f32(22, 8, 512),) * 2, bytes_accessed=3 * 10 ** 6)  1.41 us
    pallas_call x1, Pallas kernels, body(): call(own_kernel, (f32(8, 48, 512), f32(2, 48, 128), jax.ShapeDtypeStruct(...  1.35 us
  transfers between devices with their start and end apart: 4, of which 2 were waited for; matrix products, arithmetic and copies ran while one was open for 1% of the time, Pallas kernels for 2%

profile of v2, /device:TPU:1, one launch (start us, length us, event | category | flops | bytes accessed | tf_op | source)
XLA Modules:
  0.0 56.6 jit_solution(5671480733679013924)
XLA Ops:
  0.6 0.0 copy-start
  0.6 1.0 %copy-done = f32[2,11,8,512]{3,2,1,0:T(8,128)S(1)} copy-done((f32[2,11,8,512]{3,2,1,0:T(8,128)S(1)}, f32[2,11,8,512]{3,2,1,0:T(8,128)}, u32[]{:S(2)}) %copy-start) | copy-done | bytes 360472
  1.6 1.0 %copy-done.2 = f32[10,2,8,512]{3,2,1,0:T(8,128)S(1)} copy-done((f32[10,2,8,512]{3,2,1,0:T(8,128)S(1)}, f32[10,2,8,512]{3,2,1,0:T(8,128)}, u32[]{:S(2)}) %copy-start.2) | copy-done | bytes 327704
  2.6 0.7 %copy-done.4 = s32[8,512]{1,0:T(8,128)S(1)} copy-done((s32[8,512]{1,0:T(8,128)S(1)}, s32[8,512]{1,0:T(8,128)}, u32[]{:S(2)}) %copy-start.4) | copy-done | bytes 16408
  3.3 0.7 %copy-done.6 = f32[8,512]{1,0:T(8,128)S(1)} copy-done((f32[8,512]{1,0:T(8,128)S(1)}, f32[8,512]{1,0:T(8,128)}, u32[]{:S(2)}) %copy-start.6) | copy-done | bytes 16408
  4.0 0.2 shard_map.69
  4.2 3.3 %collective-permute-start = (f32[3,48,512]{2,1,0:T(8,128)S(1)}, f32[3,48,512]{2,1,0:T(8,128)S(1)}, u32[]{:S(2)}, u32[]{:S(2)}) collective-permute-start(f32[3,48,512]{2,1,0:T(8,128)S(1)} %get-tuple-element.14), channel_id=1, source_target_pairs={{0,32},{32,0},{64,96},{96,64},{128,160},{160,128},{192,224},{224,1... | collective-permute-start | bytes 884744 | tf_op jit(solution)/shard_map/ppermute | solution.py:316
  7.5 1.9 %collective-permute-start.1 = (f32[3,48,512]{2,1,0:T(8,128)S(1)}, f32[3,48,512]{2,1,0:T(8,128)S(1)}, u32[]{:S(2)}, u32[]{:S(2)}) collective-permute-start(f32[3,48,512]{2,1,0:T(8,128)S(1)} %get-tuple-element.15), channel_id=1, source_target_pairs={{32,64},{64,32},{96,128},{128,96},{160,192},{192,160},{33,65},{65,... | collective-permute-start | bytes 884744 | tf_op jit(solution)/shard_map/ppermute | solution.py:316
  9.5 0.7 %copy.10.stiff = f32[2,12,12]{2,1,0:T(8,128)S(1)} copy(f32[2,12,12]{2,0,1:T(2,128)} %param.9) | data formatting | bytes 2304 | tf_op args[4]
  10.2 1.0 %copy-done.1 = f32[2,11,8,512]{3,2,1,0:T(8,128)S(1)} copy-done((f32[2,11,8,512]{3,2,1,0:T(8,128)S(1)}, f32[2,11,8,512]{3,2,1,0:T(8,128)}, u32[]{:S(2)}) %copy-start.1) | copy-done | bytes 360472
  11.2 1.0 %copy-done.3 = f32[10,2,8,512]{3,2,1,0:T(8,128)S(1)} copy-done((f32[10,2,8,512]{3,2,1,0:T(8,128)S(1)}, f32[10,2,8,512]{3,2,1,0:T(8,128)}, u32[]{:S(2)}) %copy-start.3) | copy-done | bytes 327704
  12.1 0.7 %copy-done.5 = s32[8,512]{1,0:T(8,128)S(1)} copy-done((s32[8,512]{1,0:T(8,128)S(1)}, s32[8,512]{1,0:T(8,128)}, u32[]{:S(2)}) %copy-start.5) | copy-done | bytes 16408
  12.8 0.7 %copy-done.7 = f32[8,512]{1,0:T(8,128)S(1)} copy-done((f32[8,512]{1,0:T(8,128)S(1)}, f32[8,512]{1,0:T(8,128)}, u32[]{:S(2)}) %copy-start.7) | copy-done | bytes 16408
  13.6 1.3 %shard_map.68 = (f32[8,48,512]{2,1,0:T(8,128)S(1)}, f32[2,48,128]{2,1,0:T(8,128)S(1)}, bf16[2,144,240]{2,1,0:T(8,128)(2,1)S(1)}) custom-call(f32[22,8,512]{2,1,0:T(8,128)S(1)} %bitcast.8, f32[10,2,8,512]{3,2,1,0:T(8,128)S(1)} %copy-done.3, s32[8,512]{1,0:T(8,128)S(1)} %copy-done.5, f32[8,512]{1,0:T(8,128)S(1)} %copy-done.7, f32[2,12,12]{2,1,0:T(8,128)S(1)} %copy.10.stiff), custom_call_target="tpu_custom_call" | custom-call | flops 10000000 | bytes 1000000 | tf_op jit(solution)/shard_map/pallas_call | solution.py:327
  14.9 0.0 collective-permute-done.first_rows
  14.9 0.6 %collective-permute-done.1.second_rows = f32[3,48,512]{2,1,0:T(8,128)S(1)} collective-permute-done((f32[3,48,512]{2,1,0:T(8,128)S(1)}, f32[3,48,512]{2,1,0:T(8,128)S(1)}, u32[]{:S(2)}, u32[]{:S(2)}) %collective-permute-start.1) | collective-permute-done | bytes 294944 | tf_op jit(solution)/shard_map/ppermute | solution.py:316
  15.6 0.1 shard_map.70
  15.7 0.5 collective-permute-start.2
  16.2 0.7 %collective-permute-start.3 = (f32[48,128]{1,0:T(8,128)S(1)}, f32[48,128]{1,0:T(8,128)S(1)}, u32[]{:S(2)}, u32[]{:S(2)}) collective-permute-start(f32[48,128]{1,0:T(8,128)S(1)} %get-tuple-element.18), channel_id=1, source_target_pairs={{1,2},{2,1},{3,4},{4,3},{5,6},{6,5},{7,8},{8,7},{9,10},{10,9},{11,... | collective-permute-start | bytes 73736 | tf_op jit(solution)/shard_map/ppermute | solution.py:316
  16.9 1.6 %collective-permute-done.2.first_cols = f32[48,128]{1,0:T(8,128)S(1)} collective-permute-done((f32[48,128]{1,0:T(8,128)S(1)}, f32[48,128]{1,0:T(8,128)S(1)}, u32[]{:S(2)}, u32[]{:S(2)}) %collective-permute-start.2) | collective-permute-done | bytes 24608 | tf_op jit(solution)/shard_map/ppermute | solution.py:316
  18.5 0.0 collective-permute-done.3.second_cols
  18.5 6.1 %shard_map.71 = (f32[3,8,24,512]{3,2,1,0:T(8,128)S(1)}, f32[256,128]{1,0:T(8,128)S(1)}) custom-call(f32[8,48,512]{2,1,0:T(8,128)S(1)} %get-tuple-element.13.own, f32[3,48,512]{2,1,0:T(8,128)S(1)} %collective-permute-done.first_rows, f32[3,48,512]{2,1,0:T(8,128)S(1)} %collective-permute-done.1.second_rows, f32[48,128]{1,0:T(8,128)S(1)} %collective-permute-done.2.first_cols, ...), custom_call_target="tpu_custom_call" | custom-call | flops 3000000000 | bytes 3000000 | tf_op jit(solution)/shard_map/pallas_call | solution.py:336
  24.6 30.6 %all_to_all.5 = f32[256,1,128]{2,1,0:T(1,128)S(1)} all-to-all(f32[256,1,128]{2,1,0:T(1,128)S(1)} %bitcast.10), channel_id=1, replica_groups=mesh['rx'=8,'ry'=32] {'rx','ry'}, dimensions={0} | all-to-all | bytes 262144 | tf_op jit(solution)/shard_map/all_to_all | solution.py:351
  55.2 1.4 %shard_map.72 = (f32[22,8,512]{2,1,0:T(8,128)}, f32[22,8,512]{2,1,0:T(8,128)}) custom-call(f32[8,48,512]{2,1,0:T(8,128)S(1)} %get-tuple-element.13.own, f32[3,8,24,512]{3,2,1,0:T(8,128)S(1)} %get-tuple-element.20.powers, f32[256,128]{1,0:T(8,128)S(1)} %bitcast.9, f32[2,12,12]{2,1,0:T(8,128)S(1)} %copy.10.stiff), custom_call_target="tpu_custom_call" | custom-call | bytes 3000000 | tf_op jit(solution)/shard_map/pallas_call | solution.py:352
  (7 shorter events, 0.0 us)
Async XLA Ops:
  0.6 1.0 %copy-start = (f32[2,11,8,512]{3,2,1,0:T(8,128)S(1)}, f32[2,11,8,512]{3,2,1,0:T(8,128)}, u32[]{:S(2)}) copy-start(f32[2,11,8,512]{3,2,1,0:T(8,128)} %param.5) | copy-start | bytes 1081348
  1.6 1.0 %copy-start.2 = (f32[10,2,8,512]{3,2,1,0:T(8,128)S(1)}, f32[10,2,8,512]{3,2,1,0:T(8,128)}, u32[]{:S(2)}) copy-start(f32[10,2,8,512]{3,2,1,0:T(8,128)} %visc.3) | copy-start | bytes 983044
  2.6 0.7 %copy-start.4 = (s32[8,512]{1,0:T(8,128)S(1)}, s32[8,512]{1,0:T(8,128)}, u32[]{:S(2)}) copy-start(s32[8,512]{1,0:T(8,128)} %mask.3) | copy-start | bytes 49156
  3.3 0.7 %copy-start.6 = (f32[8,512]{1,0:T(8,128)S(1)}, f32[8,512]{1,0:T(8,128)}, u32[]{:S(2)}) copy-start(f32[8,512]{1,0:T(8,128)} %fric.3) | copy-start | bytes 49156
  4.2 10.7 %collective-permute-start = (f32[3,48,512]{2,1,0:T(8,128)S(1)}, f32[3,48,512]{2,1,0:T(8,128)S(1)}, u32[]{:S(2)}, u32[]{:S(2)}) collective-permute-start(f32[3,48,512]{2,1,0:T(8,128)S(1)} %get-tuple-element.14), channel_id=1, source_target_pairs={{0,32},{32,0},{64,96},{96,64},{128,160},{160,128},{192,224},{224,1... | collective-permute-start | bytes 884744 | tf_op jit(solution)/shard_map/ppermute | solution.py:316
  7.5 8.0 %collective-permute-start.1 = (f32[3,48,512]{2,1,0:T(8,128)S(1)}, f32[3,48,512]{2,1,0:T(8,128)S(1)}, u32[]{:S(2)}, u32[]{:S(2)}) collective-permute-start(f32[3,48,512]{2,1,0:T(8,128)S(1)} %get-tuple-element.15), channel_id=1, source_target_pairs={{32,64},{64,32},{96,128},{128,96},{160,192},{192,160},{33,65},{65,... | collective-permute-start | bytes 884744 | tf_op jit(solution)/shard_map/ppermute | solution.py:316
  10.2 1.0 %copy-start.1 = (f32[2,11,8,512]{3,2,1,0:T(8,128)S(1)}, f32[2,11,8,512]{3,2,1,0:T(8,128)}, u32[]{:S(2)}) copy-start(f32[2,11,8,512]{3,2,1,0:T(8,128)} %param.5) | copy-start | bytes 1081348
  11.2 1.0 %copy-start.3 = (f32[10,2,8,512]{3,2,1,0:T(8,128)S(1)}, f32[10,2,8,512]{3,2,1,0:T(8,128)}, u32[]{:S(2)}) copy-start(f32[10,2,8,512]{3,2,1,0:T(8,128)} %visc.3) | copy-start | bytes 983044
  12.1 0.7 %copy-start.5 = (s32[8,512]{1,0:T(8,128)S(1)}, s32[8,512]{1,0:T(8,128)}, u32[]{:S(2)}) copy-start(s32[8,512]{1,0:T(8,128)} %mask.3) | copy-start | bytes 49156
  12.8 0.7 %copy-start.7 = (f32[8,512]{1,0:T(8,128)S(1)}, f32[8,512]{1,0:T(8,128)}, u32[]{:S(2)}) copy-start(f32[8,512]{1,0:T(8,128)} %fric.3) | copy-start | bytes 49156
  15.7 2.8 %collective-permute-start.2 = (f32[48,128]{1,0:T(8,128)S(1)}, f32[48,128]{1,0:T(8,128)S(1)}, u32[]{:S(2)}, u32[]{:S(2)}) collective-permute-start(f32[48,128]{1,0:T(8,128)S(1)} %get-tuple-element.17), channel_id=1, source_target_pairs={{0,1},{1,0},{2,3},{3,2},{4,5},{5,4},{6,7},{7,6},{8,9},{9,8},{10,11... | collective-permute-start | bytes 73736 | tf_op jit(solution)/shard_map/ppermute | solution.py:316
  16.2 2.3 %collective-permute-start.3 = (f32[48,128]{1,0:T(8,128)S(1)}, f32[48,128]{1,0:T(8,128)S(1)}, u32[]{:S(2)}, u32[]{:S(2)}) collective-permute-start(f32[48,128]{1,0:T(8,128)S(1)} %get-tuple-element.18), channel_id=1, source_target_pairs={{1,2},{2,1},{3,4},{4,3},{5,6},{6,5},{7,8},{8,7},{9,10},{10,9},{11,... | collective-permute-start | bytes 73736 | tf_op jit(solution)/shard_map/ppermute | solution.py:316

commit v3 on v2

v3 whole, which is shorter than its diff:
```python
import jax
import jax.numpy as jnp
from jax import lax
from jax.experimental import pallas as pl
from jax.experimental.pallas import tpu as pltpu
from jax.sharding import PartitionSpec as P


DEPTH = 3
NROW = 8 + 2 * DEPTH
LANES = 512
PITCH = 18
EDGE = 256
PAIRS = [(a, b) for a in range(4) for b in range(a, 4)]
HALF = 80
BLOCK = 2 * HALF
GROUPS = 144


def shift_of(stiff):
    rows = lax.broadcasted_iota(jnp.int32, (12, 12), 0)
    cols = lax.broadcasted_iota(jnp.int32, (12, 12), 1)
    trace = jnp.sum(jnp.where(rows == cols, stiff[0] + stiff[1], 0.0))
    return 1.0 + trace * (1.2 * 10.0 / 22.0)


def own_row(out, rhs, visc, mask, fric, row):
    ice = mask[row : row + 1, :].astype(jnp.float32)
    out[0:22, 0:512] = rhs[:, row, :]
    out[22:23, 0:512] = jnp.ones_like(ice)
    out[23:24, 0:512] = fric[row : row + 1, :]
    out[24:34, 0:512] = visc[:, 0, row, :] * ice
    out[34:44, 0:512] = visc[:, 1, row, :] * ice
    out[44:48, 0:512] = jnp.zeros((4, 512), jnp.float32)


def odd_along(axis):
    return lax.rem(lax.axis_index(axis), 2) == 1


def rows_kernel(rhs, visc, mask, fric, first, second, rhs_out, visc_out, mask_out, fric_out, work, sems):
    copies = [
        pltpu.make_async_copy(src, dst, sems.at[n])
        for n, (src, dst) in enumerate(
            ((rhs, rhs_out), (visc, visc_out), (mask, mask_out), (fric, fric_out))
        )
    ]
    for copy in copies:
        copy.start()
    for copy in copies:
        copy.wait()
    odd = odd_along("rx")
    for j in range(DEPTH):
        own_row(work.at[0], rhs_out, visc_out, mask_out, fric_out, 8 - DEPTH + j)
        own_row(work.at[1], rhs_out, visc_out, mask_out, fric_out, j)
        up, down = (work[0], work[1])
        first[j] = jnp.where(odd, down, up)
        second[j] = jnp.where(odd, up, down)


def pack_row(row, i, lane, packed):
    ends = jnp.concatenate([row[:, 0:128], row[:, 384:512]], axis=1)
    at = lane - PITCH * i
    packed = jnp.where((at >= 0) & (at < 9), pltpu.roll(ends, (PITCH * i + 3) % EDGE, 1), packed)
    return jnp.where((at >= 9) & (at < 18), pltpu.roll(ends, (PITCH * i + 15) % EDGE, 1), packed)


def own_kernel(rhs, visc, mask, fric, stiff, own, packs, weights):
    weights_kernel(stiff, weights)
    lane = lax.broadcasted_iota(jnp.int32, (48, EDGE), 1)
    packed = jnp.zeros((48, EDGE), jnp.float32)
    for r in range(8):
        own_row(own.at[r], rhs, visc, mask, fric, r)
        packed = pack_row(own.at[r], r + DEPTH, lane, packed)
    packs[...] = packed


def cols_kernel(packs, first_rows, second_rows, out):
    odd_row = odd_along("rx")
    lane = lax.broadcasted_iota(jnp.int32, (48, EDGE), 1)
    packed = packs[...]
    for j in range(DEPTH):
        one, two = (first_rows[j], second_rows[j])
        packed = pack_row(jnp.where(odd_row, one, two), j, lane, packed)
        packed = pack_row(jnp.where(odd_row, two, one), j + 8 + DEPTH, lane, packed)
    out[...] = packed


def weights_kernel(stiff, weights):
    row = lax.broadcasted_iota(jnp.int32, (GROUPS, 12), 0)
    col = lax.broadcasted_iota(jnp.int32, (GROUPS, 12), 1)

    def of_row(r):
        group, plane = (r // 24, r % 24)
        slot, lev = (group // 2, group % 2)
        comp, level = (plane // 11, plane % 11)
        layer = level - lev
        good = (plane < 22) & (layer >= 0) & (layer < 10)
        return comp * 6 + lev * 3 + slot, layer, good

    pick = jnp.where(of_row(row)[0] == col, 1.0, 0.0)
    r = lax.broadcasted_iota(jnp.int32, (GROUPS, 3 * HALF), 0)
    k = lax.broadcasted_iota(jnp.int32, (GROUPS, 3 * HALF), 1)
    _, layer, good = of_row(r)
    part = (k % HALF) // 24
    plane = (k % HALF) % 24
    lev_in = plane % 11 - layer
    good = good & (part < 3) & (plane < 22)
    q = lax.broadcasted_iota(jnp.int32, (12, 3 * HALF), 0)
    kq = lax.broadcasted_iota(jnp.int32, (12, 3 * HALF), 1)
    comp_in = ((kq % HALF) % 24) // 11
    block = kq // HALF
    for tri in range(2):
        first, second, third = ((0, 2, 1), (2, 0, 1))[tri]
        place = jnp.where(block == 0, first, jnp.where(block == 1, second, third))
        rows = jnp.dot(
            pick, stiff[tri], precision=lax.Precision.HIGHEST, preferred_element_type=jnp.float32
        )
        total = jnp.zeros((GROUPS, 3 * HALF), jnp.float32)
        for lev in range(2):
            sel = jnp.where(comp_in * 6 + lev * 3 + place == q, 1.0, 0.0)
            spread = jnp.dot(
                rows, sel, precision=lax.Precision.HIGHEST, preferred_element_type=jnp.float32
            )
            total = jnp.where(good & (lev_in == lev), spread, total)
        high = total.astype(jnp.bfloat16).astype(jnp.float32)
        weights[tri] = jnp.where(part == 2, total - high, high).astype(jnp.bfloat16)


def split_rows(x):
    high = x.astype(jnp.bfloat16).astype(jnp.float32)
    pad = jnp.zeros((HALF - 72, x.shape[1]), jnp.float32)
    return jnp.concatenate([high, x - high, high, pad], axis=0).astype(jnp.bfloat16)


def put_operand(operand, i, x):
    operand[i * BLOCK : i * BLOCK + HALF, :] = split_rows(x)
    operand[i * BLOCK + HALF : (i + 1) * BLOCK, :] = split_rows(pltpu.roll(x, LANES - 1, 1))


def put_scale(out, coefs):
    zeros = jnp.zeros((24, out.shape[1]), jnp.float32)
    for tri in range(2):
        for lev in range(2):
            base = 48 * tri + 24 * lev
            out[base : base + 24, :] = zeros
            out[base + lev : base + lev + 10, :] = coefs[tri]
            out[base + 11 + lev : base + 21 + lev, :] = coefs[tri]


def grown_of(scale, mixed):
    parts = []
    for tri in range(2):
        upper = scale[48 * tri : 48 * tri + 24, :]
        lower = scale[48 * tri + 24 : 48 * tri + 48, :]
        for slot in range(3):
            at = 48 * slot
            parts.append(upper * mixed[tri][at : at + 24] + lower * mixed[tri][at + 24 : at + 48])
    return parts[0], parts[1] + parts[3], parts[2] + parts[5], parts[4]


def inner_products(vectors, sums, lanes):
    result = []
    for total, (a, b) in zip(sums, PAIRS):
        product = vectors[a] * vectors[b]
        for s in range(0, 24, 8):
            for l in range(0, lanes, 128):
                total = total + product[s : s + 8, l : l + 128]
        result.append(total)
    return tuple(result)


def line_of(sums):
    place = lax.broadcasted_iota(jnp.int32, (8, 128), 1)
    line = jnp.zeros((8, 128), jnp.float32)
    for n, total in enumerate(sums):
        line = jnp.where(place == n, jnp.sum(total), line)
    return line


def no_sums():
    return tuple(jnp.zeros((8, 128), jnp.float32) for _ in PAIRS)


def main_kernel(
    own, first_rows, second_rows, stiff, weights, powers, line, scale, diag, field, operand, carry
):
    odd_row = odd_along("rx")
    theta = shift_of(stiff)
    plane = lax.broadcasted_iota(jnp.int32, (24, LANES), 0)
    bottom = (plane == 0) | (plane == 11)
    real = {}
    for i in range(NROW):
        if i < DEPTH:
            row = jnp.where(odd_row, first_rows[i], second_rows[i])
        elif i >= 8 + DEPTH:
            j = i - 8 - DEPTH
            row = jnp.where(odd_row, second_rows[j], first_rows[j])
            real[i] = row[22:23, :]
        else:
            row = own[i - DEPTH]
        x = jnp.where(plane < 22, row[0:24, :], 0.0)
        field[0, i] = x
        put_operand(operand.at[0], i, x)
        diag[i] = row[22:23, :] * (1.0 - theta) + jnp.where(bottom, row[23:24, :], 0.0)
        if i < NROW - 1:
            put_scale(scale.at[i], (row[24:34, :], row[34:44, :]))

    for step in range(1, DEPTH + 1):
        source = operand.at[(step - 1) % 2]
        target = operand.at[step % 2]
        carry[...] = jnp.zeros_like(carry)
        for i in range(step - 1, NROW - step):
            start = i * BLOCK
            mixed = [
                jnp.dot(
                    weights[tri],
                    source[start + HALF * tri : start + HALF * tri + 3 * HALF, :],
                    preferred_element_type=jnp.float32,
                )
                for tri in range(2)
            ]
            a, b, c, d = grown_of(scale[i], mixed)
            total = a + carry[0] + pltpu.roll(c + carry[1], 1, 1)
            carry[0] = b
            carry[1] = d
            if i in real:
                total = total * real[i]
            x = total + diag[i] * field[step - 1, i]
            field[step, i] = x
            if DEPTH <= i < DEPTH + 8:
                powers[step - 1, i - DEPTH] = x
            if step < DEPTH:
                put_operand(target, i, x)

    lane = lax.broadcasted_iota(jnp.int32, (24, LANES), 1)
    inside = (lane >= DEPTH) & (lane < LANES - DEPTH)
    sums = no_sums()
    for r in range(8):
        vectors = [jnp.where(inside, field[a, r + DEPTH], 0.0) for a in range(4)]
        sums = inner_products(vectors, sums, LANES)
    line[...] = line_of(sums)


def edge_kernel(packs, first_cols, second_cols, stiff, weights, line, edges, gram, scale):
    odd_col = odd_along("ry")
    theta = shift_of(stiff)
    at = lax.rem(lax.broadcasted_iota(jnp.int32, (48, EDGE), 1), PITCH)
    from_left = jnp.where(odd_col, first_cols[...], second_cols[...])
    from_right = jnp.where(odd_col, second_cols[...], first_cols[...])
    full = jnp.where(at < 3, from_left, jnp.where(at >= 15, from_right, packs[...]))
    plane = lax.broadcasted_iota(jnp.int32, (24, EDGE), 0)
    bottom = (plane == 0) | (plane == 11)
    put_scale(scale, (full[24:34], full[34:44]))
    real = full[22:23]
    diag = real * (1.0 - theta) + jnp.where(bottom, full[23:24], 0.0)
    x = jnp.where(plane < 22, full[0:24], 0.0)
    vectors = [x]
    for _ in range(DEPTH):
        corners = [
            split_rows(pltpu.roll(x, (EDGE - by) % EDGE, 1) if by else x)
            for by in (0, 1, PITCH, PITCH + 1)
        ]
        mixed = [
            jnp.dot(
                weights[tri],
                jnp.concatenate(corners[tri : tri + 3], axis=0),
                preferred_element_type=jnp.float32,
            )
            for tri in range(2)
        ]
        a, b, c, d = grown_of(scale[...], mixed)
        total = a + pltpu.roll(b, PITCH, 1) + pltpu.roll(c + pltpu.roll(d, PITCH, 1), 1, 1)
        x = real * total + diag * x
        vectors.append(x)
    for a in range(4):
        edges[a] = vectors[a]
    lane = lax.broadcasted_iota(jnp.int32, (24, EDGE), 1)
    at = lax.rem(lane, PITCH)
    mine = (lane >= PITCH * DEPTH) & (lane < PITCH * (DEPTH + 8))
    mine = mine & (((at >= 3) & (at < 6)) | ((at >= 12) & (at < 15)))
    sums = inner_products([jnp.where(mine, v, 0.0) for v in vectors], no_sums(), EDGE)
    total = line[...] + line_of(sums)
    gram[...] = jnp.broadcast_to(total[0:1], gram.shape)


def combine_kernel(own, powers, edges, grams, stiff, update, last):
    theta = shift_of(stiff)
    entry = jnp.sum(grams[...], axis=0, keepdims=True)
    place = lax.broadcasted_iota(jnp.int32, (1, 128), 1)
    g = {}
    for n, pair in enumerate(PAIRS):
        g[pair] = jnp.sum(jnp.where(place == n, entry, 0.0), axis=1, keepdims=True)
    upper = [[None] * 4 for _ in range(4)]
    for a in range(4):
        for b in range(a, 4):
            value = g[a, b]
            for c in range(a):
                value = value - upper[c][a] * upper[c][b]
            if a == b:
                upper[a][a] = jnp.sqrt(value)
            else:
                upper[a][b] = value / upper[a][a]
    zero = jnp.zeros((1, 1), jnp.float32)
    table = [
        [
            (upper[a][b + 1] if a <= b + 1 else zero) + (theta * upper[a][b] if a <= b else zero)
            for b in range(3)
        ]
        for a in range(4)
    ]
    target = [upper[0][0], zero, zero, zero]
    for col in range(3):
        first, second = (table[col][col], table[col + 1][col])
        radius = jnp.sqrt(first * first + second * second)
        cosine, sine = (first / radius, second / radius)
        for c in range(col, 3):
            one, two = (table[col][c], table[col + 1][c])
            table[col][c] = cosine * one + sine * two
            table[col + 1][c] = cosine * two - sine * one
        one, two = (target[col], target[col + 1])
        target[col] = cosine * one + sine * two
        target[col + 1] = cosine * two - sine * one
    z = [None] * 3
    for col in (2, 1, 0):
        value = target[col]
        for c in range(col + 1, 3):
            value = value - table[col][c] * z[c]
        z[col] = value / table[col][col]
    w = [None] * 4
    w[3] = 1.0 / upper[3][3]
    for a in (2, 1, 0):
        value = zero
        for c in range(a + 1, 4):
            value = value - upper[a][c] * w[c]
        w[a] = value / upper[a][a]
    lane = lax.broadcasted_iota(jnp.int32, (22, 128), 1)
    for out, factors in ((update, z), (last, w)):
        ends = factors[0] * edges[0]
        for a in range(1, len(factors)):
            ends = ends + factors[a] * edges[a]
        for r in range(8):
            row = factors[0] * own[r, 0:22, :]
            for a in range(1, len(factors)):
                row = row + factors[a] * powers[a - 1, r, 0:22, :]
            at = PITCH * (r + DEPTH)
            left = pltpu.roll(ends, (EDGE - at - 3) % EDGE, 1)[0:22, 0:128]
            right = pltpu.roll(ends, (253 - at - 12) % EDGE, 1)[0:22, 128:256]
            out[:, r, 0:128] = jnp.where(lane < DEPTH, left, row[:, 0:128])
            out[:, r, 128:384] = row[:, 128:384]
            out[:, r, 384:512] = jnp.where(lane >= 128 - DEPTH, right, row[:, 384:512])


def call(kernel, outs, scratch=(), flops=0, bytes_accessed=0, limit=8, in_hbm=0):
    single = not isinstance(outs, (list, tuple))
    extra = {"in_specs": [pl.BlockSpec(memory_space=pltpu.HBM)] * in_hbm} if in_hbm else {}
    return pl.pallas_call(
        kernel,
        out_shape=outs if single else tuple(outs),
        scratch_shapes=list(scratch),
        **extra,
        compiler_params=pltpu.CompilerParams(vmem_limit_bytes=limit * 1024 * 1024),
        cost_estimate=pl.CostEstimate(
            flops=flops, bytes_accessed=bytes_accessed, transcendentals=0
        ),
    )


def f32(*shape):
    return jax.ShapeDtypeStruct(shape, jnp.float32)


def swapped(shard, axis, start):
    pairs = []
    for i in range(start, lax.axis_size(axis) - 1, 2):
        pairs += [(i, i + 1), (i + 1, i)]
    return lax.ppermute(shard, axis, pairs)


def body(rhs, viscosity, cell_mask, friction, stiffness):
    devices = lax.axis_size("rx") * lax.axis_size("ry")
    natural = [
        pltpu.with_memory_space_constraint(x, pltpu.HBM)
        for x in (rhs.reshape(22, 8, 512), viscosity, cell_mask, friction)
    ]
    first, second, *local = call(
        rows_kernel,
        (f32(DEPTH, 48, 512), f32(DEPTH, 48, 512), f32(22, 8, 512), f32(10, 2, 8, 512),
         jax.ShapeDtypeStruct((8, 512), jnp.int32), f32(8, 512)),
        [pltpu.VMEM((2, 48, 512), jnp.float32), pltpu.SemaphoreType.DMA((4,))],
        bytes_accessed=10**6,
        in_hbm=4,
    )(*natural)
    first_rows = swapped(first, "rx", 0)
    second_rows = swapped(second, "rx", 1)
    own, packs, weights = call(
        own_kernel,
        (f32(8, 48, 512), f32(48, EDGE), jax.ShapeDtypeStruct((2, GROUPS, 3 * HALF), jnp.bfloat16)),
        flops=10**7,
        bytes_accessed=10**6,
    )(*local, stiffness)
    packs = call(cols_kernel, f32(48, EDGE), bytes_accessed=10**6)(packs, first_rows, second_rows)
    first_cols = swapped(packs, "ry", 0)
    second_cols = swapped(packs, "ry", 1)
    powers, line = call(
        main_kernel,
        (f32(3, 8, 24, LANES), f32(8, 128)),
        [
            pltpu.VMEM((NROW - 1, 96, LANES), jnp.float32),
            pltpu.VMEM((NROW, 24, LANES), jnp.float32),
            pltpu.VMEM((4, NROW, 24, LANES), jnp.float32),
            pltpu.VMEM((2, NROW * BLOCK, LANES), jnp.bfloat16),
            pltpu.VMEM((2, 24, LANES), jnp.float32),
        ],
        flops=3 * 10**9,
        bytes_accessed=3 * 10**6,
        limit=28,
    )(own, first_rows, second_rows, stiffness, weights)
    edges, gram = call(
        edge_kernel,
        (f32(4, 24, EDGE), f32(devices, 128)),
        [pltpu.VMEM((96, EDGE), jnp.float32)],
        flops=10**8,
        bytes_accessed=10**6,
    )(packs, first_cols, second_cols, stiffness, weights, line)
    grams = lax.all_to_all(gram.reshape(devices, 1, 128), ("rx", "ry"), 0, 0)
    update, last = call(combine_kernel, (f32(22, 8, 512),) * 2, bytes_accessed=3 * 10**6)(
        own, powers, edges, grams.reshape(devices, 128), stiffness
    )
    return update.reshape(2, 11, 8, 512), last.reshape(2, 11, 8, 512)


def solution(mesh):
    in_specs = (
        P(None, None, "rx", "ry"),
        P(None, None, "rx", "ry"),
        P("rx", "ry"),
        P("rx", "ry"),
        P(),
    )
    out_specs = (P(None, None, "rx", "ry"), P(None, None, "rx", "ry"))
    return jax.shard_map(body, mesh=mesh, in_specs=in_specs, out_specs=out_specs, check_vma=False)
```

time: 57.2 us -> 50.1 us (0.88)
  local copies, waits for them, and re-layouts: 7.49 us -> 0.71 us
  blocking collectives: 30.6 us -> 25.5 us
  starting transfers between devices: 6.35 us -> 8.77 us
  waiting for transfers between devices: 2.29 us -> 4.36 us
    unnamed x17 -> x1, local copies, waits for them, and re-layouts: 7.49 us -> 0.71 us
    all_to_all x1, blocking collectives: 30.6 us -> 25.5 us  [body(): grams = lax.all_to_all(gram.reshape(devices, 1, 128), ('rx', 'ry'), 0, 0)]
    ppermute x4, starting transfers between devices: 6.35 us -> 8.77 us  [swapped(): return lax.ppermute(shard, axis, pairs)]
    ppermute x4, waiting for transfers between devices: 2.29 us -> 4.36 us  [swapped(): return lax.ppermute(shard, axis, pairs)]
    pallas_call x4 -> x5, Pallas kernels: 7.76 us -> 8.14 us  [the longest x1 3.95 us: body(): call(main_kernel, (f32(3, 8, 24, LANES), f32(8, 128)), [pltpu.VMEM((NROW...]
  transfers between devices with their start and end apart: 4 -> 4, of which waited for: 2 -> 1; matrix products, arithmetic and copies ran while one was open for 1% -> 1% of each run, Pallas kernels for 2% -> 11%
where the time goes in v3:
time: 50.1 us; the launch traced here: 49.8 us
  blocking collectives  25.5 us (51%)
  Pallas kernels  9.72 us (19%)
  starting transfers between devices  8.77 us (18%)
  waiting for transfers between devices  4.36 us (9%)
  local copies, waits for them, and re-layouts  0.71 us (1%)
  between operations  0.71 us (1%)
    all_to_all x1, blocking collectives, body(): grams = lax.all_to_all(gram.reshape(devices, 1, 128), ('rx', 'ry'), 0, 0)  25.5 us
    ppermute x4, starting transfers between devices, swapped(): return lax.ppermute(shard, axis, pairs)  8.77 us
    ppermute x4, waiting for transfers between devices, swapped(): return lax.ppermute(shard, axis, pairs)  4.36 us
    pallas_call x1, Pallas kernels, body(): call(main_kernel, (f32(3, 8, 24, LANES), f32(8, 128)), [pltpu.VMEM((NROW...  3.95 us
    pallas_call x1, Pallas kernels, body(): call(combine_kernel, (f32(22, 8, 512),) * 2, bytes_accessed=3 * 10 ** 6)  1.58 us
    pallas_call x1, Pallas kernels, body(): call(edge_kernel, (f32(4, 24, EDGE), f32(devices, 128)), [pltpu.VMEM((96,...  1.33 us
    pallas_call x1, Pallas kernels, body(): call(own_kernel, (f32(8, 48, 512), f32(48, EDGE), jax.ShapeDtypeStruct((2...  1.32 us
    pallas_call x1, Pallas kernels, body(): call(rows_kernel, (f32(DEPTH, 48, 512), f32(DEPTH, 48, 512), f32(22, 8, 5...  1.31 us
  transfers between devices with their start and end apart: 4, of which 1 were waited for; matrix products, arithmetic and copies ran while one was open for 1% of the time, Pallas kernels for 11%

profile of v3, /device:TPU:1, one launch (start us, length us, event | category | flops | bytes accessed | tf_op | source)
XLA Modules:
  0.0 49.8 jit_solution(8494869246301248264)
XLA Ops:
  0.6 1.3 %shard_map.68 = (f32[3,48,512]{2,1,0:T(8,128)S(1)}, f32[3,48,512]{2,1,0:T(8,128)S(1)}, f32[22,8,512]{2,1,0:T(8,128)S(1)}, f32[10,2,8,512]{3,2,1,0:T(8,128)S(1)},...) custom-call(f32[22,8,512]{2,1,0:T(8,128)} %bitcast.9, f32[10,2,8,512]{3,2,1,0:T(8,128)} %visc.1, s32[8,512]{1,0:T(8,128)} %mask.1, ...), custom_call_target="tpu_custom_call" | custom-call | bytes 1000000 | tf_op jit(solution)/shard_map/pallas_call | solution.py:386
  1.9 3.3 %collective-permute-start = (f32[3,48,512]{2,1,0:T(8,128)S(1)}, f32[3,48,512]{2,1,0:T(8,128)S(1)}, u32[]{:S(2)}, u32[]{:S(2)}) collective-permute-start(f32[3,48,512]{2,1,0:T(8,128)S(1)} %get-tuple-element.22), channel_id=1, source_target_pairs={{0,32},{32,0},{64,96},{96,64},{128,160},{160,128},{192,224},{224,1... | collective-permute-start | bytes 884744 | tf_op jit(solution)/shard_map/ppermute | solution.py:377
  5.3 1.9 %collective-permute-start.1 = (f32[3,48,512]{2,1,0:T(8,128)S(1)}, f32[3,48,512]{2,1,0:T(8,128)S(1)}, u32[]{:S(2)}, u32[]{:S(2)}) collective-permute-start(f32[3,48,512]{2,1,0:T(8,128)S(1)} %get-tuple-element.23), channel_id=1, source_target_pairs={{32,64},{64,32},{96,128},{128,96},{160,192},{192,160},{33,65},{65,... | collective-permute-start | bytes 884744 | tf_op jit(solution)/shard_map/ppermute | solution.py:377
  7.2 0.7 %copy.11.stiff = f32[2,12,12]{2,1,0:T(8,128)S(1)} copy(f32[2,12,12]{2,0,1:T(2,128)} %param.9) | data formatting | bytes 2304 | tf_op args[4]
  7.9 1.3 %shard_map.69 = (f32[8,48,512]{2,1,0:T(8,128)S(1)}, f32[48,256]{1,0:T(8,128)S(1)}, bf16[2,144,240]{2,1,0:T(8,128)(2,1)S(1)}) custom-call(f32[22,8,512]{2,1,0:T(8,128)S(1)} %get-tuple-element.17.rhs, f32[10,2,8,512]{3,2,1,0:T(8,128)S(1)} %get-tuple-element.18.visc, s32[8,512]{1,0:T(8,128)S(1)} %get-tuple-element.19.mask, ...), custom_call_target="tpu_custom_call" | custom-call | flops 10000000 | bytes 1000000 | tf_op jit(solution)/shard_map/pallas_call | solution.py:396
  9.2 0.0 collective-permute-done.first_rows
  9.2 4.4 %collective-permute-done.1.second_rows = f32[3,48,512]{2,1,0:T(8,128)S(1)} collective-permute-done((f32[3,48,512]{2,1,0:T(8,128)S(1)}, f32[3,48,512]{2,1,0:T(8,128)S(1)}, u32[]{:S(2)}, u32[]{:S(2)}) %collective-permute-start.1) | collective-permute-done | bytes 294944 | tf_op jit(solution)/shard_map/ppermute | solution.py:377
  13.6 0.2 shard_map.71.packs
  13.8 0.7 %collective-permute-start.3 = (f32[48,256]{1,0:T(8,128)S(1)}, f32[48,256]{1,0:T(8,128)S(1)}, u32[]{:S(2)}, u32[]{:S(2)}) collective-permute-start(f32[48,256]{1,0:T(8,128)S(1)} %shard_map.71.packs), channel_id=1, source_target_pairs={{1,2},{2,1},{3,4},{4,3},{5,6},{6,5},{7,8},{8,7},{9,10},{10,9},{11,... | collective-permute-start | bytes 147464 | tf_op jit(solution)/shard_map/ppermute | solution.py:377
  14.5 2.9 %collective-permute-start.2 = (f32[48,256]{1,0:T(8,128)S(1)}, f32[48,256]{1,0:T(8,128)S(1)}, u32[]{:S(2)}, u32[]{:S(2)}) collective-permute-start(f32[48,256]{1,0:T(8,128)S(1)} %shard_map.71.packs), channel_id=1, source_target_pairs={{0,1},{1,0},{2,3},{3,2},{4,5},{5,4},{6,7},{7,6},{8,9},{9,8},{10,11... | collective-permute-start | bytes 147464 | tf_op jit(solution)/shard_map/ppermute | solution.py:377
  17.4 3.9 %shard_map.70 = (f32[3,8,24,512]{3,2,1,0:T(8,128)S(1)}, f32[8,128]{1,0:T(8,128)S(1)}) custom-call(f32[8,48,512]{2,1,0:T(8,128)S(1)} %get-tuple-element.21.own, f32[3,48,512]{2,1,0:T(8,128)S(1)} %collective-permute-done.first_rows, f32[3,48,512]{2,1,0:T(8,128)S(1)} %collective-permute-done.1.second_rows, f32[2,12,12]{2,1,0:T(8,128)S(1)} %copy.11.stiff, ...), custom_call_target="tpu_custom_call" | custom-call | flops 3000000000 | bytes 3000000 | tf_op jit(solution)/shard_map/pallas_call | solution.py:405
  21.3 0.0 collective-permute-done.3.second_cols
  21.3 0.0 collective-permute-done.2.first_cols
  21.4 1.3 %shard_map.72 = (f32[4,24,256]{2,1,0:T(8,128)S(1)}, f32[256,128]{1,0:T(8,128)S(1)}) custom-call(f32[48,256]{1,0:T(8,128)S(1)} %shard_map.71.packs, f32[48,256]{1,0:T(8,128)S(1)} %collective-permute-done.2.first_cols, f32[48,256]{1,0:T(8,128)S(1)} %collective-permute-done.3.second_cols, f32[2,12,12]{2,1,0:T(8,128)S(1)} %copy.11.stiff, ...), custom_call_target="tpu_custom_call" | custom-call | flops 100000000 | bytes 1000000 | tf_op jit(solution)/shard_map/pallas_call | solution.py:419
  22.7 25.5 %all_to_all.5 = f32[256,1,128]{2,1,0:T(1,128)S(1)} all-to-all(f32[256,1,128]{2,1,0:T(1,128)S(1)} %bitcast.8), channel_id=1, replica_groups=mesh['rx'=8,'ry'=32] {'rx','ry'}, dimensions={0} | all-to-all | bytes 262144 | tf_op jit(solution)/shard_map/all_to_all | solution.py:426
  48.2 1.6 %shard_map.73 = (f32[22,8,512]{2,1,0:T(8,128)}, f32[22,8,512]{2,1,0:T(8,128)}) custom-call(f32[8,48,512]{2,1,0:T(8,128)S(1)} %get-tuple-element.21.own, f32[3,8,24,512]{3,2,1,0:T(8,128)S(1)} %get-tuple-element.25.powers, f32[4,24,256]{2,1,0:T(8,128)S(1)} %get-tuple-element.28.edges, f32[256,128]{1,0:T(8,128)S(1)} %bitcast.7, f32[2,12,12]{2,1,0:T(8,128)S(1)} %copy.11.stiff), custom_call_target="tpu_custom_call" | custom-call | bytes 3000000 | tf_op jit(solution)/shard_map/pallas_call | solution.py:427
Async XLA Ops:
  1.9 7.3 %collective-permute-start = (f32[3,48,512]{2,1,0:T(8,128)S(1)}, f32[3,48,512]{2,1,0:T(8,128)S(1)}, u32[]{:S(2)}, u32[]{:S(2)}) collective-permute-start(f32[3,48,512]{2,1,0:T(8,128)S(1)} %get-tuple-element.22), channel_id=1, source_target_pairs={{0,32},{32,0},{64,96},{96,64},{128,160},{160,128},{192,224},{224,1... | collective-permute-start | bytes 884744 | tf_op jit(solution)/shard_map/ppermute | solution.py:377
  5.3 8.3 %collective-permute-start.1 = (f32[3,48,512]{2,1,0:T(8,128)S(1)}, f32[3,48,512]{2,1,0:T(8,128)S(1)}, u32[]{:S(2)}, u32[]{:S(2)}) collective-permute-start(f32[3,48,512]{2,1,0:T(8,128)S(1)} %get-tuple-element.23), channel_id=1, source_target_pairs={{32,64},{64,32},{96,128},{128,96},{160,192},{192,160},{33,65},{65,... | collective-permute-start | bytes 884744 | tf_op jit(solution)/shard_map/ppermute | solution.py:377
  13.8 7.5 %collective-permute-start.3 = (f32[48,256]{1,0:T(8,128)S(1)}, f32[48,256]{1,0:T(8,128)S(1)}, u32[]{:S(2)}, u32[]{:S(2)}) collective-permute-start(f32[48,256]{1,0:T(8,128)S(1)} %shard_map.71.packs), channel_id=1, source_target_pairs={{1,2},{2,1},{3,4},{4,3},{5,6},{6,5},{7,8},{8,7},{9,10},{10,9},{11,... | collective-permute-start | bytes 147464 | tf_op jit(solution)/shard_map/ppermute | solution.py:377
  14.5 6.8 %collective-permute-start.2 = (f32[48,256]{1,0:T(8,128)S(1)}, f32[48,256]{1,0:T(8,128)S(1)}, u32[]{:S(2)}, u32[]{:S(2)}) collective-permute-start(f32[48,256]{1,0:T(8,128)S(1)} %shard_map.71.packs), channel_id=1, source_target_pairs={{0,1},{1,0},{2,3},{3,2},{4,5},{5,4},{6,7},{7,6},{8,9},{9,8},{10,11... | collective-permute-start | bytes 147464 | tf_op jit(solution)/shard_map/ppermute | solution.py:377

commit v4 on v3

--- a/solution.py
+++ b/solution.py
@@ -63,16 +63,6 @@
     at = lane - PITCH * i
     packed = jnp.where((at >= 0) & (at < 9), pltpu.roll(ends, (PITCH * i + 3) % EDGE, 1), packed)
     return jnp.where((at >= 9) & (at < 18), pltpu.roll(ends, (PITCH * i + 15) % EDGE, 1), packed)
-
-
-def own_kernel(rhs, visc, mask, fric, stiff, own, packs, weights):
-    weights_kernel(stiff, weights)
-    lane = lax.broadcasted_iota(jnp.int32, (48, EDGE), 1)
-    packed = jnp.zeros((48, EDGE), jnp.float32)
-    for r in range(8):
-        own_row(own.at[r], rhs, visc, mask, fric, r)
-        packed = pack_row(own.at[r], r + DEPTH, lane, packed)
-    packs[...] = packed
 
 
 def cols_kernel(packs, first_rows, second_rows, out):
@@ -182,62 +172,141 @@
     return tuple(jnp.zeros((8, 128), jnp.float32) for _ in PAIRS)
 
 
+def products(weights, source, i):
+    start = i * BLOCK
+    return [
+        jnp.dot(
+            weights[tri],
+            source[start + HALF * tri : start + HALF * (tri + 3), :],
+            preferred_element_type=jnp.float32,
+        )
+        for tri in range(2)
+    ]
+
+
+def bottom_planes(lanes):
+    plane = lax.broadcasted_iota(jnp.int32, (24, lanes), 0)
+    return (plane == 0) | (plane == 11)
+
+
+def field_planes(row):
+    plane = lax.broadcasted_iota(jnp.int32, (24, row.shape[1]), 0)
+    return jnp.where(plane < 22, row[0:24, :], 0.0)
+
+
+def diag_planes(row, theta):
+    on_bottom = jnp.where(bottom_planes(row.shape[1]), row[23:24, :], 0.0)
+    return row[22:23, :] * (1.0 - theta) + on_bottom
+
+
+def is_inner(k, i):
+    return DEPTH + k <= i <= DEPTH + 7 - k
+
+
+def own_kernel(
+    rhs, visc, mask, fric, stiff,
+    own, packs, weights, scale, diag, powers, bounds, low_parts, high_parts,
+    operand,
+):
+    weights_kernel(stiff, weights)
+    theta = shift_of(stiff)
+    lane = lax.broadcasted_iota(jnp.int32, (48, EDGE), 1)
+    packed = jnp.zeros((48, EDGE), jnp.float32)
+    for r in range(8):
+        own_row(own.at[r], rhs, visc, mask, fric, r)
+        row = own[r]
+        packed = pack_row(row, r + DEPTH, lane, packed)
+        put_operand(operand.at[0], r, field_planes(row))
+        diag[r] = diag_planes(row, theta)
+        put_scale(scale.at[r], (row[24:34, :], row[34:44, :]))
+    packs[...] = packed
+    for step in range(1, DEPTH + 1):
+        source = operand.at[(step - 1) % 2]
+        target = operand.at[step % 2]
+        first, last = (step - 1, 8 - step)
+        bounds[step - 1, 0] = source[first * BLOCK : (first + 1) * BLOCK, :]
+        bounds[step - 1, 1] = source[last * BLOCK : (last + 1) * BLOCK, :]
+        for r in range(first, last):
+            a, b, c, d = grown_of(scale[r], products(weights, source, r))
+            if r == first:
+                low_parts[step - 1] = a + pltpu.roll(c, 1, 1)
+            else:
+                total = a + upper + pltpu.roll(c + across, 1, 1)
+                before = powers[step - 2, r] if step > 1 else field_planes(own[r])
+                x = total + diag[r] * before
+                powers[step - 1, r] = x
+                if step < DEPTH:
+                    put_operand(target, r, x)
+            upper, across = (b, d)
+        high_parts[step - 1, 0] = upper
+        high_parts[step - 1, 1] = across
+
+
 def main_kernel(
-    own, first_rows, second_rows, stiff, weights, powers, line, scale, diag, field, operand, carry
+    own, weights, own_scale, own_diag, inner, bounds, low_parts, high_parts, first_rows, second_rows, stiff,
+    outer, line,
+    scale, diag, field, operand,
 ):
     odd_row = odd_along("rx")
     theta = shift_of(stiff)
-    plane = lax.broadcasted_iota(jnp.int32, (24, LANES), 0)
-    bottom = (plane == 0) | (plane == 11)
     real = {}
-    for i in range(NROW):
+    for i in (0, 1, 2, 11, 12, 13):
         if i < DEPTH:
             row = jnp.where(odd_row, first_rows[i], second_rows[i])
-        elif i >= 8 + DEPTH:
+        else:
             j = i - 8 - DEPTH
             row = jnp.where(odd_row, second_rows[j], first_rows[j])
             real[i] = row[22:23, :]
-        else:
-            row = own[i - DEPTH]
-        x = jnp.where(plane < 22, row[0:24, :], 0.0)
+        x = field_planes(row)
         field[0, i] = x
         put_operand(operand.at[0], i, x)
-        diag[i] = row[22:23, :] * (1.0 - theta) + jnp.where(bottom, row[23:24, :], 0.0)
+        diag[i] = diag_planes(row, theta)
         if i < NROW - 1:
             put_scale(scale.at[i], (row[24:34, :], row[34:44, :]))
+
+    def power(k, i):
+        if k == 0 and is_inner(0, i):
+            return field_planes(own[i - DEPTH])
+        return inner[k - 1, i - DEPTH] if is_inner(k, i) else field[k, i]
 
     for step in range(1, DEPTH + 1):
         source = operand.at[(step - 1) % 2]
         target = operand.at[step % 2]
-        carry[...] = jnp.zeros_like(carry)
-        for i in range(step - 1, NROW - step):
-            start = i * BLOCK
-            mixed = [
-                jnp.dot(
-                    weights[tri],
-                    source[start + HALF * tri : start + HALF * tri + 3 * HALF, :],
-                    preferred_element_type=jnp.float32,
-                )
-                for tri in range(2)
-            ]
-            a, b, c, d = grown_of(scale[i], mixed)
-            total = a + carry[0] + pltpu.roll(c + carry[1], 1, 1)
-            carry[0] = b
-            carry[1] = d
+        for side, i in ((0, DEPTH + step - 1), (1, DEPTH + 8 - step)):
+            source[i * BLOCK : (i + 1) * BLOCK, :] = bounds[step - 1, side]
+
+        def grown(i, source=source):
+            is_own = is_inner(0, i)
+            return grown_of(own_scale[i - DEPTH] if is_own else scale[i], products(weights, source, i))
+
+        def put(i, total, step=step, target=target):
             if i in real:
                 total = total * real[i]
-            x = total + diag[i] * field[step - 1, i]
+            x = total + (own_diag[i - DEPTH] if is_inner(0, i) else diag[i]) * power(step - 1, i)
             field[step, i] = x
-            if DEPTH <= i < DEPTH + 8:
-                powers[step - 1, i - DEPTH] = x
+            if is_inner(0, i):
+                outer[step - 1, i - DEPTH] = x
             if step < DEPTH:
                 put_operand(target, i, x)
+
+        first = step - 1
+        _, upper, _, across = grown(first)
+        for i in range(first + 1, first + 3):
+            a, b, c, d = grown(i)
+            put(i, a + upper + pltpu.roll(c + across, 1, 1))
+            upper, across = (b, d)
+        put(first + 3, low_parts[step - 1] + upper + pltpu.roll(across, 1, 1))
+        upper, across = (high_parts[step - 1, 0], high_parts[step - 1, 1])
+        for i in range(11 - step, 14 - step):
+            a, b, c, d = grown(i)
+            put(i, a + upper + pltpu.roll(c + across, 1, 1))
+            upper, across = (b, d)
 
     lane = lax.broadcasted_iota(jnp.int32, (24, LANES), 1)
     inside = (lane >= DEPTH) & (lane < LANES - DEPTH)
     sums = no_sums()
     for r in range(8):
-        vectors = [jnp.where(inside, field[a, r + DEPTH], 0.0) for a in range(4)]
+        vectors = [jnp.where(inside, power(a, r + DEPTH), 0.0) for a in range(4)]
         sums = inner_products(vectors, sums, LANES)
     line[...] = line_of(sums)
 
@@ -249,12 +318,10 @@
     from_left = jnp.where(odd_col, first_cols[...], second_cols[...])
     from_right = jnp.where(odd_col, second_cols[...], first_cols[...])
     full = jnp.where(at < 3, from_left, jnp.where(at >= 15, from_right, packs[...]))
-    plane = lax.broadcasted_iota(jnp.int32, (24, EDGE), 0)
-    bottom = (plane == 0) | (plane == 11)
     put_scale(scale, (full[24:34], full[34:44]))
     real = full[22:23]
-    diag = real * (1.0 - theta) + jnp.where(bottom, full[23:24], 0.0)
-    x = jnp.where(plane < 22, full[0:24], 0.0)
+    diag = diag_planes(full, theta)
+    x = field_planes(full)
     vectors = [x]
     for _ in range(DEPTH):
         corners = [
@@ -284,7 +351,7 @@
     gram[...] = jnp.broadcast_to(total[0:1], gram.shape)
 
 
-def combine_kernel(own, powers, edges, grams, stiff, update, last):
+def combine_kernel(own, inner, outer, edges, grams, stiff, update, last):
     theta = shift_of(stiff)
     entry = jnp.sum(grams[...], axis=0, keepdims=True)
     place = lax.broadcasted_iota(jnp.int32, (1, 128), 1)
@@ -342,7 +409,8 @@
         for r in range(8):
             row = factors[0] * own[r, 0:22, :]
             for a in range(1, len(factors)):
-                row = row + factors[a] * powers[a - 1, r, 0:22, :]
+                part = inner if is_inner(a, r + DEPTH) else outer
+                row = row + factors[a] * part[a - 1, r, 0:22, :]
             at = PITCH * (r + DEPTH)
             left = pltpu.roll(ends, (EDGE - at - 3) % EDGE, 1)[0:22, 0:128]
             right = pltpu.roll(ends, (253 - at - 12) % EDGE, 1)[0:22, 128:256]
@@ -393,16 +461,29 @@
     )(*natural)
     first_rows = swapped(first, "rx", 0)
     second_rows = swapped(second, "rx", 1)
-    own, packs, weights = call(
+    own, packs, weights, *prepared = call(
         own_kernel,
-        (f32(8, 48, 512), f32(48, EDGE), jax.ShapeDtypeStruct((2, GROUPS, 3 * HALF), jnp.bfloat16)),
-        flops=10**7,
+        (
+            f32(8, 48, LANES),
+            f32(48, EDGE),
+            jax.ShapeDtypeStruct((2, GROUPS, 3 * HALF), jnp.bfloat16),
+            f32(8, 96, LANES),
+            f32(8, 24, LANES),
+            f32(3, 8, 24, LANES),
+            jax.ShapeDtypeStruct((3, 2, BLOCK, LANES), jnp.bfloat16),
+            f32(3, 24, LANES),
+            f32(3, 2, 24, LANES),
+        ),
+        [pltpu.VMEM((2, 8 * BLOCK, LANES), jnp.bfloat16)],
+        flops=10**9,
         bytes_accessed=10**6,
+        limit=16,
     )(*local, stiffness)
+    inner = prepared[2]
     packs = call(cols_kernel, f32(48, EDGE), bytes_accessed=10**6)(packs, first_rows, second_rows)
     first_cols = swapped(packs, "ry", 0)
     second_cols = swapped(packs, "ry", 1)
-    powers, line = call(
+    outer, line = call(
         main_kernel,
         (f32(3, 8, 24, LANES), f32(8, 128)),
         [
@@ -410,12 +491,11 @@
             pltpu.VMEM((NROW, 24, LANES), jnp.float32),
             pltpu.VMEM((4, NROW, 24, LANES), jnp.float32),
             pltpu.VMEM((2, NROW * BLOCK, LANES), jnp.bfloat16),
-            pltpu.VMEM((2, 24, LANES), jnp.float32),
         ],
-        flops=3 * 10**9,
+        flops=2 * 10**9,
         bytes_accessed=3 * 10**6,
-        limit=28,
-    )(own, first_rows, second_rows, stiffness, weights)
+        limit=24,
+    )(own, weights, *prepared, first_rows, second_rows, stiffness)
     edges, gram = call(
         edge_kernel,
         (f32(4, 24, EDGE), f32(devices, 128)),
@@ -425,7 +505,7 @@
     )(packs, first_cols, second_cols, stiffness, weights, line)
     grams = lax.all_to_all(gram.reshape(devices, 1, 128), ("rx", "ry"), 0, 0)
     update, last = call(combine_kernel, (f32(22, 8, 512),) * 2, bytes_accessed=3 * 10**6)(
-        own, powers, edges, grams.reshape(devices, 128), stiffness
+        own, inner, outer, edges, grams.reshape(devices, 128), stiffness
     )
     return update.reshape(2, 11, 8, 512), last.reshape(2, 11, 8, 512)
 

time: 50.1 us -> 49.3 us (0.984)
  waiting for transfers between devices: 4.36 us -> 2.15 us
  blocking collectives: 25.5 us -> 26.7 us
    ppermute x4, waiting for transfers between devices: 4.36 us -> 2.15 us  [swapped(): return lax.ppermute(shard, axis, pairs)]
    pallas_call x1, Pallas kernels: 1.32 us -> 3.24 us  [body(): call(own_kernel, (f32(8, 48, LANES), f32(48, EDGE), jax.ShapeDtypeStruct(...]
    pallas_call x1, Pallas kernels: 3.95 us -> 2.3 us  [body(): call(main_kernel, (f32(3, 8, 24, LANES), f32(8, 128)), [pltpu.VMEM((NROW...]
    all_to_all x1, blocking collectives: 25.5 us -> 26.7 us  [body(): grams = lax.all_to_all(gram.reshape(devices, 1, 128), ('rx', 'ry'), 0, 0)]
where the time goes in v4:
time: 49.3 us; the launch traced here: 49 us
  blocking collectives  26.7 us (54%)
  Pallas kernels  9.98 us (20%)
  starting transfers between devices  8.77 us (18%)
  waiting for transfers between devices  2.15 us (4%)
  local copies, waits for them, and re-layouts  0.71 us (1%)
  between operations  0.71 us (1%)
    all_to_all x1, blocking collectives, body(): grams = lax.all_to_all(gram.reshape(devices, 1, 128), ('rx', 'ry'), 0, 0)  26.7 us
    ppermute x4, starting transfers between devices, swapped(): return lax.ppermute(shard, axis, pairs)  8.77 us
    pallas_call x1, Pallas kernels, body(): call(own_kernel, (f32(8, 48, LANES), f32(48, EDGE), jax.ShapeDtypeStruct(...  3.24 us
    pallas_call x1, Pallas kernels, body(): call(main_kernel, (f32(3, 8, 24, LANES), f32(8, 128)), [pltpu.VMEM((NROW...  2.3 us
    ppermute x4, waiting for transfers between devices, swapped(): return lax.ppermute(shard, axis, pairs)  2.15 us
    pallas_call x1, Pallas kernels, body(): call(combine_kernel, (f32(22, 8, 512),) * 2, bytes_accessed=3 * 10 ** 6)  1.57 us
    pallas_call x1, Pallas kernels, body(): call(edge_kernel, (f32(4, 24, EDGE), f32(devices, 128)), [pltpu.VMEM((96,...  1.33 us
    pallas_call x1, Pallas kernels, body(): call(rows_kernel, (f32(DEPTH, 48, 512), f32(DEPTH, 48, 512), f32(22, 8, 5...  1.31 us
  transfers between devices with their start and end apart: 4, of which 1 were waited for; matrix products, arithmetic and copies ran while one was open for 1% of the time, Pallas kernels for 11%

profile of v4, /device:TPU:1, one launch (start us, length us, event | category | flops | bytes accessed | tf_op | source)
XLA Modules:
  0.0 49.0 jit_solution(7685996463576675279)
XLA Ops:
  0.6 1.3 %shard_map.68 = (f32[3,48,512]{2,1,0:T(8,128)S(1)}, f32[3,48,512]{2,1,0:T(8,128)S(1)}, f32[22,8,512]{2,1,0:T(8,128)S(1)}, f32[10,2,8,512]{3,2,1,0:T(8,128)S(1)},...) custom-call(f32[22,8,512]{2,1,0:T(8,128)} %bitcast.9, f32[10,2,8,512]{3,2,1,0:T(8,128)} %visc.1, s32[8,512]{1,0:T(8,128)} %mask.1, ...), custom_call_target="tpu_custom_call" | custom-call | bytes 1000000 | tf_op jit(solution)/shard_map/pallas_call | solution.py:454
  1.9 3.3 %collective-permute-start = (f32[3,48,512]{2,1,0:T(8,128)S(1)}, f32[3,48,512]{2,1,0:T(8,128)S(1)}, u32[]{:S(2)}, u32[]{:S(2)}) collective-permute-start(f32[3,48,512]{2,1,0:T(8,128)S(1)} %get-tuple-element.35), channel_id=1, source_target_pairs={{0,32},{32,0},{64,96},{96,64},{128,160},{160,128},{192,224},{224,1... | collective-permute-start | bytes 884744 | tf_op jit(solution)/shard_map/ppermute | solution.py:445
  5.3 1.9 %collective-permute-start.1 = (f32[3,48,512]{2,1,0:T(8,128)S(1)}, f32[3,48,512]{2,1,0:T(8,128)S(1)}, u32[]{:S(2)}, u32[]{:S(2)}) collective-permute-start(f32[3,48,512]{2,1,0:T(8,128)S(1)} %get-tuple-element.36), channel_id=1, source_target_pairs={{32,64},{64,32},{96,128},{128,96},{160,192},{192,160},{33,65},{65,... | collective-permute-start | bytes 884744 | tf_op jit(solution)/shard_map/ppermute | solution.py:445
  7.2 0.7 %copy.11.stiff = f32[2,12,12]{2,1,0:T(8,128)S(1)} copy(f32[2,12,12]{2,0,1:T(2,128)} %param.9) | data formatting | bytes 2304 | tf_op args[4]
  7.9 3.2 %shard_map.69 = (f32[8,48,512]{2,1,0:T(8,128)S(1)}, f32[48,256]{1,0:T(8,128)S(1)}, bf16[2,144,240]{2,1,0:T(8,128)(2,1)S(1)}, f32[8,96,512]{2,1,0:T(8,128)S(1)}, ...) custom-call(f32[22,8,512]{2,1,0:T(8,128)S(1)} %get-tuple-element.23., ...), custom_call_target="tpu_custom_call" | custom-call | flops 1000000000 | bytes 1000000 | tf_op jit(solution)/shard_map/pallas_call | solution.py:464
  11.1 0.0 collective-permute-done.first_rows
  11.2 2.1 %collective-permute-done.1.second_rows = f32[3,48,512]{2,1,0:T(8,128)S(1)} collective-permute-done((f32[3,48,512]{2,1,0:T(8,128)S(1)}, f32[3,48,512]{2,1,0:T(8,128)S(1)}, u32[]{:S(2)}, u32[]{:S(2)}) %collective-permute-start.1) | collective-permute-done | bytes 294944 | tf_op jit(solution)/shard_map/ppermute | solution.py:445
  13.3 0.2 shard_map.71.packs
  13.5 0.7 %collective-permute-start.3 = (f32[48,256]{1,0:T(8,128)S(1)}, f32[48,256]{1,0:T(8,128)S(1)}, u32[]{:S(2)}, u32[]{:S(2)}) collective-permute-start(f32[48,256]{1,0:T(8,128)S(1)} %shard_map.71.packs), channel_id=1, source_target_pairs={{1,2},{2,1},{3,4},{4,3},{5,6},{6,5},{7,8},{8,7},{9,10},{10,9},{11,... | collective-permute-start | bytes 147464 | tf_op jit(solution)/shard_map/ppermute | solution.py:445
  14.2 2.9 %collective-permute-start.2 = (f32[48,256]{1,0:T(8,128)S(1)}, f32[48,256]{1,0:T(8,128)S(1)}, u32[]{:S(2)}, u32[]{:S(2)}) collective-permute-start(f32[48,256]{1,0:T(8,128)S(1)} %shard_map.71.packs), channel_id=1, source_target_pairs={{0,1},{1,0},{2,3},{3,2},{4,5},{5,4},{6,7},{7,6},{8,9},{9,8},{10,11... | collective-permute-start | bytes 147464 | tf_op jit(solution)/shard_map/ppermute | solution.py:445
  17.1 2.3 %shard_map.70 = (f32[3,8,24,512]{3,2,1,0:T(8,128)S(1)}, f32[8,128]{1,0:T(8,128)S(1)}) custom-call(f32[8,48,512]{2,1,0:T(8,128)S(1)} %get-tuple-element.27.own, bf16[2,144,240]{2,1,0:T(8,128)(2,1)S(1)} %get-tuple-element.29.weights, f32[8,96,512]{2,1,0:T(8,128)S(1)} %get-tuple-element.30.own_scale, f32[8,24,512]{2,1,0:T(8,128)S(1)} %get-tuple-element.31.own_diag, ...), custom_call_target="tpu_custom_call" | custom-call | flops 2000000000 | bytes 3000000 | tf_op jit(solution)/shard_map/pallas_call | solution.py:486
  19.4 0.0 collective-permute-done.3.second_cols
  19.4 0.0 collective-permute-done.2.first_cols
  19.4 1.3 %shard_map.72 = (f32[4,24,256]{2,1,0:T(8,128)S(1)}, f32[256,128]{1,0:T(8,128)S(1)}) custom-call(f32[48,256]{1,0:T(8,128)S(1)} %shard_map.71.packs, f32[48,256]{1,0:T(8,128)S(1)} %collective-permute-done.2.first_cols, f32[48,256]{1,0:T(8,128)S(1)} %collective-permute-done.3.second_cols, f32[2,12,12]{2,1,0:T(8,128)S(1)} %copy.11.stiff, ...), custom_call_target="tpu_custom_call" | custom-call | flops 100000000 | bytes 1000000 | tf_op jit(solution)/shard_map/pallas_call | solution.py:499
  20.7 26.7 %all_to_all.5 = f32[256,1,128]{2,1,0:T(1,128)S(1)} all-to-all(f32[256,1,128]{2,1,0:T(1,128)S(1)} %bitcast.8), channel_id=1, replica_groups=mesh['rx'=8,'ry'=32] {'rx','ry'}, dimensions={0} | all-to-all | bytes 262144 | tf_op jit(solution)/shard_map/all_to_all | solution.py:506
  47.4 1.6 %shard_map.73 = (f32[22,8,512]{2,1,0:T(8,128)}, f32[22,8,512]{2,1,0:T(8,128)}) custom-call(f32[8,48,512]{2,1,0:T(8,128)S(1)} %get-tuple-element.27.own, f32[3,8,24,512]{3,2,1,0:T(8,128)S(1)} %get-tuple-element.28.inner, f32[3,8,24,512]{3,2,1,0:T(8,128)S(1)} %get-tuple-element.37.outer, f32[4,24,256]{2,1,0:T(8,128)S(1)} %get-tuple-element.40.edges, ...), custom_call_target="tpu_custom_call" | custom-call | bytes 3000000 | tf_op jit(solution)/shard_map/pallas_call | solution.py:507
Async XLA Ops:
  1.9 9.2 %collective-permute-start = (f32[3,48,512]{2,1,0:T(8,128)S(1)}, f32[3,48,512]{2,1,0:T(8,128)S(1)}, u32[]{:S(2)}, u32[]{:S(2)}) collective-permute-start(f32[3,48,512]{2,1,0:T(8,128)S(1)} %get-tuple-element.35), channel_id=1, source_target_pairs={{0,32},{32,0},{64,96},{96,64},{128,160},{160,128},{192,224},{224,1... | collective-permute-start | bytes 884744 | tf_op jit(solution)/shard_map/ppermute | solution.py:445
  5.3 8.0 %collective-permute-start.1 = (f32[3,48,512]{2,1,0:T(8,128)S(1)}, f32[3,48,512]{2,1,0:T(8,128)S(1)}, u32[]{:S(2)}, u32[]{:S(2)}) collective-permute-start(f32[3,48,512]{2,1,0:T(8,128)S(1)} %get-tuple-element.36), channel_id=1, source_target_pairs={{32,64},{64,32},{96,128},{128,96},{160,192},{192,160},{33,65},{65,... | collective-permute-start | bytes 884744 | tf_op jit(solution)/shard_map/ppermute | solution.py:445
  13.5 5.9 %collective-permute-start.3 = (f32[48,256]{1,0:T(8,128)S(1)}, f32[48,256]{1,0:T(8,128)S(1)}, u32[]{:S(2)}, u32[]{:S(2)}) collective-permute-start(f32[48,256]{1,0:T(8,128)S(1)} %shard_map.71.packs), channel_id=1, source_target_pairs={{1,2},{2,1},{3,4},{4,3},{5,6},{6,5},{7,8},{8,7},{9,10},{10,9},{11,... | collective-permute-start | bytes 147464 | tf_op jit(solution)/shard_map/ppermute | solution.py:445
  14.2 5.2 %collective-permute-start.2 = (f32[48,256]{1,0:T(8,128)S(1)}, f32[48,256]{1,0:T(8,128)S(1)}, u32[]{:S(2)}, u32[]{:S(2)}) collective-permute-start(f32[48,256]{1,0:T(8,128)S(1)} %shard_map.71.packs), channel_id=1, source_target_pairs={{0,1},{1,0},{2,3},{3,2},{4,5},{5,4},{6,7},{7,6},{8,9},{9,8},{10,11... | collective-permute-start | bytes 147464 | tf_op jit(solution)/shard_map/ppermute | solution.py:445

commit v5 on v4

--- a/solution.py
+++ b/solution.py
@@ -20,7 +20,7 @@
 def shift_of(stiff):
     rows = lax.broadcasted_iota(jnp.int32, (12, 12), 0)
     cols = lax.broadcasted_iota(jnp.int32, (12, 12), 1)
-    trace = jnp.sum(jnp.where(rows == cols, stiff[0] + stiff[1], 0.0))
+    trace = jnp.sum(jnp.where(rows == cols, stiff[:, 0, :] + stiff[:, 1, :], 0.0))
     return 1.0 + trace * (1.2 * 10.0 / 22.0)
 
 
@@ -38,12 +38,16 @@
     return lax.rem(lax.axis_index(axis), 2) == 1
 
 
-def rows_kernel(rhs, visc, mask, fric, first, second, rhs_out, visc_out, mask_out, fric_out, work, sems):
+def rows_kernel(
+    rhs, visc, mask, fric, stiff,
+    first, second, rhs_out, visc_out, mask_out, fric_out, stiff_out,
+    work, sems,
+):
+    sources = (rhs, visc, mask, fric, stiff)
+    targets = (rhs_out, visc_out, mask_out, fric_out, stiff_out)
     copies = [
         pltpu.make_async_copy(src, dst, sems.at[n])
-        for n, (src, dst) in enumerate(
-            ((rhs, rhs_out), (visc, visc_out), (mask, mask_out), (fric, fric_out))
-        )
+        for n, (src, dst) in enumerate(zip(sources, targets))
     ]
     for copy in copies:
         copy.start()
@@ -58,22 +62,39 @@
         second[j] = jnp.where(odd, up, down)
 
 
-def pack_row(row, i, lane, packed):
-    ends = jnp.concatenate([row[:, 0:128], row[:, 384:512]], axis=1)
-    at = lane - PITCH * i
-    packed = jnp.where((at >= 0) & (at < 9), pltpu.roll(ends, (PITCH * i + 3) % EDGE, 1), packed)
-    return jnp.where((at >= 9) & (at < 18), pltpu.roll(ends, (PITCH * i + 15) % EDGE, 1), packed)
-
-
-def cols_kernel(packs, first_rows, second_rows, out):
-    odd_row = odd_along("rx")
+def pack_kernel(rhs, visc, mask, fric, packs):
     lane = lax.broadcasted_iota(jnp.int32, (48, EDGE), 1)
-    packed = packs[...]
-    for j in range(DEPTH):
-        one, two = (first_rows[j], second_rows[j])
-        packed = pack_row(jnp.where(odd_row, one, two), j, lane, packed)
-        packed = pack_row(jnp.where(odd_row, two, one), j + 8 + DEPTH, lane, packed)
-    out[...] = packed
+    packed = jnp.zeros((48, EDGE), jnp.float32)
+
+    def ends(rows):
+        return jnp.concatenate([rows[..., 0:128], rows[..., 384:512]], axis=-1)
+
+    for r in range(8):
+        ice = ends(mask[r : r + 1, :]).astype(jnp.float32)
+        row = jnp.concatenate(
+            [
+                ends(rhs[:, r, :]),
+                jnp.ones_like(ice),
+                ends(fric[r : r + 1, :]),
+                ends(visc[:, 0, r, :]) * ice,
+                ends(visc[:, 1, r, :]) * ice,
+                jnp.zeros((4, EDGE), jnp.float32),
+            ],
+            axis=0,
+        )
+        start = PITCH * (r + DEPTH)
+        at = lane - start
+        packed = jnp.where((at >= 0) & (at < 9), pltpu.roll(row, (start + 3) % EDGE, 1), packed)
+        packed = jnp.where((at >= 9) & (at < 18), pltpu.roll(row, (start + 15) % EDGE, 1), packed)
+    packs[...] = packed
+
+
+def corners_kernel(packs, first_cols, second_cols, out):
+    odd_col = odd_along("ry")
+    at = lax.rem(lax.broadcasted_iota(jnp.int32, (48, EDGE), 1), PITCH)
+    from_left = jnp.where(odd_col, first_cols[...], second_cols[...])
+    from_right = jnp.where(odd_col, second_cols[...], first_cols[...])
+    out[...] = jnp.where(at < 3, from_left, jnp.where(at >= 15, from_right, packs[...]))
 
 
 def weights_kernel(stiff, weights):
@@ -104,7 +125,7 @@
         first, second, third = ((0, 2, 1), (2, 0, 1))[tri]
         place = jnp.where(block == 0, first, jnp.where(block == 1, second, third))
         rows = jnp.dot(
-            pick, stiff[tri], precision=lax.Precision.HIGHEST, preferred_element_type=jnp.float32
+            pick, stiff[:, tri, :], precision=lax.Precision.HIGHEST, preferred_element_type=jnp.float32
         )
         total = jnp.zeros((GROUPS, 3 * HALF), jnp.float32)
         for lev in range(2):
@@ -205,21 +226,17 @@
 
 def own_kernel(
     rhs, visc, mask, fric, stiff,
-    own, packs, weights, scale, diag, powers, bounds, low_parts, high_parts,
+    own, weights, scale, diag, powers, bounds, low_parts, high_parts,
     operand,
 ):
     weights_kernel(stiff, weights)
     theta = shift_of(stiff)
-    lane = lax.broadcasted_iota(jnp.int32, (48, EDGE), 1)
-    packed = jnp.zeros((48, EDGE), jnp.float32)
     for r in range(8):
         own_row(own.at[r], rhs, visc, mask, fric, r)
         row = own[r]
-        packed = pack_row(row, r + DEPTH, lane, packed)
         put_operand(operand.at[0], r, field_planes(row))
         diag[r] = diag_planes(row, theta)
         put_scale(scale.at[r], (row[24:34, :], row[34:44, :]))
-    packs[...] = packed
     for step in range(1, DEPTH + 1):
         source = operand.at[(step - 1) % 2]
         target = operand.at[step % 2]
@@ -311,13 +328,14 @@
     line[...] = line_of(sums)
 
 
-def edge_kernel(packs, first_cols, second_cols, stiff, weights, line, edges, gram, scale):
-    odd_col = odd_along("ry")
+def edge_kernel(cols, first_rows, second_rows, stiff, weights, line, edges, gram, scale):
+    odd_row = odd_along("rx")
     theta = shift_of(stiff)
-    at = lax.rem(lax.broadcasted_iota(jnp.int32, (48, EDGE), 1), PITCH)
-    from_left = jnp.where(odd_col, first_cols[...], second_cols[...])
-    from_right = jnp.where(odd_col, second_cols[...], first_cols[...])
-    full = jnp.where(at < 3, from_left, jnp.where(at >= 15, from_right, packs[...]))
+    lane = lax.broadcasted_iota(jnp.int32, (48, EDGE), 1)
+    low = jnp.where(odd_row, first_rows[...], second_rows[...])
+    high = jnp.where(odd_row, second_rows[...], first_rows[...])
+    full = jnp.where(lane < PITCH * DEPTH, pltpu.roll(low, EDGE - 8 * PITCH, 1), cols[...])
+    full = jnp.where(lane >= PITCH * (8 + DEPTH), pltpu.roll(high, 8 * PITCH, 1), full)
     put_scale(scale, (full[24:34], full[34:44]))
     real = full[22:23]
     diag = diag_planes(full, theta)
@@ -449,23 +467,25 @@
     devices = lax.axis_size("rx") * lax.axis_size("ry")
     natural = [
         pltpu.with_memory_space_constraint(x, pltpu.HBM)
-        for x in (rhs.reshape(22, 8, 512), viscosity, cell_mask, friction)
+        for x in (rhs.reshape(22, 8, 512), viscosity, cell_mask, friction, stiffness.transpose(1, 0, 2))
     ]
-    first, second, *local = call(
+    first, second, *local, stiff = call(
         rows_kernel,
         (f32(DEPTH, 48, 512), f32(DEPTH, 48, 512), f32(22, 8, 512), f32(10, 2, 8, 512),
-         jax.ShapeDtypeStruct((8, 512), jnp.int32), f32(8, 512)),
-        [pltpu.VMEM((2, 48, 512), jnp.float32), pltpu.SemaphoreType.DMA((4,))],
+         jax.ShapeDtypeStruct((8, 512), jnp.int32), f32(8, 512), f32(12, 2, 12)),
+        [pltpu.VMEM((2, 48, 512), jnp.float32), pltpu.SemaphoreType.DMA((5,))],
         bytes_accessed=10**6,
-        in_hbm=4,
+        in_hbm=5,
     )(*natural)
     first_rows = swapped(first, "rx", 0)
     second_rows = swapped(second, "rx", 1)
-    own, packs, weights, *prepared = call(
+    packs = call(pack_kernel, f32(48, EDGE), bytes_accessed=10**5)(*local)
+    first_cols = swapped(packs, "ry", 0)
+    second_cols = swapped(packs, "ry", 1)
+    own, weights, *prepared = call(
         own_kernel,
         (
             f32(8, 48, LANES),
-            f32(48, EDGE),
             jax.ShapeDtypeStruct((2, GROUPS, 3 * HALF), jnp.bfloat16),
             f32(8, 96, LANES),
             f32(8, 24, LANES),
@@ -478,11 +498,11 @@
         flops=10**9,
         bytes_accessed=10**6,
         limit=16,
-    )(*local, stiffness)
+    )(*local, stiff)
     inner = prepared[2]
-    packs = call(cols_kernel, f32(48, EDGE), bytes_accessed=10**6)(packs, first_rows, second_rows)
-    first_cols = swapped(packs, "ry", 0)
-    second_cols = swapped(packs, "ry", 1)
+    cols = call(corners_kernel, f32(48, EDGE), bytes_accessed=10**5)(packs, first_cols, second_cols)
+    first_corners = swapped(cols, "rx", 0)
+    second_corners = swapped(cols, "rx", 1)
     outer, line = call(
         main_kernel,
         (f32(3, 8, 24, LANES), f32(8, 128)),
@@ -495,17 +515,17 @@
         flops=2 * 10**9,
         bytes_accessed=3 * 10**6,
         limit=24,
-    )(own, weights, *prepared, first_rows, second_rows, stiffness)
+    )(own, weights, *prepared, first_rows, second_rows, stiff)
     edges, gram = call(
         edge_kernel,
         (f32(4, 24, EDGE), f32(devices, 128)),
         [pltpu.VMEM((96, EDGE), jnp.float32)],
         flops=10**8,
         bytes_accessed=10**6,
-    )(packs, first_cols, second_cols, stiffness, weights, line)
+    )(cols, first_corners, second_corners, stiff, weights, line)
     grams = lax.all_to_all(gram.reshape(devices, 1, 128), ("rx", "ry"), 0, 0)
     update, last = call(combine_kernel, (f32(22, 8, 512),) * 2, bytes_accessed=3 * 10**6)(
-        own, inner, outer, edges, grams.reshape(devices, 128), stiffness
+        own, inner, outer, edges, grams.reshape(devices, 128), stiff
     )
     return update.reshape(2, 11, 8, 512), last.reshape(2, 11, 8, 512)
 

time: 49.3 us -> 50.3 us (1.020)
  starting transfers between devices: 8.77 us -> 13.1 us
  waiting for transfers between devices: 2.15 us -> 0.02 us
  blocking collectives: 26.7 us -> 25.7 us
  local copies, waits for them, and re-layouts: 0.71 us -> 0 us
  Pallas kernels: 9.98 us -> 10.6 us
    ppermute x4 -> x6, starting transfers between devices: 8.77 us -> 13.1 us  [swapped(): return lax.ppermute(shard, axis, pairs)]
    ppermute x4 -> x6, waiting for transfers between devices: 2.15 us -> 0.02 us  [swapped(): return lax.ppermute(shard, axis, pairs)]
    all_to_all x1, blocking collectives: 26.7 us -> 25.7 us  [body(): grams = lax.all_to_all(gram.reshape(devices, 1, 128), ('rx', 'ry'), 0, 0)]
    unnamed x1 -> x0, local copies, waits for them, and re-layouts: 0.71 us -> none
    pallas_call x2 -> x3, Pallas kernels: 3.46 us -> 3.67 us  [the longest x1 3.34 us: body(): call(own_kernel, (f32(8, 48, LANES), jax.ShapeDtypeStruct((2, GROUPS, 3 *...]
  transfers between devices with their start and end apart: 4 -> 6, of which waited for: 1 -> 0; matrix products, arithmetic and copies ran while one was open for 1% -> 0% of each run, Pallas kernels for 11% -> 12%
where the time goes in v5:
time: 50.3 us; the launch traced here: 50.1 us
  blocking collectives  25.7 us (51%)
  starting transfers between devices  13.1 us (26%)
  Pallas kernels  10.6 us (21%)
  between operations  0.76 us (2%)
    all_to_all x1, blocking collectives, body(): grams = lax.all_to_all(gram.reshape(devices, 1, 128), ('rx', 'ry'), 0, 0)  25.7 us
    ppermute x6, starting transfers between devices, swapped(): return lax.ppermute(shard, axis, pairs)  13.1 us
    pallas_call x1, Pallas kernels, body(): call(own_kernel, (f32(8, 48, LANES), jax.ShapeDtypeStruct((2, GROUPS, 3 *...  3.34 us
    pallas_call x1, Pallas kernels, body(): call(main_kernel, (f32(3, 8, 24, LANES), f32(8, 128)), [pltpu.VMEM((NROW...  2.57 us
    pallas_call x1, Pallas kernels, body(): call(combine_kernel, (f32(22, 8, 512),) * 2, bytes_accessed=3 * 10 ** 6)  1.59 us
    pallas_call x1, Pallas kernels, body(): call(edge_kernel, (f32(4, 24, EDGE), f32(devices, 128)), [pltpu.VMEM((96,...  1.41 us
    pallas_call x1, Pallas kernels, body(): call(rows_kernel, (f32(DEPTH, 48, 512), f32(DEPTH, 48, 512), f32(22, 8, 5...  1.32 us
  transfers between devices with their start and end apart: 6, of which 0 were waited for; matrix products, arithmetic and copies ran while one was open for 0% of the time, Pallas kernels for 12%

profile of v5, /device:TPU:1, one launch (start us, length us, event | category | flops | bytes accessed | tf_op | source)
XLA Modules:
  0.0 50.1 jit_solution(14222232955663024396)
XLA Ops:
  0.6 1.3 %shard_map.68 = (f32[3,48,512]{2,1,0:T(8,128)S(1)}, f32[3,48,512]{2,1,0:T(8,128)S(1)}, f32[22,8,512]{2,1,0:T(8,128)S(1)}, f32[10,2,8,512]{3,2,1,0:T(8,128)S(1)},...) custom-call(f32[22,8,512]{2,1,0:T(8,128)} %bitcast.10, f32[10,2,8,512]{3,2,1,0:T(8,128)} %visc.1, ...), custom_call_target="tpu_custom_call" | custom-call | bytes 1000000 | tf_op jit(solution)/shard_map/pallas_call | solution.py:472
  2.0 3.3 %collective-permute-start = (f32[3,48,512]{2,1,0:T(8,128)S(1)}, f32[3,48,512]{2,1,0:T(8,128)S(1)}, u32[]{:S(2)}, u32[]{:S(2)}) collective-permute-start(f32[3,48,512]{2,1,0:T(8,128)S(1)} %get-tuple-element.36), channel_id=1, source_target_pairs={{0,32},{32,0},{64,96},{96,64},{128,160},{160,128},{192,224},{224,1... | collective-permute-start | bytes 884744 | tf_op jit(solution)/shard_map/ppermute | solution.py:463
  5.3 1.9 %collective-permute-start.1 = (f32[3,48,512]{2,1,0:T(8,128)S(1)}, f32[3,48,512]{2,1,0:T(8,128)S(1)}, u32[]{:S(2)}, u32[]{:S(2)}) collective-permute-start(f32[3,48,512]{2,1,0:T(8,128)S(1)} %get-tuple-element.37), channel_id=1, source_target_pairs={{32,64},{64,32},{96,128},{128,96},{160,192},{192,160},{33,65},{65,... | collective-permute-start | bytes 884744 | tf_op jit(solution)/shard_map/ppermute | solution.py:463
  7.2 0.3 shard_map.71.packs
  7.5 0.7 %collective-permute-start.3 = (f32[48,256]{1,0:T(8,128)S(1)}, f32[48,256]{1,0:T(8,128)S(1)}, u32[]{:S(2)}, u32[]{:S(2)}) collective-permute-start(f32[48,256]{1,0:T(8,128)S(1)} %shard_map.71.packs), channel_id=1, source_target_pairs={{1,2},{2,1},{3,4},{4,3},{5,6},{6,5},{7,8},{8,7},{9,10},{10,9},{11,... | collective-permute-start | bytes 147464 | tf_op jit(solution)/shard_map/ppermute | solution.py:463
  8.2 4.0 %collective-permute-start.2 = (f32[48,256]{1,0:T(8,128)S(1)}, f32[48,256]{1,0:T(8,128)S(1)}, u32[]{:S(2)}, u32[]{:S(2)}) collective-permute-start(f32[48,256]{1,0:T(8,128)S(1)} %shard_map.71.packs), channel_id=1, source_target_pairs={{0,1},{1,0},{2,3},{3,2},{4,5},{5,4},{6,7},{7,6},{8,9},{9,8},{10,11... | collective-permute-start | bytes 147464 | tf_op jit(solution)/shard_map/ppermute | solution.py:463
  12.2 3.3 %shard_map.69 = (f32[8,48,512]{2,1,0:T(8,128)S(1)}, bf16[2,144,240]{2,1,0:T(8,128)(2,1)S(1)}, f32[8,96,512]{2,1,0:T(8,128)S(1)}, f32[8,24,512]{2,1,0:T(8,128)S(1...) custom-call(f32[22,8,512]{2,1,0:T(8,128)S(1)} %get-tuple-element.23., ...), custom_call_target="tpu_custom_call" | custom-call | flops 1000000000 | bytes 1000000 | tf_op jit(solution)/shard_map/pallas_call | solution.py:485
  15.5 0.0 collective-permute-done.3.second_cols
  15.5 0.0 collective-permute-done.2.first_cols
  15.6 3.1 %collective-permute-start.5 = (f32[48,256]{1,0:T(8,128)S(1)}, f32[48,256]{1,0:T(8,128)S(1)}, u32[]{:S(2)}, u32[]{:S(2)}) collective-permute-start(f32[48,256]{1,0:T(8,128)S(1)} %shard_map.72.cols), channel_id=1, source_target_pairs={{32,64},{64,32},{96,128},{128,96},{160,192},{192,160},{33,65},{65,... | collective-permute-start | bytes 147464 | tf_op jit(solution)/shard_map/ppermute | solution.py:463
  18.7 0.1 collective-permute-start.4
  18.8 0.0 collective-permute-done.first_rows
  18.8 0.0 collective-permute-done.1.second_rows
  18.8 2.6 %shard_map.70 = (f32[3,8,24,512]{3,2,1,0:T(8,128)S(1)}, f32[8,128]{1,0:T(8,128)S(1)}) custom-call(f32[8,48,512]{2,1,0:T(8,128)S(1)} %get-tuple-element.28.own, bf16[2,144,240]{2,1,0:T(8,128)(2,1)S(1)} %get-tuple-element.30.weights, f32[8,96,512]{2,1,0:T(8,128)S(1)} %get-tuple-element.31.own_scale, f32[8,24,512]{2,1,0:T(8,128)S(1)} %get-tuple-element.32.own_diag, ...), custom_call_target="tpu_custom_call" | custom-call | flops 2000000000 | bytes 3000000 | tf_op jit(solution)/shard_map/pallas_call | solution.py:506
  21.4 0.0 collective-permute-done.5.second_rows
  21.4 0.0 collective-permute-done.4.first_rows
  21.4 1.4 %shard_map.73 = (f32[4,24,256]{2,1,0:T(8,128)S(1)}, f32[256,128]{1,0:T(8,128)S(1)}) custom-call(f32[48,256]{1,0:T(8,128)S(1)} %shard_map.72.cols, f32[48,256]{1,0:T(8,128)S(1)} %collective-permute-done.4.first_rows, f32[48,256]{1,0:T(8,128)S(1)} %collective-permute-done.5.second_rows, f32[12,2,12]{2,1,0:T(2,128)S(1)} %get-tuple-element.27.stiff, ...), custom_call_target="tpu_custom_call" | custom-call | flops 100000000 | bytes 1000000 | tf_op jit(solution)/shard_map/pallas_call | solution.py:519
  22.8 25.7 %all_to_all.5 = f32[256,1,128]{2,1,0:T(1,128)S(1)} all-to-all(f32[256,1,128]{2,1,0:T(1,128)S(1)} %bitcast.9), channel_id=1, replica_groups=mesh['rx'=8,'ry'=32] {'rx','ry'}, dimensions={0} | all-to-all | bytes 262144 | tf_op jit(solution)/shard_map/all_to_all | solution.py:526
  48.5 1.6 %shard_map.74 = (f32[22,8,512]{2,1,0:T(8,128)}, f32[22,8,512]{2,1,0:T(8,128)}) custom-call(f32[8,48,512]{2,1,0:T(8,128)S(1)} %get-tuple-element.28.own, f32[3,8,24,512]{3,2,1,0:T(8,128)S(1)} %get-tuple-element.29.inner, f32[3,8,24,512]{3,2,1,0:T(8,128)S(1)} %get-tuple-element.38.outer, f32[4,24,256]{2,1,0:T(8,128)S(1)} %get-tuple-element.40.edges, ...), custom_call_target="tpu_custom_call" | custom-call | bytes 3000000 | tf_op jit(solution)/shard_map/pallas_call | solution.py:527
  (1 shorter events, 0.0 us)
Async XLA Ops:
  2.0 16.8 %collective-permute-start = (f32[3,48,512]{2,1,0:T(8,128)S(1)}, f32[3,48,512]{2,1,0:T(8,128)S(1)}, u32[]{:S(2)}, u32[]{:S(2)}) collective-permute-start(f32[3,48,512]{2,1,0:T(8,128)S(1)} %get-tuple-element.36), channel_id=1, source_target_pairs={{0,32},{32,0},{64,96},{96,64},{128,160},{160,128},{192,224},{224,1... | collective-permute-start | bytes 884744 | tf_op jit(solution)/shard_map/ppermute | solution.py:463
  5.3 13.5 %collective-permute-start.1 = (f32[3,48,512]{2,1,0:T(8,128)S(1)}, f32[3,48,512]{2,1,0:T(8,128)S(1)}, u32[]{:S(2)}, u32[]{:S(2)}) collective-permute-start(f32[3,48,512]{2,1,0:T(8,128)S(1)} %get-tuple-element.37), channel_id=1, source_target_pairs={{32,64},{64,32},{96,128},{128,96},{160,192},{192,160},{33,65},{65,... | collective-permute-start | bytes 884744 | tf_op jit(solution)/shard_map/ppermute | solution.py:463
  7.5 8.0 %collective-permute-start.3 = (f32[48,256]{1,0:T(8,128)S(1)}, f32[48,256]{1,0:T(8,128)S(1)}, u32[]{:S(2)}, u32[]{:S(2)}) collective-permute-start(f32[48,256]{1,0:T(8,128)S(1)} %shard_map.71.packs), channel_id=1, source_target_pairs={{1,2},{2,1},{3,4},{4,3},{5,6},{6,5},{7,8},{8,7},{9,10},{10,9},{11,... | collective-permute-start | bytes 147464 | tf_op jit(solution)/shard_map/ppermute | solution.py:463
  8.2 7.3 %collective-permute-start.2 = (f32[48,256]{1,0:T(8,128)S(1)}, f32[48,256]{1,0:T(8,128)S(1)}, u32[]{:S(2)}, u32[]{:S(2)}) collective-permute-start(f32[48,256]{1,0:T(8,128)S(1)} %shard_map.71.packs), channel_id=1, source_target_pairs={{0,1},{1,0},{2,3},{3,2},{4,5},{5,4},{6,7},{7,6},{8,9},{9,8},{10,11... | collective-permute-start | bytes 147464 | tf_op jit(solution)/shard_map/ppermute | solution.py:463
  15.6 5.8 %collective-permute-start.5 = (f32[48,256]{1,0:T(8,128)S(1)}, f32[48,256]{1,0:T(8,128)S(1)}, u32[]{:S(2)}, u32[]{:S(2)}) collective-permute-start(f32[48,256]{1,0:T(8,128)S(1)} %shard_map.72.cols), channel_id=1, source_target_pairs={{32,64},{64,32},{96,128},{128,96},{160,192},{192,160},{33,65},{65,... | collective-permute-start | bytes 147464 | tf_op jit(solution)/shard_map/ppermute | solution.py:463
  18.7 2.7 %collective-permute-start.4 = (f32[48,256]{1,0:T(8,128)S(1)}, f32[48,256]{1,0:T(8,128)S(1)}, u32[]{:S(2)}, u32[]{:S(2)}) collective-permute-start(f32[48,256]{1,0:T(8,128)S(1)} %shard_map.72.cols), channel_id=1, source_target_pairs={{0,32},{32,0},{64,96},{96,64},{128,160},{160,128},{192,224},{224,1... | collective-permute-start | bytes 147464 | tf_op jit(solution)/shard_map/ppermute | solution.py:463

commit v6 on v4

--- a/solution.py
+++ b/solution.py
@@ -20,7 +20,7 @@
 def shift_of(stiff):
     rows = lax.broadcasted_iota(jnp.int32, (12, 12), 0)
     cols = lax.broadcasted_iota(jnp.int32, (12, 12), 1)
-    trace = jnp.sum(jnp.where(rows == cols, stiff[0] + stiff[1], 0.0))
+    trace = jnp.sum(jnp.where(rows == cols, stiff[:, 0, :] + stiff[:, 1, :], 0.0))
     return 1.0 + trace * (1.2 * 10.0 / 22.0)
 
 
@@ -38,12 +38,16 @@
     return lax.rem(lax.axis_index(axis), 2) == 1
 
 
-def rows_kernel(rhs, visc, mask, fric, first, second, rhs_out, visc_out, mask_out, fric_out, work, sems):
+def rows_kernel(
+    rhs, visc, mask, fric, stiff,
+    first, second, rhs_out, visc_out, mask_out, fric_out, stiff_out,
+    work, sems,
+):
+    sources = (rhs, visc, mask, fric, stiff)
+    targets = (rhs_out, visc_out, mask_out, fric_out, stiff_out)
     copies = [
         pltpu.make_async_copy(src, dst, sems.at[n])
-        for n, (src, dst) in enumerate(
-            ((rhs, rhs_out), (visc, visc_out), (mask, mask_out), (fric, fric_out))
-        )
+        for n, (src, dst) in enumerate(zip(sources, targets))
     ]
     for copy in copies:
         copy.start()
@@ -104,7 +108,7 @@
         first, second, third = ((0, 2, 1), (2, 0, 1))[tri]
         place = jnp.where(block == 0, first, jnp.where(block == 1, second, third))
         rows = jnp.dot(
-            pick, stiff[tri], precision=lax.Precision.HIGHEST, preferred_element_type=jnp.float32
+            pick, stiff[:, tri, :], precision=lax.Precision.HIGHEST, preferred_element_type=jnp.float32
         )
         total = jnp.zeros((GROUPS, 3 * HALF), jnp.float32)
         for lev in range(2):
@@ -161,11 +165,13 @@
 
 
 def line_of(sums):
-    place = lax.broadcasted_iota(jnp.int32, (8, 128), 1)
-    line = jnp.zeros((8, 128), jnp.float32)
-    for n, total in enumerate(sums):
-        line = jnp.where(place == n, jnp.sum(total), line)
-    return line
+    rows = [jnp.sum(total, axis=0, keepdims=True) for total in sums]
+    rows.append(jnp.zeros((16 - len(rows), 128), jnp.float32))
+    totals = jnp.sum(jnp.concatenate(rows, axis=0), axis=1, keepdims=True)
+    row = lax.broadcasted_iota(jnp.int32, (16, 128), 0)
+    place = lax.broadcasted_iota(jnp.int32, (16, 128), 1)
+    line = jnp.sum(jnp.where(place == row, totals, 0.0), axis=0, keepdims=True)
+    return jnp.broadcast_to(line, (8, 128))
 
 
 def no_sums():
@@ -351,7 +357,7 @@
     gram[...] = jnp.broadcast_to(total[0:1], gram.shape)
 
 
-def combine_kernel(own, inner, outer, edges, grams, stiff, update, last):
+def combine_kernel(own, inner, outer, edges, grams, stiff, update, last, parts, sems):
     theta = shift_of(stiff)
     entry = jnp.sum(grams[...], axis=0, keepdims=True)
     place = lax.broadcasted_iota(jnp.int32, (1, 128), 1)
@@ -401,27 +407,41 @@
         for c in range(a + 1, 4):
             value = value - upper[a][c] * w[c]
         w[a] = value / upper[a][a]
-    lane = lax.broadcasted_iota(jnp.int32, (22, 128), 1)
-    for out, factors in ((update, z), (last, w)):
+    lane = lax.broadcasted_iota(jnp.int32, (8, 128), 1)
+    copies = []
+    for n, (out, factors) in enumerate(((update, z), (last, w))):
         ends = factors[0] * edges[0]
         for a in range(1, len(factors)):
             ends = ends + factors[a] * edges[a]
-        for r in range(8):
-            row = factors[0] * own[r, 0:22, :]
-            for a in range(1, len(factors)):
-                part = inner if is_inner(a, r + DEPTH) else outer
-                row = row + factors[a] * part[a - 1, r, 0:22, :]
-            at = PITCH * (r + DEPTH)
-            left = pltpu.roll(ends, (EDGE - at - 3) % EDGE, 1)[0:22, 0:128]
-            right = pltpu.roll(ends, (253 - at - 12) % EDGE, 1)[0:22, 128:256]
-            out[:, r, 0:128] = jnp.where(lane < DEPTH, left, row[:, 0:128])
-            out[:, r, 128:384] = row[:, 128:384]
-            out[:, r, 384:512] = jnp.where(lane >= 128 - DEPTH, right, row[:, 384:512])
-
-
-def call(kernel, outs, scratch=(), flops=0, bytes_accessed=0, limit=8, in_hbm=0):
+        for g, planes in enumerate((slice(0, 8), slice(8, 16), slice(16, 22))):
+            count = planes.stop - planes.start
+            for r in range(8):
+                row = factors[0] * own[r, planes, :]
+                for a in range(1, len(factors)):
+                    part = inner if is_inner(a, r + DEPTH) else outer
+                    row = row + factors[a] * part[a - 1, r, planes, :]
+                at = PITCH * (r + DEPTH)
+                left = pltpu.roll(ends[planes], (EDGE - at - 3) % EDGE, 1)[:, 0:128]
+                right = pltpu.roll(ends[planes], (253 - at - 12) % EDGE, 1)[:, 128:256]
+                inside = lane[0:count]
+                parts[n, planes, r, 0:128] = jnp.where(inside < DEPTH, left, row[:, 0:128])
+                parts[n, planes, r, 128:384] = row[:, 128:384]
+                parts[n, planes, r, 384:512] = jnp.where(
+                    inside >= 128 - DEPTH, right, row[:, 384:512]
+                )
+            copies.append(
+                pltpu.make_async_copy(parts.at[n, planes], out.at[planes], sems.at[3 * n + g])
+            )
+            copies[-1].start()
+    for copy in copies:
+        copy.wait()
+
+
+def call(kernel, outs, scratch=(), flops=0, bytes_accessed=0, limit=8, in_hbm=0, out_hbm=0):
     single = not isinstance(outs, (list, tuple))
     extra = {"in_specs": [pl.BlockSpec(memory_space=pltpu.HBM)] * in_hbm} if in_hbm else {}
+    if out_hbm:
+        extra["out_specs"] = (pl.BlockSpec(memory_space=pltpu.HBM),) * out_hbm
     return pl.pallas_call(
         kernel,
         out_shape=outs if single else tuple(outs),
@@ -449,15 +469,15 @@
     devices = lax.axis_size("rx") * lax.axis_size("ry")
     natural = [
         pltpu.with_memory_space_constraint(x, pltpu.HBM)
-        for x in (rhs.reshape(22, 8, 512), viscosity, cell_mask, friction)
+        for x in (rhs.reshape(22, 8, 512), viscosity, cell_mask, friction, stiffness.transpose(1, 0, 2))
     ]
-    first, second, *local = call(
+    first, second, *local, stiff = call(
         rows_kernel,
         (f32(DEPTH, 48, 512), f32(DEPTH, 48, 512), f32(22, 8, 512), f32(10, 2, 8, 512),
-         jax.ShapeDtypeStruct((8, 512), jnp.int32), f32(8, 512)),
-        [pltpu.VMEM((2, 48, 512), jnp.float32), pltpu.SemaphoreType.DMA((4,))],
+         jax.ShapeDtypeStruct((8, 512), jnp.int32), f32(8, 512), f32(12, 2, 12)),
+        [pltpu.VMEM((2, 48, 512), jnp.float32), pltpu.SemaphoreType.DMA((5,))],
         bytes_accessed=10**6,
-        in_hbm=4,
+        in_hbm=5,
     )(*natural)
     first_rows = swapped(first, "rx", 0)
     second_rows = swapped(second, "rx", 1)
@@ -478,7 +498,7 @@
         flops=10**9,
         bytes_accessed=10**6,
         limit=16,
-    )(*local, stiffness)
+    )(*local, stiff)
     inner = prepared[2]
     packs = call(cols_kernel, f32(48, EDGE), bytes_accessed=10**6)(packs, first_rows, second_rows)
     first_cols = swapped(packs, "ry", 0)
@@ -495,17 +515,23 @@
         flops=2 * 10**9,
         bytes_accessed=3 * 10**6,
         limit=24,
-    )(own, weights, *prepared, first_rows, second_rows, stiffness)
+    )(own, weights, *prepared, first_rows, second_rows, stiff)
     edges, gram = call(
         edge_kernel,
         (f32(4, 24, EDGE), f32(devices, 128)),
         [pltpu.VMEM((96, EDGE), jnp.float32)],
         flops=10**8,
         bytes_accessed=10**6,
-    )(packs, first_cols, second_cols, stiffness, weights, line)
+    )(packs, first_cols, second_cols, stiff, weights, line)
     grams = lax.all_to_all(gram.reshape(devices, 1, 128), ("rx", "ry"), 0, 0)
-    update, last = call(combine_kernel, (f32(22, 8, 512),) * 2, bytes_accessed=3 * 10**6)(
-        own, inner, outer, edges, grams.reshape(devices, 128), stiffness
+    update, last = call(
+        combine_kernel,
+        (f32(22, 8, 512),) * 2,
+        [pltpu.VMEM((2, 22, 8, 512), jnp.float32), pltpu.SemaphoreType.DMA((6,))],
+        bytes_accessed=3 * 10**6,
+        out_hbm=2,
+    )(
+        own, inner, outer, edges, grams.reshape(devices, 128), stiff
     )
     return update.reshape(2, 11, 8, 512), last.reshape(2, 11, 8, 512)
 

time: 49.3 us -> 49.1 us (level)
  local copies, waits for them, and re-layouts: 0.71 us -> 0 us
  waiting for transfers between devices: 2.15 us -> 2.71 us
    unnamed x1 -> x0, local copies, waits for them, and re-layouts: 0.71 us -> none
    ppermute x4, waiting for transfers between devices: 2.15 us -> 2.71 us  [swapped(): return lax.ppermute(shard, axis, pairs)]
  transfers between devices with their start and end apart: 4 -> 4, of which waited for: 1 -> 1; matrix products, arithmetic and copies ran while one was open for 1% -> 0% of each run, Pallas kernels for 11% -> 12%
where the time goes in v6:
time: 49.1 us; the launch traced here: 48.9 us
  blocking collectives  26.5 us (54%)
  Pallas kernels  10.2 us (21%)
  starting transfers between devices  8.77 us (18%)
  waiting for transfers between devices  2.71 us (6%)
  between operations  0.69 us (1%)
    all_to_all x1, blocking collectives, body(): grams = lax.all_to_all(gram.reshape(devices, 1, 128), ('rx', 'ry'), 0, 0)  26.5 us
    ppermute x4, starting transfers between devices, swapped(): return lax.ppermute(shard, axis, pairs)  8.77 us
    pallas_call x1, Pallas kernels, body(): call(own_kernel, (f32(8, 48, LANES), f32(48, EDGE), jax.ShapeDtypeStruct(...  3.4 us
    ppermute x4, waiting for transfers between devices, swapped(): return lax.ppermute(shard, axis, pairs)  2.71 us
    pallas_call x1, Pallas kernels, body(): call(main_kernel, (f32(3, 8, 24, LANES), f32(8, 128)), [pltpu.VMEM((NROW...  2.51 us
    pallas_call x1, Pallas kernels, body(): call(combine_kernel, (f32(22, 8, 512),) * 2, [pltpu.VMEM((2, 22, 8, 512),...  1.5 us
    pallas_call x1, Pallas kernels, body(): call(rows_kernel, (f32(DEPTH, 48, 512), f32(DEPTH, 48, 512), f32(22, 8, 5...  1.32 us
    pallas_call x1, Pallas kernels, body(): call(edge_kernel, (f32(4, 24, EDGE), f32(devices, 128)), [pltpu.VMEM((96,...  1.3 us
  transfers between devices with their start and end apart: 4, of which 1 were waited for; matrix products, arithmetic and copies ran while one was open for 0% of the time, Pallas kernels for 12%

profile of v6, /device:TPU:1, one launch (start us, length us, event | category | flops | bytes accessed | tf_op | source)
XLA Modules:
  0.0 48.9 jit_solution(12241773030123594476)
XLA Ops:
  0.6 1.3 %shard_map.68 = (f32[3,48,512]{2,1,0:T(8,128)S(1)}, f32[3,48,512]{2,1,0:T(8,128)S(1)}, f32[22,8,512]{2,1,0:T(8,128)S(1)}, f32[10,2,8,512]{3,2,1,0:T(8,128)S(1)},...) custom-call(f32[22,8,512]{2,1,0:T(8,128)} %bitcast.10, f32[10,2,8,512]{3,2,1,0:T(8,128)} %visc.1, ...), custom_call_target="tpu_custom_call" | custom-call | bytes 1000000 | tf_op jit(solution)/shard_map/pallas_call | solution.py:474
  2.0 3.3 %collective-permute-start = (f32[3,48,512]{2,1,0:T(8,128)S(1)}, f32[3,48,512]{2,1,0:T(8,128)S(1)}, u32[]{:S(2)}, u32[]{:S(2)}) collective-permute-start(f32[3,48,512]{2,1,0:T(8,128)S(1)} %get-tuple-element.37), channel_id=1, source_target_pairs={{0,32},{32,0},{64,96},{96,64},{128,160},{160,128},{192,224},{224,1... | collective-permute-start | bytes 884744 | tf_op jit(solution)/shard_map/ppermute | solution.py:465
  5.3 1.9 %collective-permute-start.1 = (f32[3,48,512]{2,1,0:T(8,128)S(1)}, f32[3,48,512]{2,1,0:T(8,128)S(1)}, u32[]{:S(2)}, u32[]{:S(2)}) collective-permute-start(f32[3,48,512]{2,1,0:T(8,128)S(1)} %get-tuple-element.38), channel_id=1, source_target_pairs={{32,64},{64,32},{96,128},{128,96},{160,192},{192,160},{33,65},{65,... | collective-permute-start | bytes 884744 | tf_op jit(solution)/shard_map/ppermute | solution.py:465
  7.2 3.4 %shard_map.69 = (f32[8,48,512]{2,1,0:T(8,128)S(1)}, f32[48,256]{1,0:T(8,128)S(1)}, bf16[2,144,240]{2,1,0:T(8,128)(2,1)S(1)}, f32[8,96,512]{2,1,0:T(8,128)S(1)}, ...) custom-call(f32[22,8,512]{2,1,0:T(8,128)S(1)} %get-tuple-element.24., ...), custom_call_target="tpu_custom_call" | custom-call | flops 1000000000 | bytes 1000000 | tf_op jit(solution)/shard_map/pallas_call | solution.py:484
  10.6 0.0 collective-permute-done.first_rows
  10.6 2.7 %collective-permute-done.1.second_rows = f32[3,48,512]{2,1,0:T(8,128)S(1)} collective-permute-done((f32[3,48,512]{2,1,0:T(8,128)S(1)}, f32[3,48,512]{2,1,0:T(8,128)S(1)}, u32[]{:S(2)}, u32[]{:S(2)}) %collective-permute-start.1) | collective-permute-done | bytes 294944 | tf_op jit(solution)/shard_map/ppermute | solution.py:465
  13.3 0.2 shard_map.71.packs
  13.5 0.7 %collective-permute-start.3 = (f32[48,256]{1,0:T(8,128)S(1)}, f32[48,256]{1,0:T(8,128)S(1)}, u32[]{:S(2)}, u32[]{:S(2)}) collective-permute-start(f32[48,256]{1,0:T(8,128)S(1)} %shard_map.71.packs), channel_id=1, source_target_pairs={{1,2},{2,1},{3,4},{4,3},{5,6},{6,5},{7,8},{8,7},{9,10},{10,9},{11,... | collective-permute-start | bytes 147464 | tf_op jit(solution)/shard_map/ppermute | solution.py:465
  14.2 2.9 %collective-permute-start.2 = (f32[48,256]{1,0:T(8,128)S(1)}, f32[48,256]{1,0:T(8,128)S(1)}, u32[]{:S(2)}, u32[]{:S(2)}) collective-permute-start(f32[48,256]{1,0:T(8,128)S(1)} %shard_map.71.packs), channel_id=1, source_target_pairs={{0,1},{1,0},{2,3},{3,2},{4,5},{5,4},{6,7},{7,6},{8,9},{9,8},{10,11... | collective-permute-start | bytes 147464 | tf_op jit(solution)/shard_map/ppermute | solution.py:465
  17.1 2.5 %shard_map.70 = (f32[3,8,24,512]{3,2,1,0:T(8,128)S(1)}, f32[8,128]{1,0:T(8,128)S(1)}) custom-call(f32[8,48,512]{2,1,0:T(8,128)S(1)} %get-tuple-element.29.own, bf16[2,144,240]{2,1,0:T(8,128)(2,1)S(1)} %get-tuple-element.31.weights, f32[8,96,512]{2,1,0:T(8,128)S(1)} %get-tuple-element.32.own_scale, f32[8,24,512]{2,1,0:T(8,128)S(1)} %get-tuple-element.33.own_diag, ...), custom_call_target="tpu_custom_call" | custom-call | flops 2000000000 | bytes 3000000 | tf_op jit(solution)/shard_map/pallas_call | solution.py:506
  19.6 0.0 collective-permute-done.3.second_cols
  19.6 0.0 collective-permute-done.2.first_cols
  19.6 1.3 %shard_map.72 = (f32[4,24,256]{2,1,0:T(8,128)S(1)}, f32[256,128]{1,0:T(8,128)S(1)}) custom-call(f32[48,256]{1,0:T(8,128)S(1)} %shard_map.71.packs, f32[48,256]{1,0:T(8,128)S(1)} %collective-permute-done.2.first_cols, f32[48,256]{1,0:T(8,128)S(1)} %collective-permute-done.3.second_cols, f32[12,2,12]{2,1,0:T(2,128)S(1)} %get-tuple-element.28.stiff, ...), custom_call_target="tpu_custom_call" | custom-call | flops 100000000 | bytes 1000000 | tf_op jit(solution)/shard_map/pallas_call | solution.py:519
  20.9 26.5 %all_to_all.5 = f32[256,1,128]{2,1,0:T(1,128)S(1)} all-to-all(f32[256,1,128]{2,1,0:T(1,128)S(1)} %bitcast.9), channel_id=1, replica_groups=mesh['rx'=8,'ry'=32] {'rx','ry'}, dimensions={0} | all-to-all | bytes 262144 | tf_op jit(solution)/shard_map/all_to_all | solution.py:526
  47.4 1.5 %shard_map.73 = (f32[22,8,512]{2,1,0:T(8,128)}, f32[22,8,512]{2,1,0:T(8,128)}) custom-call(f32[8,48,512]{2,1,0:T(8,128)S(1)} %get-tuple-element.29.own, f32[3,8,24,512]{3,2,1,0:T(8,128)S(1)} %get-tuple-element.30.inner, f32[3,8,24,512]{3,2,1,0:T(8,128)S(1)} %get-tuple-element.39.outer, f32[4,24,256]{2,1,0:T(8,128)S(1)} %get-tuple-element.42.edges, ...), custom_call_target="tpu_custom_call" | custom-call | bytes 3000000 | tf_op jit(solution)/shard_map/pallas_call | solution.py:527
Async XLA Ops:
  2.0 8.6 %collective-permute-start = (f32[3,48,512]{2,1,0:T(8,128)S(1)}, f32[3,48,512]{2,1,0:T(8,128)S(1)}, u32[]{:S(2)}, u32[]{:S(2)}) collective-permute-start(f32[3,48,512]{2,1,0:T(8,128)S(1)} %get-tuple-element.37), channel_id=1, source_target_pairs={{0,32},{32,0},{64,96},{96,64},{128,160},{160,128},{192,224},{224,1... | collective-permute-start | bytes 884744 | tf_op jit(solution)/shard_map/ppermute | solution.py:465
  5.3 8.0 %collective-permute-start.1 = (f32[3,48,512]{2,1,0:T(8,128)S(1)}, f32[3,48,512]{2,1,0:T(8,128)S(1)}, u32[]{:S(2)}, u32[]{:S(2)}) collective-permute-start(f32[3,48,512]{2,1,0:T(8,128)S(1)} %get-tuple-element.38), channel_id=1, source_target_pairs={{32,64},{64,32},{96,128},{128,96},{160,192},{192,160},{33,65},{65,... | collective-permute-start | bytes 884744 | tf_op jit(solution)/shard_map/ppermute | solution.py:465
  13.5 6.1 %collective-permute-start.3 = (f32[48,256]{1,0:T(8,128)S(1)}, f32[48,256]{1,0:T(8,128)S(1)}, u32[]{:S(2)}, u32[]{:S(2)}) collective-permute-start(f32[48,256]{1,0:T(8,128)S(1)} %shard_map.71.packs), channel_id=1, source_target_pairs={{1,2},{2,1},{3,4},{4,3},{5,6},{6,5},{7,8},{8,7},{9,10},{10,9},{11,... | collective-permute-start | bytes 147464 | tf_op jit(solution)/shard_map/ppermute | solution.py:465
  14.2 5.4 %collective-permute-start.2 = (f32[48,256]{1,0:T(8,128)S(1)}, f32[48,256]{1,0:T(8,128)S(1)}, u32[]{:S(2)}, u32[]{:S(2)}) collective-permute-start(f32[48,256]{1,0:T(8,128)S(1)} %shard_map.71.packs), channel_id=1, source_target_pairs={{0,1},{1,0},{2,3},{3,2},{4,5},{5,4},{6,7},{7,6},{8,9},{9,8},{10,11... | collective-permute-start | bytes 147464 | tf_op jit(solution)/shard_map/ppermute | solution.py:465

commit v7 on v6

--- a/solution.py
+++ b/solution.py
@@ -69,15 +69,25 @@
     return jnp.where((at >= 9) & (at < 18), pltpu.roll(ends, (PITCH * i + 15) % EDGE, 1), packed)
 
 
-def cols_kernel(packs, first_rows, second_rows, out):
+def cols_kernel(packs, second_rows, first_rows, out):
     odd_row = odd_along("rx")
-    lane = lax.broadcasted_iota(jnp.int32, (48, EDGE), 1)
-    packed = packs[...]
+    lane = lax.broadcasted_iota(jnp.int32, (48, 128), 1)
+    halves = [packs[:, 0:128], packs[:, 128:256]]
     for j in range(DEPTH):
-        one, two = (first_rows[j], second_rows[j])
-        packed = pack_row(jnp.where(odd_row, one, two), j, lane, packed)
-        packed = pack_row(jnp.where(odd_row, two, one), j + 8 + DEPTH, lane, packed)
-    out[...] = packed
+        one, two = [
+            jnp.where(lane < 64, rows[j, :, 0:128], rows[j, :, 384:512])
+            for rows in (first_rows, second_rows)
+        ]
+        low, high = (jnp.where(odd_row, one, two), jnp.where(odd_row, two, one))
+        for half, row, i in ((0, low, j), (1, high, j + 8 + DEPTH)):
+            start = PITCH * i - 128 * half
+            at = lane - start
+            packed = jnp.where((at >= 0) & (at < 9), pltpu.roll(row, start + 3, 1), halves[half])
+            halves[half] = jnp.where(
+                (at >= 9) & (at < 18), pltpu.roll(row, (start + 15) % 128, 1), packed
+            )
+    out[:, 0:128] = halves[0]
+    out[:, 128:256] = halves[1]
 
 
 def weights_kernel(stiff, weights):
@@ -249,7 +259,7 @@
 
 
 def main_kernel(
-    own, weights, own_scale, own_diag, inner, bounds, low_parts, high_parts, first_rows, second_rows, stiff,
+    own, weights, own_scale, own_diag, inner, bounds, low_parts, high_parts, second_rows, first_rows, stiff,
     outer, line,
     scale, diag, field, operand,
 ):
@@ -365,15 +375,17 @@
     for n, pair in enumerate(PAIRS):
         g[pair] = jnp.sum(jnp.where(place == n, entry, 0.0), axis=1, keepdims=True)
     upper = [[None] * 4 for _ in range(4)]
+    inverse = [None] * 4
     for a in range(4):
         for b in range(a, 4):
             value = g[a, b]
             for c in range(a):
                 value = value - upper[c][a] * upper[c][b]
             if a == b:
-                upper[a][a] = jnp.sqrt(value)
+                inverse[a] = lax.rsqrt(value)
+                upper[a][a] = value * inverse[a]
             else:
-                upper[a][b] = value / upper[a][a]
+                upper[a][b] = value * inverse[a]
     zero = jnp.zeros((1, 1), jnp.float32)
     table = [
         [
@@ -383,10 +395,11 @@
         for a in range(4)
     ]
     target = [upper[0][0], zero, zero, zero]
+    turned = [None] * 3
     for col in range(3):
         first, second = (table[col][col], table[col + 1][col])
-        radius = jnp.sqrt(first * first + second * second)
-        cosine, sine = (first / radius, second / radius)
+        turned[col] = lax.rsqrt(first * first + second * second)
+        cosine, sine = (first * turned[col], second * turned[col])
         for c in range(col, 3):
             one, two = (table[col][c], table[col + 1][c])
             table[col][c] = cosine * one + sine * two
@@ -399,14 +412,14 @@
         value = target[col]
         for c in range(col + 1, 3):
             value = value - table[col][c] * z[c]
-        z[col] = value / table[col][col]
+        z[col] = value * turned[col]
     w = [None] * 4
-    w[3] = 1.0 / upper[3][3]
+    w[3] = inverse[3]
     for a in (2, 1, 0):
         value = zero
         for c in range(a + 1, 4):
             value = value - upper[a][c] * w[c]
-        w[a] = value / upper[a][a]
+        w[a] = value * inverse[a]
     lane = lax.broadcasted_iota(jnp.int32, (8, 128), 1)
     copies = []
     for n, (out, factors) in enumerate(((update, z), (last, w))):
@@ -500,7 +513,7 @@
         limit=16,
     )(*local, stiff)
     inner = prepared[2]
-    packs = call(cols_kernel, f32(48, EDGE), bytes_accessed=10**6)(packs, first_rows, second_rows)
+    packs = call(cols_kernel, f32(48, EDGE), bytes_accessed=10**6)(packs, second_rows, first_rows)
     first_cols = swapped(packs, "ry", 0)
     second_cols = swapped(packs, "ry", 1)
     outer, line = call(
@@ -515,7 +528,7 @@
         flops=2 * 10**9,
         bytes_accessed=3 * 10**6,
         limit=24,
-    )(own, weights, *prepared, first_rows, second_rows, stiff)
+    )(own, weights, *prepared, second_rows, first_rows, stiff)
     edges, gram = call(
         edge_kernel,
         (f32(4, 24, EDGE), f32(devices, 128)),

time: 49.1 us -> 48.8 us (level)
  waiting for transfers between devices: 2.71 us -> 0.86 us
  starting transfers between devices: 8.77 us -> 9.87 us
  blocking collectives: 26.5 us -> 27 us
    ppermute x4, waiting for transfers between devices: 2.71 us -> 0.86 us  [swapped(): return lax.ppermute(shard, axis, pairs)]
    ppermute x4, starting transfers between devices: 8.77 us -> 9.87 us  [swapped(): return lax.ppermute(shard, axis, pairs)]
    all_to_all x1, blocking collectives: 26.5 us -> 27 us  [body(): grams = lax.all_to_all(gram.reshape(devices, 1, 128), ('rx', 'ry'), 0, 0)]
where the time goes in v7:
time: 48.8 us; the launch traced here: 48.6 us
  blocking collectives  27 us (55%)
  Pallas kernels  10.1 us (21%)
  starting transfers between devices  9.87 us (20%)
  waiting for transfers between devices  0.86 us (2%)
  between operations  0.69 us (1%)
    all_to_all x1, blocking collectives, body(): grams = lax.all_to_all(gram.reshape(devices, 1, 128), ('rx', 'ry'), 0, 0)  27 us
    ppermute x4, starting transfers between devices, swapped(): return lax.ppermute(shard, axis, pairs)  9.87 us
    pallas_call x1, Pallas kernels, body(): call(own_kernel, (f32(8, 48, LANES), f32(48, EDGE), jax.ShapeDtypeStruct(...  3.43 us
    pallas_call x1, Pallas kernels, body(): call(main_kernel, (f32(3, 8, 24, LANES), f32(8, 128)), [pltpu.VMEM((NROW...  2.52 us
    pallas_call x1, Pallas kernels, body(): call(combine_kernel, (f32(22, 8, 512),) * 2, [pltpu.VMEM((2, 22, 8, 512),...  1.42 us
    pallas_call x1, Pallas kernels, body(): call(rows_kernel, (f32(DEPTH, 48, 512), f32(DEPTH, 48, 512), f32(22, 8, 5...  1.32 us
    pallas_call x1, Pallas kernels, body(): call(edge_kernel, (f32(4, 24, EDGE), f32(devices, 128)), [pltpu.VMEM((96,...  1.3 us
  transfers between devices with their start and end apart: 4, of which 1 were waited for; matrix products, arithmetic and copies ran while one was open for 0% of the time, Pallas kernels for 12%

profile of v7, /device:TPU:1, one launch (start us, length us, event | category | flops | bytes accessed | tf_op | source)
XLA Modules:
  0.0 48.6 jit_solution(14608609228220217958)
XLA Ops:
  0.6 1.3 %shard_map.68 = (f32[3,48,512]{2,1,0:T(8,128)S(1)}, f32[3,48,512]{2,1,0:T(8,128)S(1)}, f32[22,8,512]{2,1,0:T(8,128)S(1)}, f32[10,2,8,512]{3,2,1,0:T(8,128)S(1)},...) custom-call(f32[22,8,512]{2,1,0:T(8,128)} %bitcast.10, f32[10,2,8,512]{3,2,1,0:T(8,128)} %visc.1, ...), custom_call_target="tpu_custom_call" | custom-call | bytes 1000000 | tf_op jit(solution)/shard_map/pallas_call | solution.py:487
  2.0 4.5 %collective-permute-start = (f32[3,48,512]{2,1,0:T(8,128)S(1)}, f32[3,48,512]{2,1,0:T(8,128)S(1)}, u32[]{:S(2)}, u32[]{:S(2)}) collective-permute-start(f32[3,48,512]{2,1,0:T(8,128)S(1)} %get-tuple-element.37), channel_id=1, source_target_pairs={{32,64},{64,32},{96,128},{128,96},{160,192},{192,160},{33,65},{65,... | collective-permute-start | bytes 884744 | tf_op jit(solution)/shard_map/ppermute | solution.py:478
  6.5 0.1 collective-permute-start.1
  6.6 3.4 %shard_map.69 = (f32[8,48,512]{2,1,0:T(8,128)S(1)}, f32[48,256]{1,0:T(8,128)S(1)}, bf16[2,144,240]{2,1,0:T(8,128)(2,1)S(1)}, f32[8,96,512]{2,1,0:T(8,128)S(1)}, ...) custom-call(f32[22,8,512]{2,1,0:T(8,128)S(1)} %get-tuple-element.24., ...), custom_call_target="tpu_custom_call" | custom-call | flops 1000000000 | bytes 1000000 | tf_op jit(solution)/shard_map/pallas_call | solution.py:497
  10.0 0.9 %collective-permute-done.second_rows = f32[3,48,512]{2,1,0:T(8,128)S(1)} collective-permute-done((f32[3,48,512]{2,1,0:T(8,128)S(1)}, f32[3,48,512]{2,1,0:T(8,128)S(1)}, u32[]{:S(2)}, u32[]{:S(2)}) %collective-permute-start) | collective-permute-done | bytes 294944 | tf_op jit(solution)/shard_map/ppermute | solution.py:478
  10.9 0.0 collective-permute-done.1.first_rows
  10.9 0.2 shard_map.71.packs
  11.0 0.7 %collective-permute-start.3 = (f32[48,256]{1,0:T(8,128)S(1)}, f32[48,256]{1,0:T(8,128)S(1)}, u32[]{:S(2)}, u32[]{:S(2)}) collective-permute-start(f32[48,256]{1,0:T(8,128)S(1)} %shard_map.71.packs), channel_id=1, source_target_pairs={{1,2},{2,1},{3,4},{4,3},{5,6},{6,5},{7,8},{8,7},{9,10},{10,9},{11,... | collective-permute-start | bytes 147464 | tf_op jit(solution)/shard_map/ppermute | solution.py:478
  11.7 4.6 %collective-permute-start.2 = (f32[48,256]{1,0:T(8,128)S(1)}, f32[48,256]{1,0:T(8,128)S(1)}, u32[]{:S(2)}, u32[]{:S(2)}) collective-permute-start(f32[48,256]{1,0:T(8,128)S(1)} %shard_map.71.packs), channel_id=1, source_target_pairs={{0,1},{1,0},{2,3},{3,2},{4,5},{5,4},{6,7},{7,6},{8,9},{9,8},{10,11... | collective-permute-start | bytes 147464 | tf_op jit(solution)/shard_map/ppermute | solution.py:478
  16.3 2.5 %shard_map.70 = (f32[3,8,24,512]{3,2,1,0:T(8,128)S(1)}, f32[8,128]{1,0:T(8,128)S(1)}) custom-call(f32[8,48,512]{2,1,0:T(8,128)S(1)} %get-tuple-element.29.own, bf16[2,144,240]{2,1,0:T(8,128)(2,1)S(1)} %get-tuple-element.31.weights, f32[8,96,512]{2,1,0:T(8,128)S(1)} %get-tuple-element.32.own_scale, f32[8,24,512]{2,1,0:T(8,128)S(1)} %get-tuple-element.33.own_diag, ...), custom_call_target="tpu_custom_call" | custom-call | flops 2000000000 | bytes 3000000 | tf_op jit(solution)/shard_map/pallas_call | solution.py:519
  18.8 0.0 collective-permute-done.3.second_cols
  18.8 0.0 collective-permute-done.2.first_cols
  18.8 1.3 %shard_map.72 = (f32[4,24,256]{2,1,0:T(8,128)S(1)}, f32[256,128]{1,0:T(8,128)S(1)}) custom-call(f32[48,256]{1,0:T(8,128)S(1)} %shard_map.71.packs, f32[48,256]{1,0:T(8,128)S(1)} %collective-permute-done.2.first_cols, f32[48,256]{1,0:T(8,128)S(1)} %collective-permute-done.3.second_cols, f32[12,2,12]{2,1,0:T(2,128)S(1)} %get-tuple-element.28.stiff, ...), custom_call_target="tpu_custom_call" | custom-call | flops 100000000 | bytes 1000000 | tf_op jit(solution)/shard_map/pallas_call | solution.py:532
  20.1 27.0 %all_to_all.5 = f32[256,1,128]{2,1,0:T(1,128)S(1)} all-to-all(f32[256,1,128]{2,1,0:T(1,128)S(1)} %bitcast.9), channel_id=1, replica_groups=mesh['rx'=8,'ry'=32] {'rx','ry'}, dimensions={0} | all-to-all | bytes 262144 | tf_op jit(solution)/shard_map/all_to_all | solution.py:539
  47.2 1.4 %shard_map.73 = (f32[22,8,512]{2,1,0:T(8,128)}, f32[22,8,512]{2,1,0:T(8,128)}) custom-call(f32[8,48,512]{2,1,0:T(8,128)S(1)} %get-tuple-element.29.own, f32[3,8,24,512]{3,2,1,0:T(8,128)S(1)} %get-tuple-element.30.inner, f32[3,8,24,512]{3,2,1,0:T(8,128)S(1)} %get-tuple-element.39.outer, f32[4,24,256]{2,1,0:T(8,128)S(1)} %get-tuple-element.42.edges, ...), custom_call_target="tpu_custom_call" | custom-call | bytes 3000000 | tf_op jit(solution)/shard_map/pallas_call | solution.py:540
Async XLA Ops:
  2.0 8.9 %collective-permute-start = (f32[3,48,512]{2,1,0:T(8,128)S(1)}, f32[3,48,512]{2,1,0:T(8,128)S(1)}, u32[]{:S(2)}, u32[]{:S(2)}) collective-permute-start(f32[3,48,512]{2,1,0:T(8,128)S(1)} %get-tuple-element.37), channel_id=1, source_target_pairs={{32,64},{64,32},{96,128},{128,96},{160,192},{192,160},{33,65},{65,... | collective-permute-start | bytes 884744 | tf_op jit(solution)/shard_map/ppermute | solution.py:478
  6.5 4.4 %collective-permute-start.1 = (f32[3,48,512]{2,1,0:T(8,128)S(1)}, f32[3,48,512]{2,1,0:T(8,128)S(1)}, u32[]{:S(2)}, u32[]{:S(2)}) collective-permute-start(f32[3,48,512]{2,1,0:T(8,128)S(1)} %get-tuple-element.38), channel_id=1, source_target_pairs={{0,32},{32,0},{64,96},{96,64},{128,160},{160,128},{192,224},{224,1... | collective-permute-start | bytes 884744 | tf_op jit(solution)/shard_map/ppermute | solution.py:478
  11.0 7.8 %collective-permute-start.3 = (f32[48,256]{1,0:T(8,128)S(1)}, f32[48,256]{1,0:T(8,128)S(1)}, u32[]{:S(2)}, u32[]{:S(2)}) collective-permute-start(f32[48,256]{1,0:T(8,128)S(1)} %shard_map.71.packs), channel_id=1, source_target_pairs={{1,2},{2,1},{3,4},{4,3},{5,6},{6,5},{7,8},{8,7},{9,10},{10,9},{11,... | collective-permute-start | bytes 147464 | tf_op jit(solution)/shard_map/ppermute | solution.py:478
  11.7 7.1 %collective-permute-start.2 = (f32[48,256]{1,0:T(8,128)S(1)}, f32[48,256]{1,0:T(8,128)S(1)}, u32[]{:S(2)}, u32[]{:S(2)}) collective-permute-start(f32[48,256]{1,0:T(8,128)S(1)} %shard_map.71.packs), channel_id=1, source_target_pairs={{0,1},{1,0},{2,3},{3,2},{4,5},{5,4},{6,7},{7,6},{8,9},{9,8},{10,11... | collective-permute-start | bytes 147464 | tf_op jit(solution)/shard_map/ppermute | solution.py:478

commit v8 on v7

--- a/solution.py
+++ b/solution.py
@@ -165,27 +165,77 @@
 
 def inner_products(vectors, sums, lanes):
     result = []
-    for total, (a, b) in zip(sums, PAIRS):
+    for (high, low), (a, b) in zip(sums, PAIRS):
         product = vectors[a] * vectors[b]
-        for s in range(0, 24, 8):
-            for l in range(0, lanes, 128):
-                total = total + product[s : s + 8, l : l + 128]
-        result.append(total)
+        terms = [
+            product[s : s + 8, l : l + 128] for s in range(0, 24, 8) for l in range(0, lanes, 128)
+        ]
+        while len(terms) > 1:
+            terms = [sum(terms[n : n + 2][1:], terms[n]) for n in range(0, len(terms), 2)]
+        high, rest = two_sum(high, terms[0])
+        result.append((high, low + rest))
     return tuple(result)
 
 
+def two_sum(a, b):
+    total = a + b
+    back = total - a
+    return total, (a - (total - back)) + (b - back)
+
+
+def pair_of(high, low):
+    total = high + low
+    return total, low - (total - high)
+
+
+def parts_of(a):
+    wide = a * 4097.0
+    high = wide - (wide - a)
+    return high, a - high
+
+
+def pair_times(x, y):
+    product = x[0] * y[0]
+    (xh, xl), (yh, yl) = (parts_of(x[0]), parts_of(y[0]))
+    rest = ((xh * yh - product) + xh * yl + xl * yh) + xl * yl
+    return pair_of(product, rest + (x[0] * y[1] + x[1] * y[0]))
+
+
+def pair_less(x, y):
+    total, rest = two_sum(x[0], -y[0])
+    return pair_of(total, rest + (x[1] - y[1]))
+
+
+def pair_over(x, y):
+    zero = jnp.zeros_like(x[0])
+    first = x[0] / y[0]
+    rest = pair_less(x, pair_times(y, (first, zero)))
+    return pair_of(first, rest[0] / y[0])
+
+
+def folded(high, low, axis, shifts):
+    for by in shifts:
+        total, rest = two_sum(high, pltpu.roll(high, by, axis))
+        low = low + pltpu.roll(low, by, axis) + rest
+        high = total
+    return high, low
+
+
 def line_of(sums):
-    rows = [jnp.sum(total, axis=0, keepdims=True) for total in sums]
-    rows.append(jnp.zeros((16 - len(rows), 128), jnp.float32))
-    totals = jnp.sum(jnp.concatenate(rows, axis=0), axis=1, keepdims=True)
+    rows = [folded(high, low, 0, (4, 2, 1)) for high, low in sums]
+    pad = [jnp.zeros((16 - len(rows), 128), jnp.float32)]
+    high = jnp.concatenate([h[0:1] for h, _ in rows] + pad, axis=0)
+    low = jnp.concatenate([l[0:1] for _, l in rows] + pad, axis=0)
+    high, low = folded(high, low, 1, (64, 32, 16, 8, 4, 2, 1))
     row = lax.broadcasted_iota(jnp.int32, (16, 128), 0)
     place = lax.broadcasted_iota(jnp.int32, (16, 128), 1)
-    line = jnp.sum(jnp.where(place == row, totals, 0.0), axis=0, keepdims=True)
-    return jnp.broadcast_to(line, (8, 128))
+    line = jnp.where(place == row, high, jnp.where(place == row + 16, low, 0.0))
+    return jnp.broadcast_to(jnp.sum(line, axis=0, keepdims=True), (8, 128))
 
 
 def no_sums():
-    return tuple(jnp.zeros((8, 128), jnp.float32) for _ in PAIRS)
+    zero = jnp.zeros((8, 128), jnp.float32)
+    return tuple((zero, zero) for _ in PAIRS)
 
 
 def products(weights, source, i):
@@ -363,29 +413,46 @@
     mine = (lane >= PITCH * DEPTH) & (lane < PITCH * (DEPTH + 8))
     mine = mine & (((at >= 3) & (at < 6)) | ((at >= 12) & (at < 15)))
     sums = inner_products([jnp.where(mine, v, 0.0) for v in vectors], no_sums(), EDGE)
-    total = line[...] + line_of(sums)
+    total, rest = two_sum(line[...], line_of(sums))
+    total = total + pltpu.roll(rest, 16, 1)
     gram[...] = jnp.broadcast_to(total[0:1], gram.shape)
 
 
 def combine_kernel(own, inner, outer, edges, grams, stiff, update, last, parts, sems):
     theta = shift_of(stiff)
-    entry = jnp.sum(grams[...], axis=0, keepdims=True)
+    high, low = (grams[...], jnp.zeros(grams.shape, jnp.float32))
+    while high.shape[0] > 8 and high.shape[0] % 16 == 0:
+        half = high.shape[0] // 2
+        high, rest = two_sum(high[:half], high[half:])
+        low = low[:half] + low[half:] + rest
+    for start in range(8, high.shape[0], 8):
+        total, rest = two_sum(high[0:8], high[start : start + 8])
+        high = jnp.concatenate([total, high[8:]], axis=0)
+        low = jnp.concatenate([low[0:8] + low[start : start + 8] + rest, low[8:]], axis=0)
+    if high.shape[0] >= 8:
+        high, low = folded(high[0:8], low[0:8], 0, (4, 2, 1))
+    else:
+        high, low = (jnp.sum(high, axis=0, keepdims=True), jnp.sum(low, axis=0, keepdims=True))
+    high, low = (high[0:1], low[0:1])
     place = lax.broadcasted_iota(jnp.int32, (1, 128), 1)
+
+    def lane_of(line, n):
+        return jnp.sum(jnp.where(place == n, line, 0.0), axis=1, keepdims=True)
+
     g = {}
     for n, pair in enumerate(PAIRS):
-        g[pair] = jnp.sum(jnp.where(place == n, entry, 0.0), axis=1, keepdims=True)
+        g[pair] = pair_of(lane_of(high, n), lane_of(high, n + 16) + lane_of(low, n))
     upper = [[None] * 4 for _ in range(4)]
     inverse = [None] * 4
     for a in range(4):
-        for b in range(a, 4):
-            value = g[a, b]
-            for c in range(a):
-                value = value - upper[c][a] * upper[c][b]
-            if a == b:
-                inverse[a] = lax.rsqrt(value)
-                upper[a][a] = value * inverse[a]
-            else:
-                upper[a][b] = value * inverse[a]
+        inverse[a] = lax.rsqrt(g[a, a][0])
+        upper[a][a] = g[a, a][0] * inverse[a]
+        for b in range(a + 1, 4):
+            upper[a][b] = g[a, b][0] * inverse[a]
+        for b in range(a + 1, 4):
+            ratio = pair_over(g[a, b], g[a, a])
+            for c in range(b, 4):
+                g[b, c] = pair_less(g[b, c], pair_times(ratio, g[a, c]))
     zero = jnp.zeros((1, 1), jnp.float32)
     table = [
         [

time: 48.8 us -> 49.5 us (1.014)
  Pallas kernels: 10.1 us -> 11.3 us
    pallas_call x1, Pallas kernels: 1.3 us -> 1.81 us  [body(): call(edge_kernel, (f32(4, 24, EDGE), f32(devices, 128)), [pltpu.VMEM((96,...]
  transfers between devices with their start and end apart: 4 -> 4, of which waited for: 1 -> 1; matrix products, arithmetic and copies ran while one was open for 0% -> 0% of each run, Pallas kernels for 12% -> 13%
where the time goes in v8:
time: 49.5 us; the launch traced here: 49.3 us
  blocking collectives  26.6 us (54%)
  Pallas kernels  11.3 us (23%)
  starting transfers between devices  9.87 us (20%)
  waiting for transfers between devices  0.86 us (2%)
  between operations  0.7 us (1%)
    all_to_all x1, blocking collectives, body(): grams = lax.all_to_all(gram.reshape(devices, 1, 128), ('rx', 'ry'), 0, 0)  26.6 us
    ppermute x4, starting transfers between devices, swapped(): return lax.ppermute(shard, axis, pairs)  9.87 us
    pallas_call x1, Pallas kernels, body(): call(own_kernel, (f32(8, 48, LANES), f32(48, EDGE), jax.ShapeDtypeStruct(...  3.43 us
    pallas_call x1, Pallas kernels, body(): call(main_kernel, (f32(3, 8, 24, LANES), f32(8, 128)), [pltpu.VMEM((NROW...  2.99 us
    pallas_call x1, Pallas kernels, body(): call(edge_kernel, (f32(4, 24, EDGE), f32(devices, 128)), [pltpu.VMEM((96,...  1.81 us
    pallas_call x1, Pallas kernels, body(): call(combine_kernel, (f32(22, 8, 512),) * 2, [pltpu.VMEM((2, 22, 8, 512),...  1.58 us
    pallas_call x1, Pallas kernels, body(): call(rows_kernel, (f32(DEPTH, 48, 512), f32(DEPTH, 48, 512), f32(22, 8, 5...  1.32 us
  transfers between devices with their start and end apart: 4, of which 1 were waited for; matrix products, arithmetic and copies ran while one was open for 0% of the time, Pallas kernels for 13%

profile of v8, /device:TPU:1, one launch (start us, length us, event | category | flops | bytes accessed | tf_op | source)
XLA Modules:
  0.0 49.3 jit_solution(2512301328296527070)
XLA Ops:
  0.6 1.3 %shard_map.68 = (f32[3,48,512]{2,1,0:T(8,128)S(1)}, f32[3,48,512]{2,1,0:T(8,128)S(1)}, f32[22,8,512]{2,1,0:T(8,128)S(1)}, f32[10,2,8,512]{3,2,1,0:T(8,128)S(1)},...) custom-call(f32[22,8,512]{2,1,0:T(8,128)} %bitcast.10, f32[10,2,8,512]{3,2,1,0:T(8,128)} %visc.1, ...), custom_call_target="tpu_custom_call" | custom-call | bytes 1000000 | tf_op jit(solution)/shard_map/pallas_call | solution.py:554
  2.0 4.5 %collective-permute-start = (f32[3,48,512]{2,1,0:T(8,128)S(1)}, f32[3,48,512]{2,1,0:T(8,128)S(1)}, u32[]{:S(2)}, u32[]{:S(2)}) collective-permute-start(f32[3,48,512]{2,1,0:T(8,128)S(1)} %get-tuple-element.37), channel_id=1, source_target_pairs={{32,64},{64,32},{96,128},{128,96},{160,192},{192,160},{33,65},{65,... | collective-permute-start | bytes 884744 | tf_op jit(solution)/shard_map/ppermute | solution.py:545
  6.5 0.1 collective-permute-start.1
  6.6 3.4 %shard_map.69 = (f32[8,48,512]{2,1,0:T(8,128)S(1)}, f32[48,256]{1,0:T(8,128)S(1)}, bf16[2,144,240]{2,1,0:T(8,128)(2,1)S(1)}, f32[8,96,512]{2,1,0:T(8,128)S(1)}, ...) custom-call(f32[22,8,512]{2,1,0:T(8,128)S(1)} %get-tuple-element.24., ...), custom_call_target="tpu_custom_call" | custom-call | flops 1000000000 | bytes 1000000 | tf_op jit(solution)/shard_map/pallas_call | solution.py:564
  10.0 0.9 %collective-permute-done.second_rows = f32[3,48,512]{2,1,0:T(8,128)S(1)} collective-permute-done((f32[3,48,512]{2,1,0:T(8,128)S(1)}, f32[3,48,512]{2,1,0:T(8,128)S(1)}, u32[]{:S(2)}, u32[]{:S(2)}) %collective-permute-start) | collective-permute-done | bytes 294944 | tf_op jit(solution)/shard_map/ppermute | solution.py:545
  10.9 0.0 collective-permute-done.1.first_rows
  10.9 0.2 shard_map.71.packs
  11.0 0.7 %collective-permute-start.3 = (f32[48,256]{1,0:T(8,128)S(1)}, f32[48,256]{1,0:T(8,128)S(1)}, u32[]{:S(2)}, u32[]{:S(2)}) collective-permute-start(f32[48,256]{1,0:T(8,128)S(1)} %shard_map.71.packs), channel_id=1, source_target_pairs={{1,2},{2,1},{3,4},{4,3},{5,6},{6,5},{7,8},{8,7},{9,10},{10,9},{11,... | collective-permute-start | bytes 147464 | tf_op jit(solution)/shard_map/ppermute | solution.py:545
  11.7 4.6 %collective-permute-start.2 = (f32[48,256]{1,0:T(8,128)S(1)}, f32[48,256]{1,0:T(8,128)S(1)}, u32[]{:S(2)}, u32[]{:S(2)}) collective-permute-start(f32[48,256]{1,0:T(8,128)S(1)} %shard_map.71.packs), channel_id=1, source_target_pairs={{0,1},{1,0},{2,3},{3,2},{4,5},{5,4},{6,7},{7,6},{8,9},{9,8},{10,11... | collective-permute-start | bytes 147464 | tf_op jit(solution)/shard_map/ppermute | solution.py:545
  16.3 3.0 %shard_map.70 = (f32[3,8,24,512]{3,2,1,0:T(8,128)S(1)}, f32[8,128]{1,0:T(8,128)S(1)}) custom-call(f32[8,48,512]{2,1,0:T(8,128)S(1)} %get-tuple-element.29.own, bf16[2,144,240]{2,1,0:T(8,128)(2,1)S(1)} %get-tuple-element.31.weights, f32[8,96,512]{2,1,0:T(8,128)S(1)} %get-tuple-element.32.own_scale, f32[8,24,512]{2,1,0:T(8,128)S(1)} %get-tuple-element.33.own_diag, ...), custom_call_target="tpu_custom_call" | custom-call | flops 2000000000 | bytes 3000000 | tf_op jit(solution)/shard_map/pallas_call | solution.py:586
  19.3 0.0 collective-permute-done.3.second_cols
  19.3 0.0 collective-permute-done.2.first_cols
  19.3 1.8 %shard_map.72 = (f32[4,24,256]{2,1,0:T(8,128)S(1)}, f32[256,128]{1,0:T(8,128)S(1)}) custom-call(f32[48,256]{1,0:T(8,128)S(1)} %shard_map.71.packs, f32[48,256]{1,0:T(8,128)S(1)} %collective-permute-done.2.first_cols, f32[48,256]{1,0:T(8,128)S(1)} %collective-permute-done.3.second_cols, f32[12,2,12]{2,1,0:T(2,128)S(1)} %get-tuple-element.28.stiff, ...), custom_call_target="tpu_custom_call" | custom-call | flops 100000000 | bytes 1000000 | tf_op jit(solution)/shard_map/pallas_call | solution.py:599
  21.1 26.6 %all_to_all.5 = f32[256,1,128]{2,1,0:T(1,128)S(1)} all-to-all(f32[256,1,128]{2,1,0:T(1,128)S(1)} %bitcast.9), channel_id=1, replica_groups=mesh['rx'=8,'ry'=32] {'rx','ry'}, dimensions={0} | all-to-all | bytes 262144 | tf_op jit(solution)/shard_map/all_to_all | solution.py:606
  47.7 1.6 %shard_map.73 = (f32[22,8,512]{2,1,0:T(8,128)}, f32[22,8,512]{2,1,0:T(8,128)}) custom-call(f32[8,48,512]{2,1,0:T(8,128)S(1)} %get-tuple-element.29.own, f32[3,8,24,512]{3,2,1,0:T(8,128)S(1)} %get-tuple-element.30.inner, f32[3,8,24,512]{3,2,1,0:T(8,128)S(1)} %get-tuple-element.39.outer, f32[4,24,256]{2,1,0:T(8,128)S(1)} %get-tuple-element.42.edges, ...), custom_call_target="tpu_custom_call" | custom-call | bytes 3000000 | tf_op jit(solution)/shard_map/pallas_call | solution.py:607
Async XLA Ops:
  2.0 8.9 %collective-permute-start = (f32[3,48,512]{2,1,0:T(8,128)S(1)}, f32[3,48,512]{2,1,0:T(8,128)S(1)}, u32[]{:S(2)}, u32[]{:S(2)}) collective-permute-start(f32[3,48,512]{2,1,0:T(8,128)S(1)} %get-tuple-element.37), channel_id=1, source_target_pairs={{32,64},{64,32},{96,128},{128,96},{160,192},{192,160},{33,65},{65,... | collective-permute-start | bytes 884744 | tf_op jit(solution)/shard_map/ppermute | solution.py:545
  6.5 4.4 %collective-permute-start.1 = (f32[3,48,512]{2,1,0:T(8,128)S(1)}, f32[3,48,512]{2,1,0:T(8,128)S(1)}, u32[]{:S(2)}, u32[]{:S(2)}) collective-permute-start(f32[3,48,512]{2,1,0:T(8,128)S(1)} %get-tuple-element.38), channel_id=1, source_target_pairs={{0,32},{32,0},{64,96},{96,64},{128,160},{160,128},{192,224},{224,1... | collective-permute-start | bytes 884744 | tf_op jit(solution)/shard_map/ppermute | solution.py:545
  11.0 8.3 %collective-permute-start.3 = (f32[48,256]{1,0:T(8,128)S(1)}, f32[48,256]{1,0:T(8,128)S(1)}, u32[]{:S(2)}, u32[]{:S(2)}) collective-permute-start(f32[48,256]{1,0:T(8,128)S(1)} %shard_map.71.packs), channel_id=1, source_target_pairs={{1,2},{2,1},{3,4},{4,3},{5,6},{6,5},{7,8},{8,7},{9,10},{10,9},{11,... | collective-permute-start | bytes 147464 | tf_op jit(solution)/shard_map/ppermute | solution.py:545
  11.7 7.6 %collective-permute-start.2 = (f32[48,256]{1,0:T(8,128)S(1)}, f32[48,256]{1,0:T(8,128)S(1)}, u32[]{:S(2)}, u32[]{:S(2)}) collective-permute-start(f32[48,256]{1,0:T(8,128)S(1)} %shard_map.71.packs), channel_id=1, source_target_pairs={{0,1},{1,0},{2,3},{3,2},{4,5},{5,4},{6,7},{7,6},{8,9},{9,8},{10,11... | collective-permute-start | bytes 147464 | tf_op jit(solution)/shard_map/ppermute | solution.py:545

commit v9 on v7

--- a/solution.py
+++ b/solution.py
@@ -167,10 +167,12 @@
     result = []
     for total, (a, b) in zip(sums, PAIRS):
         product = vectors[a] * vectors[b]
-        for s in range(0, 24, 8):
-            for l in range(0, lanes, 128):
-                total = total + product[s : s + 8, l : l + 128]
-        result.append(total)
+        terms = [
+            product[s : s + 8, l : l + 128] for s in range(0, 24, 8) for l in range(0, lanes, 128)
+        ]
+        while len(terms) > 1:
+            terms = [sum(terms[n : n + 2][1:], terms[n]) for n in range(0, len(terms), 2)]
+        result.append(total + terms[0])
     return tuple(result)
 
 

time: 48.8 us -> 48.8 us (level)
  no operation moved by 1% of the time
where the time goes in v9:
time: 48.8 us; the launch traced here: 48.6 us
  blocking collectives  27.1 us (56%)
  Pallas kernels  10.1 us (21%)
  starting transfers between devices  9.87 us (20%)
  waiting for transfers between devices  0.86 us (2%)
  between operations  0.69 us (1%)
    all_to_all x1, blocking collectives, body(): grams = lax.all_to_all(gram.reshape(devices, 1, 128), ('rx', 'ry'), 0, 0)  27.1 us
    ppermute x4, starting transfers between devices, swapped(): return lax.ppermute(shard, axis, pairs)  9.87 us
    pallas_call x1, Pallas kernels, body(): call(own_kernel, (f32(8, 48, LANES), f32(48, EDGE), jax.ShapeDtypeStruct(...  3.43 us
    pallas_call x1, Pallas kernels, body(): call(main_kernel, (f32(3, 8, 24, LANES), f32(8, 128)), [pltpu.VMEM((NROW...  2.49 us
    pallas_call x1, Pallas kernels, body(): call(combine_kernel, (f32(22, 8, 512),) * 2, [pltpu.VMEM((2, 22, 8, 512),...  1.42 us
    pallas_call x1, Pallas kernels, body(): call(rows_kernel, (f32(DEPTH, 48, 512), f32(DEPTH, 48, 512), f32(22, 8, 5...  1.32 us
    pallas_call x1, Pallas kernels, body(): call(edge_kernel, (f32(4, 24, EDGE), f32(devices, 128)), [pltpu.VMEM((96,...  1.31 us
  transfers between devices with their start and end apart: 4, of which 1 were waited for; matrix products, arithmetic and copies ran while one was open for 0% of the time, Pallas kernels for 12%

profile of v9, /device:TPU:1, one launch (start us, length us, event | category | flops | bytes accessed | tf_op | source)
XLA Modules:
  0.0 48.6 jit_solution(15645472149433838311)
XLA Ops:
  0.6 1.3 %shard_map.68 = (f32[3,48,512]{2,1,0:T(8,128)S(1)}, f32[3,48,512]{2,1,0:T(8,128)S(1)}, f32[22,8,512]{2,1,0:T(8,128)S(1)}, f32[10,2,8,512]{3,2,1,0:T(8,128)S(1)},...) custom-call(f32[22,8,512]{2,1,0:T(8,128)} %bitcast.10, f32[10,2,8,512]{3,2,1,0:T(8,128)} %visc.1, ...), custom_call_target="tpu_custom_call" | custom-call | bytes 1000000 | tf_op jit(solution)/shard_map/pallas_call | solution.py:489
  2.0 4.5 %collective-permute-start = (f32[3,48,512]{2,1,0:T(8,128)S(1)}, f32[3,48,512]{2,1,0:T(8,128)S(1)}, u32[]{:S(2)}, u32[]{:S(2)}) collective-permute-start(f32[3,48,512]{2,1,0:T(8,128)S(1)} %get-tuple-element.37), channel_id=1, source_target_pairs={{32,64},{64,32},{96,128},{128,96},{160,192},{192,160},{33,65},{65,... | collective-permute-start | bytes 884744 | tf_op jit(solution)/shard_map/ppermute | solution.py:480
  6.5 0.1 collective-permute-start.1
  6.6 3.4 %shard_map.69 = (f32[8,48,512]{2,1,0:T(8,128)S(1)}, f32[48,256]{1,0:T(8,128)S(1)}, bf16[2,144,240]{2,1,0:T(8,128)(2,1)S(1)}, f32[8,96,512]{2,1,0:T(8,128)S(1)}, ...) custom-call(f32[22,8,512]{2,1,0:T(8,128)S(1)} %get-tuple-element.24., ...), custom_call_target="tpu_custom_call" | custom-call | flops 1000000000 | bytes 1000000 | tf_op jit(solution)/shard_map/pallas_call | solution.py:499
  10.0 0.9 %collective-permute-done.second_rows = f32[3,48,512]{2,1,0:T(8,128)S(1)} collective-permute-done((f32[3,48,512]{2,1,0:T(8,128)S(1)}, f32[3,48,512]{2,1,0:T(8,128)S(1)}, u32[]{:S(2)}, u32[]{:S(2)}) %collective-permute-start) | collective-permute-done | bytes 294944 | tf_op jit(solution)/shard_map/ppermute | solution.py:480
  10.9 0.0 collective-permute-done.1.first_rows
  10.9 0.2 shard_map.71.packs
  11.0 0.7 %collective-permute-start.3 = (f32[48,256]{1,0:T(8,128)S(1)}, f32[48,256]{1,0:T(8,128)S(1)}, u32[]{:S(2)}, u32[]{:S(2)}) collective-permute-start(f32[48,256]{1,0:T(8,128)S(1)} %shard_map.71.packs), channel_id=1, source_target_pairs={{1,2},{2,1},{3,4},{4,3},{5,6},{6,5},{7,8},{8,7},{9,10},{10,9},{11,... | collective-permute-start | bytes 147464 | tf_op jit(solution)/shard_map/ppermute | solution.py:480
  11.7 4.6 %collective-permute-start.2 = (f32[48,256]{1,0:T(8,128)S(1)}, f32[48,256]{1,0:T(8,128)S(1)}, u32[]{:S(2)}, u32[]{:S(2)}) collective-permute-start(f32[48,256]{1,0:T(8,128)S(1)} %shard_map.71.packs), channel_id=1, source_target_pairs={{0,1},{1,0},{2,3},{3,2},{4,5},{5,4},{6,7},{7,6},{8,9},{9,8},{10,11... | collective-permute-start | bytes 147464 | tf_op jit(solution)/shard_map/ppermute | solution.py:480
  16.3 2.5 %shard_map.70 = (f32[3,8,24,512]{3,2,1,0:T(8,128)S(1)}, f32[8,128]{1,0:T(8,128)S(1)}) custom-call(f32[8,48,512]{2,1,0:T(8,128)S(1)} %get-tuple-element.29.own, bf16[2,144,240]{2,1,0:T(8,128)(2,1)S(1)} %get-tuple-element.31.weights, f32[8,96,512]{2,1,0:T(8,128)S(1)} %get-tuple-element.32.own_scale, f32[8,24,512]{2,1,0:T(8,128)S(1)} %get-tuple-element.33.own_diag, ...), custom_call_target="tpu_custom_call" | custom-call | flops 2000000000 | bytes 3000000 | tf_op jit(solution)/shard_map/pallas_call | solution.py:521
  18.8 0.0 collective-permute-done.3.second_cols
  18.8 0.0 collective-permute-done.2.first_cols
  18.8 1.3 %shard_map.72 = (f32[4,24,256]{2,1,0:T(8,128)S(1)}, f32[256,128]{1,0:T(8,128)S(1)}) custom-call(f32[48,256]{1,0:T(8,128)S(1)} %shard_map.71.packs, f32[48,256]{1,0:T(8,128)S(1)} %collective-permute-done.2.first_cols, f32[48,256]{1,0:T(8,128)S(1)} %collective-permute-done.3.second_cols, f32[12,2,12]{2,1,0:T(2,128)S(1)} %get-tuple-element.28.stiff, ...), custom_call_target="tpu_custom_call" | custom-call | flops 100000000 | bytes 1000000 | tf_op jit(solution)/shard_map/pallas_call | solution.py:534
  20.1 27.1 %all_to_all.5 = f32[256,1,128]{2,1,0:T(1,128)S(1)} all-to-all(f32[256,1,128]{2,1,0:T(1,128)S(1)} %bitcast.9), channel_id=1, replica_groups=mesh['rx'=8,'ry'=32] {'rx','ry'}, dimensions={0} | all-to-all | bytes 262144 | tf_op jit(solution)/shard_map/all_to_all | solution.py:541
  47.2 1.4 %shard_map.73 = (f32[22,8,512]{2,1,0:T(8,128)}, f32[22,8,512]{2,1,0:T(8,128)}) custom-call(f32[8,48,512]{2,1,0:T(8,128)S(1)} %get-tuple-element.29.own, f32[3,8,24,512]{3,2,1,0:T(8,128)S(1)} %get-tuple-element.30.inner, f32[3,8,24,512]{3,2,1,0:T(8,128)S(1)} %get-tuple-element.39.outer, f32[4,24,256]{2,1,0:T(8,128)S(1)} %get-tuple-element.42.edges, ...), custom_call_target="tpu_custom_call" | custom-call | bytes 3000000 | tf_op jit(solution)/shard_map/pallas_call | solution.py:542
Async XLA Ops:
  2.0 8.9 %collective-permute-start = (f32[3,48,512]{2,1,0:T(8,128)S(1)}, f32[3,48,512]{2,1,0:T(8,128)S(1)}, u32[]{:S(2)}, u32[]{:S(2)}) collective-permute-start(f32[3,48,512]{2,1,0:T(8,128)S(1)} %get-tuple-element.37), channel_id=1, source_target_pairs={{32,64},{64,32},{96,128},{128,96},{160,192},{192,160},{33,65},{65,... | collective-permute-start | bytes 884744 | tf_op jit(solution)/shard_map/ppermute | solution.py:480
  6.5 4.4 %collective-permute-start.1 = (f32[3,48,512]{2,1,0:T(8,128)S(1)}, f32[3,48,512]{2,1,0:T(8,128)S(1)}, u32[]{:S(2)}, u32[]{:S(2)}) collective-permute-start(f32[3,48,512]{2,1,0:T(8,128)S(1)} %get-tuple-element.38), channel_id=1, source_target_pairs={{0,32},{32,0},{64,96},{96,64},{128,160},{160,128},{192,224},{224,1... | collective-permute-start | bytes 884744 | tf_op jit(solution)/shard_map/ppermute | solution.py:480
  11.0 7.8 %collective-permute-start.3 = (f32[48,256]{1,0:T(8,128)S(1)}, f32[48,256]{1,0:T(8,128)S(1)}, u32[]{:S(2)}, u32[]{:S(2)}) collective-permute-start(f32[48,256]{1,0:T(8,128)S(1)} %shard_map.71.packs), channel_id=1, source_target_pairs={{1,2},{2,1},{3,4},{4,3},{5,6},{6,5},{7,8},{8,7},{9,10},{10,9},{11,... | collective-permute-start | bytes 147464 | tf_op jit(solution)/shard_map/ppermute | solution.py:480
  11.7 7.1 %collective-permute-start.2 = (f32[48,256]{1,0:T(8,128)S(1)}, f32[48,256]{1,0:T(8,128)S(1)}, u32[]{:S(2)}, u32[]{:S(2)}) collective-permute-start(f32[48,256]{1,0:T(8,128)S(1)} %shard_map.71.packs), channel_id=1, source_target_pairs={{0,1},{1,0},{2,3},{3,2},{4,5},{5,4},{6,7},{7,6},{8,9},{9,8},{10,11... | collective-permute-start | bytes 147464 | tf_op jit(solution)/shard_map/ppermute | solution.py:480
